TPU v7x, 256 devices: a whole 4x4x8 slice. The times are simulated.
256 devices in a mesh: dp: 4 (over z_hi, core), seq: 64 (over x, y, z_lo).
Axes of the slice: x: 4, y: 4, z: 8 (z_hi: 2, z_lo: 4; z = z_hi * 4 + z_lo), core: 2. Of those that a mesh axis runs over, the one named last changes fastest.
Arguments:
- queries: bfloat16 [4, 16384, 768], P('dp', 'seq'), may hold values from -8 to 8
- keys: bfloat16 [4, 16384, 768], P('dp', 'seq'), may hold values from -8 to 8
- values: bfloat16 [4, 16384, 768], P('dp', 'seq'), may hold values from -6 to 6
- out_weight: bfloat16 [768, 768], replicated, may hold values from -0.21875 to 0.21875
- out_cotangent: bfloat16 [4, 16384, 768], P('dp', 'seq'), may hold values from -16 to 16
- offsets: int32 [3, 12], replicated, may hold values from 0 to 7, as said below
Outputs:
- mixed: bfloat16 [4, 16384, 768], P('dp', 'seq')
- query_grad: bfloat16 [4, 16384, 768], P('dp', 'seq')
- key_grad: bfloat16 [4, 16384, 768], P('dp', 'seq')
- value_grad: bfloat16 [4, 16384, 768], P('dp', 'seq')
- weight_grad: bfloat16 [768, 768], P('seq')
Inputs may be any that keep to these rules, and one draw needn't show every extreme that they name: offsets[k - 1, h] is below 2^k.
All inputs are finite; a program needn't handle non-finite values.
Results may differ from a plain program's by a relative error of at most 0.025.
Values may be sent and summed in bfloat16 or wider, within the bound.
No kernel may reach another device: no remote copies, remote signals or barrier semaphores. Data moves between devices by JAX's collectives and lax.ppermute only.
A program may use at most 64 MiB of HBM per device.

v0:
```python
import math

import jax
import jax.numpy as jnp
from jax import lax
from jax.sharding import PartitionSpec as P

HEADS = 12
HEAD_DIM = 64
LEVELS = 3


def swapped(block, axis, apart):
    count = lax.axis_size(axis)
    route = []
    for low in range(count):
        high = low | 1 << apart
        if high != low and high < count:
            route += [(low, high), (high, low)]
    return lax.ppermute(block, axis, route)


def pick_rows(source, chosen, rate):
    row_count, feature = source.shape
    regrouped = source.reshape(row_count // rate, rate, HEADS, feature // HEADS)
    picked = jnp.einsum("arhd,rh->ahd", regrouped, chosen, preferred_element_type=jnp.float32)
    return picked.astype(jnp.bfloat16).reshape(row_count // rate, feature)


def spread_rows(source, chosen, rate):
    row_count, feature = source.shape
    expanded = (
        source.reshape(row_count, 1, HEADS, feature // HEADS)
        * chosen.astype(jnp.float32)[None, :, :, None]
    )
    return expanded.reshape(row_count * rate, feature)


def double_rows(source, bit_idx, lower_side):
    partner = swapped(source, "seq", bit_idx)
    return jnp.where(
        lower_side, jnp.concatenate([source, partner], 1), jnp.concatenate([partner, source], 1)
    )


def halve_rows(source, bit_idx, lower_side):
    half_rows = source.shape[1] // 2
    kept = jnp.where(lower_side, source[:, :half_rows], source[:, half_rows:])
    outgoing = jnp.where(lower_side, source[:, half_rows:], source[:, :half_rows])
    return kept + swapped(outgoing.astype(jnp.bfloat16), "seq", bit_idx).astype(outgoing.dtype)


def split_heads(source):
    row_count, feature = source.shape
    return source.reshape(row_count, HEADS // 2, 2 * HEAD_DIM).transpose(1, 0, 2)


def merge_heads(source):
    group_count, row_count, pair_width = source.shape
    return source.transpose(1, 0, 2).reshape(row_count, group_count * pair_width)


def head_pair(inputs):
    query_part, key_part, value_part, grad_part = inputs
    score_scale = 1.0 / math.sqrt(HEAD_DIM)
    row_count = query_part.shape[0]
    set_rows = key_part.shape[0]
    query_four = query_part.reshape(row_count, 2, HEAD_DIM)
    key_four = key_part.reshape(set_rows, 2, HEAD_DIM)
    value_four = value_part.reshape(set_rows, 2, HEAD_DIM)
    grad_four = grad_part.reshape(row_count, 2, HEAD_DIM)
    scores = (
        jnp.einsum("ihd,jhd->hij", query_four, key_four, preferred_element_type=jnp.float32)
        * score_scale
    )
    row_max = jnp.max(scores, axis=-1, keepdims=True)
    raw_weights = jnp.exp(scores - row_max)
    probs = raw_weights / jnp.sum(raw_weights, axis=-1, keepdims=True)
    probs_rounded = probs.astype(jnp.bfloat16)
    attended = jnp.einsum(
        "hij,jhd->ihd", probs_rounded, value_four, preferred_element_type=jnp.float32
    ).astype(jnp.bfloat16)
    prob_grad = jnp.einsum(
        "ihd,jhd->hij", grad_four, value_four, preferred_element_type=jnp.float32
    )
    delta = jnp.sum(grad_four.astype(jnp.float32) * attended.astype(jnp.float32), axis=-1).T[
        :, :, None
    ]
    score_grad = (probs * (prob_grad - delta)).astype(jnp.bfloat16)
    query_grad = (
        jnp.einsum("hij,jhd->ihd", score_grad, key_four, preferred_element_type=jnp.float32)
        * score_scale
    ).astype(jnp.bfloat16)
    set_key_grad = (
        jnp.einsum("hij,ihd->jhd", score_grad, query_four, preferred_element_type=jnp.float32)
        * score_scale
    )
    set_value_grad = jnp.einsum(
        "hij,ihd->jhd", probs_rounded, grad_four, preferred_element_type=jnp.float32
    )
    pair_width = 2 * HEAD_DIM
    return (
        attended.reshape(row_count, pair_width),
        query_grad.reshape(row_count, pair_width),
        set_key_grad.reshape(set_rows, pair_width),
        set_value_grad.reshape(set_rows, pair_width),
    )


def shards(queries, keys, values, out_weight, out_cotangent, offsets):
    query_rows = queries[0]
    key_rows = keys[0]
    value_rows = values[0]
    cotangent = out_cotangent[0]
    rows_dev, feature = query_rows.shape
    position = lax.axis_index("seq")
    lower_side = [position // 2**bit_idx % 2 == 0 for bit_idx in range(LEVELS)]
    chosen = [
        (
            jnp.arange(2 ** (level_idx + 1), dtype=jnp.int32)[:, None]
            == offsets[level_idx][None, :]
        ).astype(jnp.bfloat16)
        for level_idx in range(LEVELS)
    ]
    picked = [
        jnp.stack(
            [
                pick_rows(key_rows, chosen[level_idx], 2 ** (level_idx + 1)),
                pick_rows(value_rows, chosen[level_idx], 2 ** (level_idx + 1)),
            ]
        )
        for level_idx in range(LEVELS)
    ]
    for level_idx in range(LEVELS):
        for bit_idx in range(level_idx + 1):
            picked[level_idx] = double_rows(picked[level_idx], bit_idx, lower_side[bit_idx])
    key_all = jnp.concatenate([key_rows] + [stacked[0] for stacked in picked], axis=0)
    value_all = jnp.concatenate([value_rows] + [stacked[1] for stacked in picked], axis=0)
    attended_grad = jnp.dot(cotangent, out_weight, preferred_element_type=jnp.float32).astype(
        jnp.bfloat16
    )
    results = lax.map(
        head_pair,
        (
            split_heads(query_rows),
            split_heads(key_all),
            split_heads(value_all),
            split_heads(attended_grad),
        ),
    )
    attended = merge_heads(results[0])
    query_grad = merge_heads(results[1])
    set_key_grad = merge_heads(results[2])
    set_value_grad = merge_heads(results[3])
    mixed = lax.dot_general(
        attended, out_weight, (((1,), (1,)), ((), ())), preferred_element_type=jnp.float32
    ).astype(jnp.bfloat16)
    returned = [
        jnp.stack(
            [
                set_key_grad[(level_idx + 1) * rows_dev : (level_idx + 2) * rows_dev],
                set_value_grad[(level_idx + 1) * rows_dev : (level_idx + 2) * rows_dev],
            ]
        )
        for level_idx in range(LEVELS)
    ]
    for level_idx in range(LEVELS):
        for bit_idx in reversed(range(level_idx + 1)):
            returned[level_idx] = halve_rows(returned[level_idx], bit_idx, lower_side[bit_idx])
    key_total = set_key_grad[:rows_dev]
    value_total = set_value_grad[:rows_dev]
    for level_idx in range(LEVELS):
        key_total = key_total + spread_rows(
            returned[level_idx][0], chosen[level_idx], 2 ** (level_idx + 1)
        )
        value_total = value_total + spread_rows(
            returned[level_idx][1], chosen[level_idx], 2 ** (level_idx + 1)
        )
    slide_count = lax.axis_size("dp")
    shard_count = lax.axis_size("seq")
    norm_factor = 1.0 / math.sqrt(slide_count * shard_count * rows_dev)
    shares = lax.psum_scatter(
        lax.dot_general(
            cotangent, attended, (((0,), (0,)), ((), ())), preferred_element_type=jnp.float32
        ),
        "seq",
        scatter_dimension=0,
        tiled=True,
    )
    summed = lax.psum(shares.astype(jnp.bfloat16), "dp").astype(jnp.float32)
    weight_grad = (summed * norm_factor).astype(jnp.bfloat16)
    return (
        mixed[None],
        query_grad[None],
        key_total.astype(jnp.bfloat16)[None],
        value_total.astype(jnp.bfloat16)[None],
        weight_grad,
    )


def solution(mesh):
    placed = (
        P("dp", "seq", None),
        P("dp", "seq", None),
        P("dp", "seq", None),
        P(),
        P("dp", "seq", None),
        P(),
    )
    return jax.shard_map(
        shards,
        mesh=mesh,
        in_specs=placed,
        out_specs=(
            P("dp", "seq", None),
            P("dp", "seq", None),
            P("dp", "seq", None),
            P("dp", "seq", None),
            P("seq", None),
        ),
        check_vma=False,
    )
```

profile of v0, /device:TPU:1, one launch (start us, length us, event | category | flops | bytes accessed | tf_op | source)
XLA Modules:
  0.0 646.5 jit_solution(1598770685440052655)
XLA Ops:
  6.6 2.5 collective-permute-start.3
  11.3 2.0 multiply_reduce_fusion.3
  17.0 2.9 multiply_reduce_fusion.5
  24.0 2.7 maximum_select_fusion.4
  26.6 3.0 collective-permute-start.4
  34.0 1.9 copy.73
  38.8 3.7 collective-permute-done.4
  47.1 16.9 %collective-permute-done.2 = bf16[2,128,768]{1,2,0:T(8,128)(2,1)S(1)} collective-permute-done((bf16[2,128,768]{1,2,0:T(8,128)(2,1)S(1)}, bf16[2,128,768]{1,2,0:T(8,128)(2,1)S(1)}, u32[]{:S(2)}, u32[]{:S(2)}) %collective-permute-start.2) | collective-permute-done | bytes 393248 | tf_op jit(solution)/shard_map/ppermute | solution.py:20
  66.7 67.8 %while.16 = (s32[]{:T(128)}, bf16[6,256,128]{1,2,0:T(8,128)(2,1)}, bf16[6,256,128]{1,2,0:T(8,128)(2,1)}, f32[6,1024,128]{1,2,0:T(8,128)}, f32[6,1024,128]{1,2,0:...) while((s32[]{:T(128)}, bf16[6,256,128]{1,2,0:T(8,128)(2,1)}, ...), condition=%wide.region_4.5_spmd, body=%wide.region_0.4_spmd.sunk | while | flops 407732736 | bytes 32975120 | solution.py:142
  136.4 3.2 fusion.36
  147.0 358.9 %all-reduce.2 = bf16[768,768]{0,1:T(8,128)(2,1)} all-reduce(f32[768,768]{0,1:T(8,128)S(1)} %convolution_bitcast_fusion), channel_id=2, replica_groups=mesh['dp'=4,'seq'=64] {'seq'}, use_global_device_ids=true, to_apply=%region_5.6.clone | all-reduce | flops 589824 | bytes 3538944
  507.1 80.5 %psum.7 = bf16[12,768]{0,1:T(8,128)(2,1)S(1)} all-reduce(bf16[12,768]{0,1:T(8,128)(2,1)S(1)} %dynamic-slice_convert_fusion), channel_id=1, replica_groups=mesh['dp'=4,'seq'=64] {'dp'}, use_global_device_ids=true, to_apply=%region_6.7 | all-reduce | flops 9216 | bytes 36864 | tf_op jit(solution)/shard_map/psum | solution.py:190
  588.4 2.3 fusion.8
  599.0 4.2 broadcast_multiply_fusion.2
  603.2 2.0 mul.179
  606.3 2.0 mul.193
  615.5 2.7 broadcast_multiply_fusion.1
  618.1 2.0 mul.184
  621.3 2.0 mul.197
  626.9 2.9 broadcast_multiply_fusion
  629.8 2.8 mul.189
  632.6 2.3 copy.79
  634.9 2.8 fusion.17
  642.5 2.1 fusion.14
  (292 shorter events, 136.2 us)
Async XLA Ops:
  0.6 29.0 %copy-start = (bf16[768,768]{1,0:T(8,128)(2,1)S(1)}, bf16[768,768]{1,0:T(8,128)(2,1)}, u32[]{:S(2)}) copy-start(bf16[768,768]{1,0:T(8,128)(2,1)} %param.11) | copy-start | bytes 3538948
  6.6 17.3 %collective-permute-start.3 = (bf16[2,32,768]{1,2,0:T(8,128)(2,1)}, bf16[2,32,768]{1,2,0:T(8,128)(2,1)}, u32[]{:S(2)}, u32[]{:S(2)}) collective-permute-start(bf16[2,32,768]{1,2,0:T(8,128)(2,1)} %copy.69), channel_id=1, source_target_pairs={{0,1},{1,0},{2,3},{3,2},{4,5},{5,4},{6,7},{7,6},{8,9},{9,8},{10,11... | collective-permute-start | bytes 294920 | tf_op jit(solution)/shard_map/ppermute | solution.py:20
  14.7 22.4 %collective-permute-start.1 = (bf16[2,64,768]{1,2,0:T(8,128)(2,1)}, bf16[2,64,768]{1,2,0:T(8,128)(2,1)}, u32[]{:S(2)}, u32[]{:S(2)}) collective-permute-start(bf16[2,64,768]{1,2,0:T(8,128)(2,1)} %pad_maximum_fusion.4), channel_id=1, source_target_pairs={{0,1},{1,0},{2,3},{3,2},{4,5},{5,4},{6,7},{7,6},{8,9},{9,8},{10,11... | collective-permute-start | bytes 589832 | tf_op jit(solution)/shard_map/ppermute | solution.py:20
  19.9 9.7 %copy-start.28 = (bf16[1,256,768]{2,1,0:T(8,128)(2,1)S(1)}, bf16[1,256,768]{2,1,0:T(8,128)(2,1)}, u32[]{:S(2)}) copy-start(bf16[1,256,768]{2,1,0:T(8,128)(2,1)} %param.12) | copy-start | bytes 1179652
  22.5 23.2 %collective-permute-start = (bf16[2,128,768]{1,2,0:T(8,128)(2,1)}, bf16[2,128,768]{1,2,0:T(8,128)(2,1)}, u32[]{:S(2)}, u32[]{:S(2)}) collective-permute-start(bf16[2,128,768]{1,2,0:T(8,128)(2,1)} %pad_maximum_fusion.3), channel_id=1, source_target_pairs={{0,1},{1,0},{2,3},{3,2},{4,5},{5,4},{6,7},{7,6},{8,9},{9,8},{10,11... | collective-permute-start | bytes 1179656 | tf_op jit(solution)/shard_map/ppermute | solution.py:20
  26.6 15.9 %collective-permute-start.4 = (bf16[2,64,768]{1,2,0:T(8,128)(2,1)}, bf16[2,64,768]{1,2,0:T(8,128)(2,1)}, u32[]{:S(2)}, u32[]{:S(2)}) collective-permute-start(bf16[2,64,768]{1,2,0:T(8,128)(2,1)} %maximum_select_fusion.4), channel_id=1, source_target_pairs={{0,2},{2,0},{1,3},{3,1},{4,6},{6,4},{5,7},{7,5},{8,10},{10,8},{9,1... | collective-permute-start | bytes 589832 | tf_op jit(solution)/shard_map/ppermute | solution.py:20
  30.9 5.1 copy-start.32
  30.9 6.2 copy-start.24
  30.9 6.2 copy-start.26
  38.7 25.3 %collective-permute-start.2 = (bf16[2,128,768]{1,2,0:T(8,128)(2,1)S(1)}, bf16[2,128,768]{1,2,0:T(8,128)(2,1)S(1)}, u32[]{:S(2)}, u32[]{:S(2)}) collective-permute-start(bf16[2,128,768]{1,2,0:T(8,128)(2,1)S(1)} %maximum_select_fusion.3), channel_id=1, source_target_pairs={{0,2},{2,0},{1,3},{3,1},{4,6},{6,4},{5,7},{7,5},{8,10},{10,8},{9,1... | collective-permute-start | bytes 1179656 | tf_op jit(solution)/shard_map/ppermute | solution.py:20
  44.3 20.0 %collective-permute-start.5 = (bf16[2,128,768]{1,2,0:T(8,128)(2,1)S(1)}, bf16[2,128,768]{1,2,0:T(8,128)(2,1)S(1)}, u32[]{:S(2)}, u32[]{:S(2)}) collective-permute-start(bf16[2,128,768]{1,2,0:T(8,128)(2,1)S(1)} %maximum_select_fusion.5), channel_id=1, source_target_pairs={{0,4},{4,0},{1,5},{5,1},{2,6},{6,2},{3,7},{7,3},{8,12},{12,8},{9,1... | collective-permute-start | bytes 1179656 | tf_op jit(solution)/shard_map/ppermute | solution.py:20
  66.7 4.8 copy-start.18
  89.3 4.8 copy-start.18
  100.6 4.8 copy-start.18
  111.9 4.8 copy-start.18
  123.2 4.8 copy-start.18
  142.1 448.6 %collective-permute-start.9 = (bf16[2,128,768]{1,2,0:T(8,128)(2,1)}, bf16[2,128,768]{1,2,0:T(8,128)(2,1)}, u32[]{:S(2)}, u32[]{:S(2)}) collective-permute-start(bf16[2,128,768]{1,2,0:T(8,128)(2,1)} %select_convert_fusion.2), channel_id=1, source_target_pairs={{0,4},{4,0},{1,5},{5,1},{2,6},{6,2},{3,7},{7,3},{8,12},{12,8},{9,1... | collective-permute-start | bytes 1179656 | tf_op jit(solution)/shard_map/ppermute | solution.py:20
  144.2 448.6 %collective-permute-start.7 = (bf16[2,128,768]{1,2,0:T(8,128)(2,1)}, bf16[2,128,768]{1,2,0:T(8,128)(2,1)}, u32[]{:S(2)}, u32[]{:S(2)}) collective-permute-start(bf16[2,128,768]{1,2,0:T(8,128)(2,1)} %select_convert_fusion.4), channel_id=1, source_target_pairs={{0,2},{2,0},{1,3},{3,1},{4,6},{6,4},{5,7},{7,5},{8,10},{10,8},{9,1... | collective-permute-start | bytes 1179656 | tf_op jit(solution)/shard_map/ppermute | solution.py:20
  145.1 449.9 %collective-permute-start.6 = (bf16[2,128,768]{1,2,0:T(8,128)(2,1)}, bf16[2,128,768]{1,2,0:T(8,128)(2,1)}, u32[]{:S(2)}, u32[]{:S(2)}) collective-permute-start(bf16[2,128,768]{1,2,0:T(8,128)(2,1)} %select_convert_fusion.5), channel_id=1, source_target_pairs={{0,1},{1,0},{2,3},{3,2},{4,5},{5,4},{6,7},{7,6},{8,9},{9,8},{10,11... | collective-permute-start | bytes 1179656 | tf_op jit(solution)/shard_map/ppermute | solution.py:20
  505.9 84.8 %copy-start.12 = (f32[256,6,128]{0,2,1:T(8,128)S(1)}, f32[256,6,128]{0,2,1:T(8,128)}, u32[]{:S(2)}) copy-start(f32[256,6,128]{0,2,1:T(8,128)} %copy-done.11) | copy-start | bytes 2359300
  505.9 84.8 %copy-start.14 = (f32[256,6,128]{0,2,1:T(8,128)S(1)}, f32[256,6,128]{0,2,1:T(8,128)}, u32[]{:S(2)}) copy-start(f32[256,6,128]{0,2,1:T(8,128)} %copy-done.13) | copy-start | bytes 2359300
  592.8 16.7 %collective-permute-start.10 = (bf16[2,64,768]{1,2,0:T(8,128)(2,1)}, bf16[2,64,768]{1,2,0:T(8,128)(2,1)}, u32[]{:S(2)}, u32[]{:S(2)}) collective-permute-start(bf16[2,64,768]{1,2,0:T(8,128)(2,1)} %select_convert_fusion.1), channel_id=1, source_target_pairs={{0,2},{2,0},{1,3},{3,1},{4,6},{6,4},{5,7},{7,5},{8,10},{10,8},{9,1... | collective-permute-start | bytes 589832 | tf_op jit(solution)/shard_map/ppermute | solution.py:20
  595.0 18.6 %collective-permute-start.8 = (bf16[2,64,768]{1,2,0:T(8,128)(2,1)}, bf16[2,64,768]{1,2,0:T(8,128)(2,1)}, u32[]{:S(2)}, u32[]{:S(2)}) collective-permute-start(bf16[2,64,768]{1,2,0:T(8,128)(2,1)} %select_convert_fusion.3), channel_id=1, source_target_pairs={{0,1},{1,0},{2,3},{3,2},{4,5},{5,4},{6,7},{7,6},{8,9},{9,8},{10,11... | collective-permute-start | bytes 589832 | tf_op jit(solution)/shard_map/ppermute | solution.py:20
  611.7 12.7 %collective-permute-start.11 = (bf16[2,32,768]{1,2,0:T(8,128)(2,1)}, bf16[2,32,768]{1,2,0:T(8,128)(2,1)}, u32[]{:S(2)}, u32[]{:S(2)}) collective-permute-start(bf16[2,32,768]{1,2,0:T(8,128)(2,1)} %select_convert_fusion), channel_id=1, source_target_pairs={{0,1},{1,0},{2,3},{3,2},{4,5},{5,4},{6,7},{7,6},{8,9},{9,8},{10,11... | collective-permute-start | bytes 294920 | tf_op jit(solution)/shard_map/ppermute | solution.py:20
  (46 other events, 93.9 us)
where the time goes:
time: 649 us; the launch traced here: 647 us
  blocking collectives  439 us (68%)
  local copies, waits for them, and re-layouts  99.5 us (15%)
  other arithmetic  45 us (7%)
  matrix products  26.9 us (4%)
  waiting for transfers between devices  21 us (3%)
  starting transfers between devices  12.6 us (2%)
    unnamed x1, blocking collectives  359 us
    psum x1, blocking collectives, shards(): summed = lax.psum(shares.astype(jnp.bfloat16), 'dp').astype(jnp.float32)  80.5 us
    dynamic_slice x24, local copies, waits for them, and re-layouts, shards(): lax.map(head_pair, (split_heads(query_rows), split_heads(key_all), split_...  28.8 us
    mul x18, local copies, waits for them, and re-layouts, spread_rows(): source.reshape(row_count, 1, HEADS, feature // HEADS)  25 us
    ppermute x12, waiting for transfers between devices, swapped(): return lax.ppermute(block, axis, route)  21 us
  transfers between devices with their start and end apart: 12, of which 3 were waited for; matrix products, arithmetic and copies ran while one was open for 10% of the time, Pallas kernels for 0%

commit v1 on v0

v1 whole, which is shorter than its diff:
```python
import functools
import math

import jax
import jax.numpy as jnp
from jax import lax
from jax.experimental import pallas as pl
from jax.experimental.pallas import tpu as pltpu
from jax.sharding import PartitionSpec as P

HEADS = 12
HEAD_DIM = 64
LEVELS = 3
PAIR = 2 * HEAD_DIM
VMEM_LIMIT = 48 * 1024 * 1024
F32 = jnp.float32
BF16 = jnp.bfloat16


def lane_masks(row_count):
    lane = lax.broadcasted_iota(jnp.int32, (row_count, PAIR), 1)
    return lane < HEAD_DIM, lane >= HEAD_DIM


def selection(offsets_ref, head, rows_dev, transposed):
    picked_count = rows_dev // 2 + rows_dev // 4 + rows_dev // 8
    shape = (rows_dev, picked_count) if transposed else (picked_count, rows_dev)
    slot = lax.broadcasted_iota(jnp.int32, shape, 1 if transposed else 0)
    row = lax.broadcasted_iota(jnp.int32, shape, 0 if transposed else 1)
    first, second = rows_dev // 2, rows_dev // 2 + rows_dev // 4
    target = jnp.where(
        slot < first,
        2 * slot + offsets_ref[0, head],
        jnp.where(
            slot < second,
            4 * (slot - first) + offsets_ref[1, head],
            8 * (slot - second) + offsets_ref[2, head],
        ),
    )
    return (row == target).astype(F32).astype(BF16)


def pick_kernel(first_pair, offsets_ref, key_ref, value_ref, near_ref, far_ref):
    rows_dev = key_ref.shape[1]
    head = 2 * (first_pair + pl.program_id(0))
    both = jnp.concatenate([key_ref[0], value_ref[0]], axis=1)
    rows = []
    for side in range(2):
        chosen = selection(offsets_ref, head + side, rows_dev, False)
        rows.append(jnp.dot(chosen, both, preferred_element_type=F32))
    low, _ = lane_masks(rows[0].shape[0])
    key_rows = jnp.where(low, rows[0][:, :PAIR], rows[1][:, :PAIR]).astype(BF16)
    value_rows = jnp.where(low, rows[0][:, PAIR:], rows[1][:, PAIR:]).astype(BF16)
    first, second, third = rows_dev // 2, rows_dev // 4, rows_dev // 8
    near_ref[:first] = key_rows[:first]
    near_ref[first:] = value_rows[:first]
    far_ref[:second] = key_rows[first : first + second]
    far_ref[second : 2 * second] = value_rows[first : first + second]
    far_ref[2 * second : 2 * second + third] = key_rows[first + second :]
    far_ref[2 * second + third :] = value_rows[first + second :]


def pick(offsets, keys, values, first_pair, pair_count):
    rows_dev = keys.shape[1]
    width = pair_count * PAIR
    whole = pl.BlockSpec((1, rows_dev, PAIR), lambda i: (0, 0, first_pair + i))
    return pl.pallas_call(
        functools.partial(pick_kernel, first_pair),
        grid=(pair_count,),
        in_specs=[pl.BlockSpec(memory_space=pltpu.SMEM), whole, whole],
        out_specs=[
            pl.BlockSpec((rows_dev, PAIR), lambda i: (0, i)),
            pl.BlockSpec((3 * rows_dev // 4, PAIR), lambda i: (0, i)),
        ],
        out_shape=[
            jax.ShapeDtypeStruct((rows_dev, width), BF16),
            jax.ShapeDtypeStruct((3 * rows_dev // 4, width), BF16),
        ],
        compiler_params=pltpu.CompilerParams(vmem_limit_bytes=VMEM_LIMIT),
        name="pick_rows",
    )(offsets, keys, values)


def attend_kernel(
    query_ref, key_ref, value_ref, grad_ref,
    near_ref, near_pair_ref, far_ref, far_pair_ref,
    third_in_ref, third_out_ref, fourth_in_ref, fourth_out_ref, cross_ref,
    attended_ref, query_grad_ref, local_ref,
    own1_ref, send1_ref, own2_ref, pair2_ref, send2_ref, own3_ref, pair3_ref, send3_ref, cross3_ref,
    keys_scr, values_scr, key_sum, value_sum,
):
    rows_dev = query_ref.shape[1]
    n1, n2, n3 = rows_dev // 2, rows_dev // 4, rows_dev // 8
    keys_scr[:rows_dev] = key_ref[0]
    values_scr[:rows_dev] = value_ref[0]
    at = rows_dev
    for source in (near_ref, near_pair_ref):
        keys_scr[at : at + n1] = source[:n1]
        values_scr[at : at + n1] = source[n1:]
        at += n1
    third = third_in_ref[...] + third_out_ref[...]
    fourth = fourth_in_ref[...] + fourth_out_ref[...]
    blocks = (far_ref[...], far_pair_ref[...], third, fourth)
    for block in blocks:
        keys_scr[at : at + n2] = block[:n2]
        values_scr[at : at + n2] = block[n2 : 2 * n2]
        at += n2
    for block in blocks:
        keys_scr[at : at + n3] = block[2 * n2 : 2 * n2 + n3]
        values_scr[at : at + n3] = block[2 * n2 + n3 :]
        at += n3
    for idx in range(4):
        base = 2 * n3 * idx
        keys_scr[at : at + n3] = cross_ref[base : base + n3]
        values_scr[at : at + n3] = cross_ref[base + n3 : base + 2 * n3]
        at += n3

    query = query_ref[0]
    grad = grad_ref[...]
    scaled = (query.astype(F32) * (1.0 / math.sqrt(HEAD_DIM))).astype(BF16)
    grad_t = grad.T
    keys_t = keys_scr[...].T
    values_t = values_scr[...].T
    nt = (((1,), (1,)), ((), ()))
    attended_parts = []
    query_parts = []
    for side, mask in enumerate(lane_masks(rows_dev)):
        rows = slice(side * HEAD_DIM, (side + 1) * HEAD_DIM)
        query_side = jnp.where(mask, scaled, jnp.zeros_like(scaled))
        grad_side = jnp.where(mask, grad, jnp.zeros_like(grad))
        scores = lax.dot_general(keys_scr[...], query_side, nt, preferred_element_type=F32)
        row_max = jnp.max(scores, axis=0, keepdims=True)
        raw = jnp.exp(scores - row_max)
        probs = raw * (1.0 / jnp.sum(raw, axis=0, keepdims=True))
        rounded = probs.astype(BF16)
        attended = jnp.dot(values_t[rows], rounded, preferred_element_type=F32).astype(BF16)
        attended_parts.append(attended)
        prob_grad = lax.dot_general(values_scr[...], grad_side, nt, preferred_element_type=F32)
        delta = jnp.sum(grad_t[rows].astype(F32) * attended.astype(F32), axis=0, keepdims=True)
        score_grad = (probs * (prob_grad - delta)).astype(BF16)
        query_parts.append(jnp.dot(keys_t[rows], score_grad, preferred_element_type=F32))
        key_part = jnp.dot(score_grad, query_side, preferred_element_type=F32)
        value_part = jnp.dot(rounded, grad_side, preferred_element_type=F32)
        if side == 0:
            key_sum[...] = key_part
            value_sum[...] = value_part
        else:
            key_sum[...] += key_part
            value_sum[...] += value_part
    attended_ref[...] = jnp.concatenate(attended_parts, axis=0).T
    query_t = jnp.concatenate(query_parts, axis=0) * (1.0 / math.sqrt(HEAD_DIM))
    query_grad_ref[0] = query_t.astype(BF16).T

    local_ref[:rows_dev] = key_sum[:rows_dev]
    local_ref[rows_dev:] = value_sum[:rows_dev]
    at = rows_dev
    own1_ref[:n1] = key_sum[at : at + n1]
    own1_ref[n1:] = value_sum[at : at + n1]
    at += n1
    send1_ref[:n1] = key_sum[at : at + n1].astype(BF16)
    send1_ref[n1:] = value_sum[at : at + n1].astype(BF16)
    at += n1
    for refs, step in (((own2_ref, pair2_ref, send2_ref), n2), ((own3_ref, pair3_ref, send3_ref), n3)):
        own, pair, send = refs
        for out, base in ((own, 0), (pair, 0), (send, 0), (send, 2 * step)):
            out[base : base + step] = key_sum[at : at + step].astype(out.dtype)
            out[base + step : base + 2 * step] = value_sum[at : at + step].astype(out.dtype)
            at += step
    for idx in range(4):
        base = 2 * n3 * idx
        cross3_ref[base : base + n3] = key_sum[at : at + n3].astype(BF16)
        cross3_ref[base + n3 : base + 2 * n3] = value_sum[at : at + n3].astype(BF16)
        at += n3


def attend(queries, keys, values, grads, near, near_pair, far, far_pair, third, fourth, cross, first_pair, pair_count):
    rows_dev = queries.shape[1]
    width = pair_count * PAIR
    whole = pl.BlockSpec((1, rows_dev, PAIR), lambda i: (0, 0, first_pair + i))

    def part(count):
        return pl.BlockSpec((count, PAIR), lambda i: (0, i))

    n1, n2, n3 = rows_dev, rows_dev // 2, rows_dev // 4
    far_rows = n2 + n3
    outs = [
        (rows_dev, BF16),
        (None, BF16),
        (2 * rows_dev, F32),
        (n1, F32), (n1, BF16),
        (n2, F32), (n2, F32), (2 * n2, BF16),
        (n3, F32), (n3, F32), (2 * n3, BF16), (4 * n3, BF16),
    ]
    set_rows = 4 * rows_dev
    return pl.pallas_call(
        attend_kernel,
        grid=(pair_count,),
        in_specs=[
            whole, whole, whole,
            pl.BlockSpec((rows_dev, PAIR), lambda i: (0, first_pair + i)),
            part(n1), part(n1),
            part(far_rows), part(far_rows),
            part(far_rows), part(far_rows), part(far_rows), part(far_rows),
            part(4 * n3),
        ],
        out_specs=[
            pl.BlockSpec((1, rows_dev, PAIR), lambda i: (0, 0, i)) if rows is None else part(rows)
            for rows, _ in outs
        ],
        out_shape=[
            jax.ShapeDtypeStruct((1, rows_dev, width) if rows is None else (rows, width), kind)
            for rows, kind in outs
        ],
        scratch_shapes=[
            pltpu.VMEM((set_rows, PAIR), BF16),
            pltpu.VMEM((set_rows, PAIR), BF16),
            pltpu.VMEM((set_rows, PAIR), F32),
            pltpu.VMEM((set_rows, PAIR), F32),
        ],
        compiler_params=pltpu.CompilerParams(vmem_limit_bytes=VMEM_LIMIT),
        cost_estimate=pl.CostEstimate(
            flops=12 * pair_count * 2 * set_rows * rows_dev * HEAD_DIM * 4,
            bytes_accessed=24 * rows_dev * width,
            transcendentals=2 * pair_count * set_rows * rows_dev,
        ),
        name="attend",
    )(queries, keys, values, grads, near, near_pair, far, far_pair, *third, *fourth, cross)


def spread_kernel(
    first_pair, offsets_ref, local_ref, own1_ref, back1_ref,
    own2_ref, mid2_ref, back2_ref, own3_ref, mid3_ref, back3_ref,
    key_ref, value_ref,
):
    rows_dev = local_ref.shape[0] // 2
    head = 2 * (first_pair + pl.program_id(0))
    totals = (
        own1_ref[...] + back1_ref[...].astype(F32),
        own2_ref[...] + mid2_ref[...].astype(F32) + back2_ref[...].astype(F32),
        own3_ref[...] + mid3_ref[...].astype(F32) + back3_ref[...].astype(F32),
    )
    key_rows = jnp.concatenate([t[: t.shape[0] // 2] for t in totals], axis=0)
    value_rows = jnp.concatenate([t[t.shape[0] // 2 :] for t in totals], axis=0)
    both = jnp.concatenate([key_rows, value_rows], axis=1).astype(BF16)
    spread = []
    for side in range(2):
        chosen = selection(offsets_ref, head + side, rows_dev, True)
        spread.append(jnp.dot(chosen, both, preferred_element_type=F32))
    low, _ = lane_masks(rows_dev)
    key_ref[0] = (local_ref[:rows_dev] + jnp.where(low, spread[0][:, :PAIR], spread[1][:, :PAIR])).astype(BF16)
    value_ref[0] = (local_ref[rows_dev:] + jnp.where(low, spread[0][:, PAIR:], spread[1][:, PAIR:])).astype(BF16)


def spread(offsets, parts, first_pair, pair_count):
    rows_dev = parts[0].shape[0] // 2
    width = pair_count * PAIR
    out = pl.BlockSpec((1, rows_dev, PAIR), lambda i: (0, 0, i))
    shape = jax.ShapeDtypeStruct((1, rows_dev, width), BF16)
    return pl.pallas_call(
        functools.partial(spread_kernel, first_pair),
        grid=(pair_count,),
        in_specs=[pl.BlockSpec(memory_space=pltpu.SMEM)]
        + [pl.BlockSpec((part.shape[0], PAIR), lambda i: (0, i)) for part in parts],
        out_specs=[out, out],
        out_shape=[shape, shape],
        compiler_params=pltpu.CompilerParams(vmem_limit_bytes=VMEM_LIMIT),
        name="spread_rows",
    )(offsets, *parts)


def routes(shard_count):
    place = range(shard_count)
    return {
        "pair": [(i, i ^ 1) for i in place],
        "middle": [(i, i + 1 if i % 4 == 1 else i - 1) for i in place if i % 4 in (1, 2)],
        "outward": [(i, i - 1 if i % 4 == 1 else i + 1) for i in place if i % 4 in (1, 2)],
        "inward": [(i, i + 1 if i % 4 == 0 else i - 1) for i in place if i % 4 in (0, 3)],
        "cross": [(i, i ^ 4) for i in place],
    }


def weight_share(cotangent, attended, norm_factor):
    shard_count = lax.axis_size("seq")
    core = lax.axis_index("dp") % 2
    position = lax.axis_index("seq")
    feature = cotangent.shape[1]
    half = feature // 2
    product = lax.dot_general(
        cotangent, attended, (((0,), (0,)), ((), ())), preferred_element_type=F32
    )
    kept = lax.dynamic_slice_in_dim(product, core * half, half, 1)
    sent = lax.dynamic_slice_in_dim(product, (1 - core) * half, half, 1).astype(BF16)
    slide_route = [(i, i ^ 1) for i in range(lax.axis_size("dp"))]
    far_route = [(i, i ^ 2) for i in range(lax.axis_size("dp"))]
    total = (kept + lax.ppermute(sent, "dp", slide_route).astype(F32)).astype(BF16)
    along = 4
    plane = shard_count // along
    x_idx = position // plane
    rows = feature // along
    shares = lax.dynamic_slice_in_dim(total, x_idx * rows, rows, 0).astype(F32)
    for step in (1, 3, 2):
        target = (x_idx + step) % along
        outgoing = lax.dynamic_slice_in_dim(total, target * rows, rows, 0)
        route = [(i, (i + step * plane) % shard_count) for i in range(shard_count)]
        shares = shares + lax.ppermute(outgoing, "seq", route).astype(F32)
    shares = shares.astype(BF16).reshape(plane, rows // plane, half)
    groups = [[g * plane + i for i in range(plane)] for g in range(along)]
    shares = lax.all_to_all(shares, "seq", 0, 0, axis_index_groups=groups, tiled=True)
    shares = jnp.sum(shares.astype(F32), axis=0).astype(BF16)
    other = lax.ppermute(shares, "dp", far_route)
    summed = ((shares.astype(F32) + other.astype(F32)) * norm_factor).astype(BF16)
    across = lax.ppermute(summed, "dp", slide_route)
    return jnp.where(
        core == 0,
        jnp.concatenate([summed, across], 1),
        jnp.concatenate([across, summed], 1),
    )


def gather(near, far, rows_dev, route):
    def move(block, name):
        return lax.ppermute(block, "seq", route[name])

    n3 = rows_dev // 4
    far_pair = move(far, "pair")
    third_in = move(far, "middle")
    fourth_in = move(far_pair, "middle")
    third_out = move(third_in, "outward")
    fourth_out = move(fourth_in, "outward")
    near_pair = move(near, "pair")
    mine = jnp.concatenate(
        [far[-n3:], far_pair[-n3:], (third_in + third_out)[-n3:], (fourth_in + fourth_out)[-n3:]], 0
    )
    cross = move(mine, "cross")
    return near_pair, far_pair, (third_in, third_out), (fourth_in, fourth_out), cross


def give_back(outs, route):
    def move(block, name):
        return lax.ppermute(block, "seq", route[name])

    own1, send1, own2, pair2, send2, own3, pair3, send3, cross3 = outs
    cross = move(cross3, "cross")
    ways = []
    n3 = own3.shape[0]
    own3 = own3 + cross[:n3].astype(F32)
    pair3 = pair3 + cross[n3 : 2 * n3].astype(F32)
    send3 = (send3.astype(F32) + cross[2 * n3 :].astype(F32)).astype(BF16)
    for own, pair, send in ((own2, pair2, send2), (own3, pair3, send3)):
        count = own.shape[0]
        inward = move(send, "inward")
        passed = (send.astype(F32) + inward.astype(F32)).astype(BF16)
        middle = move(passed, "middle")
        last = (pair + middle[count:].astype(F32)).astype(BF16)
        ways.append((own, middle[:count], move(last, "pair")))
    back1 = move(send1, "pair")
    return (own1, back1) + ways[0] + ways[1]


def shards(queries, keys, values, out_weight, out_cotangent, offsets):
    rows_dev, feature = queries.shape[1:]
    cotangent = out_cotangent[0]
    route = routes(lax.axis_size("seq"))
    pairs = HEADS // 2
    near, far = pick(offsets, keys, values, 0, pairs)
    gathered = gather(near, far, rows_dev, route)
    near_pair, far_pair, third, fourth, cross = gathered
    grads = jnp.dot(cotangent, out_weight, preferred_element_type=F32).astype(BF16)
    results = attend(
        queries, keys, values, grads, near, near_pair, far, far_pair, third, fourth, cross, 0, pairs
    )
    attended, query_grad, local = results[:3]
    key_grad, value_grad = spread(offsets, (local,) + give_back(results[3:], route), 0, pairs)
    mixed = lax.dot_general(
        attended, out_weight, (((1,), (1,)), ((), ())), preferred_element_type=F32
    ).astype(BF16)
    tiles = lax.axis_size("dp") * lax.axis_size("seq") * rows_dev
    weight_grad = weight_share(cotangent, attended, 1.0 / math.sqrt(tiles))
    return mixed[None], query_grad, key_grad, value_grad, weight_grad


def solution(mesh):
    split = P("dp", "seq", None)
    return jax.shard_map(
        shards,
        mesh=mesh,
        in_specs=(split, split, split, P(), split, P()),
        out_specs=(split, split, split, split, P("seq", None)),
        check_vma=False,
    )
```

time: 649 us -> 131 us (0.20)
  blocking collectives: 439 us -> 0 us
  local copies, waits for them, and re-layouts: 99.5 us -> 10.7 us
  starting transfers between devices: 12.6 us -> 59.6 us
  other arithmetic: 45 us -> 7.69 us
  Pallas kernels: 0 us -> 28.1 us
  matrix products: 26.9 us -> 3 us
    unnamed x1 -> x0, blocking collectives: 359 us -> none
    psum x1 -> x0, blocking collectives: 80.5 us -> none  [shards(): summed = lax.psum(shares.astype(jnp.bfloat16), 'dp').astype(jnp.float32)]
    ppermute x12 -> x21, starting transfers between devices: 12.6 us -> 53.4 us  [the longest x15 32.5 us: move(): return lax.ppermute(block, 'seq', route[name])]
    dynamic_slice x24 -> x1, local copies, waits for them, and re-layouts: 28.8 us -> 0.06 us  [weight_share(): outgoing = lax.dynamic_slice_in_dim(total, target * rows, rows, 0)]
    pallas_call x0 -> x3, Pallas kernels: none -> 28.1 us  [the longest x1 22 us: attend(): pl.pallas_call(attend_kernel, grid=(pair_count,), in_specs=[whole, whole,...]
    mul x18 -> x0, local copies, waits for them, and re-layouts: 25 us -> none  [spread_rows(): source.reshape(row_count, 1, HEADS, feature // HEADS)]
    dot_general x34 -> x2, matrix products: 14.4 us -> 1.75 us  [the longest x1 1.23 us: shards(): jnp.dot(cotangent, out_weight, preferred_element_type=F32).astype(BF16)]
    dynamic_update_slice x12 -> x0, local copies, waits for them, and re-layouts: 10.7 us -> none  [shards(): lax.map(head_pair, (split_heads(query_rows), split_heads(key_all), split_...]
  transfers between devices with their start and end apart: 12 -> 22, of which waited for: 3 -> 7; matrix products, arithmetic and copies ran while one was open for 10% -> 10% of each run, Pallas kernels for 0% -> 3%
where the time goes in v1:
time: 131 us
  starting transfers between devices  59.6 us (45%)
  Pallas kernels  28.1 us (21%)
  waiting for transfers between devices  20.4 us (16%)
  local copies, waits for them, and re-layouts  10.7 us (8%)
  other arithmetic  7.69 us (6%)
  matrix products  3 us (2%)
    ppermute x15, starting transfers between devices, move(): return lax.ppermute(block, 'seq', route[name])  32.5 us
    pallas_call x1, Pallas kernels, attend(): pl.pallas_call(attend_kernel, grid=(pair_count,), in_specs=[whole, whole,...  22 us
    ppermute x15, waiting for transfers between devices, move(): return lax.ppermute(block, 'seq', route[name])  18 us
    ppermute x1, starting transfers between devices, weight_share(): across = lax.ppermute(summed, 'dp', slide_route)  7.27 us
    unnamed x72, local copies, waits for them, and re-layouts  7.12 us
    all_to_all x1, starting transfers between devices, weight_share(): lax.all_to_all(shares, 'seq', 0, 0, axis_index_groups=groups, tiled=True)  6.27 us
    ppermute x3, starting transfers between devices, weight_share(): shares = shares + lax.ppermute(outgoing, 'seq', route).astype(F32)  4.91 us
    ppermute x1, starting transfers between devices, weight_share(): other = lax.ppermute(shares, 'dp', far_route)  4.83 us
  transfers between devices with their start and end apart: 22, of which 7 were waited for; matrix products, arithmetic and copies ran while one was open for 10% of the time, Pallas kernels for 3%

profile of v1, /device:TPU:1, one launch (start us, length us, event | category | flops | bytes accessed | tf_op | source)
XLA Modules:
  0.0 130.7 jit_solution(16944421520552858019)
XLA Ops:
  3.4 2.3 %pick_rows.1 = (bf16[256,768]{1,0:T(8,128)(2,1)S(1)}, bf16[192,768]{1,0:T(8,128)(2,1)S(1)}) custom-call(s32[3,12]{1,0:T(4,128)S(1)} %copy-done.25, bf16[1,256,768]{2,1,0:T(8,128)(2,1)S(1)} %copy-done.3, bf16[1,256,768]{2,1,0:T(8,128)(2,1)S(1)} %copy-done.5), custom_call_target="tpu_custom_call" | custom-call | tf_op jit(solution)/shard_map/pick_rows/pallas_call | solution.py:67
  5.7 2.6 %collective-permute-start.1 = (bf16[192,768]{1,0:T(8,128)(2,1)S(1)}, bf16[192,768]{1,0:T(8,128)(2,1)S(1)}, u32[]{:S(2)}, u32[]{:S(2)}) collective-permute-start(bf16[192,768]{1,0:T(8,128)(2,1)S(1)} %get-tuple-element.22.far_ref), channel_id=1, source_target_pairs={{0,1},{1,0},{2,3},{3,2},{4,5},{5,4},{6,7},{7,6},{8,9},{9,8},{10,11... | collective-permute-start | bytes 884744 | tf_op jit(solution)/shard_map/ppermute | solution.py:322
  9.0 5.0 %collective-permute-done.1.far_pair_ref = bf16[192,768]{1,0:T(8,128)(2,1)S(1)} collective-permute-done((bf16[192,768]{1,0:T(8,128)(2,1)S(1)}, bf16[192,768]{1,0:T(8,128)(2,1)S(1)}, u32[]{:S(2)}, u32[]{:S(2)}) %collective-permute-start.1) | collective-permute-done | bytes 294944 | tf_op jit(solution)/shard_map/ppermute | solution.py:322
  14.7 1.3 collective-permute-start.3
  16.0 1.3 collective-permute-start.5
  17.3 10.2 %collective-permute-start = (bf16[256,768]{1,0:T(8,128)(2,1)S(1)}, bf16[256,768]{1,0:T(8,128)(2,1)S(1)}, u32[]{:S(2)}, u32[]{:S(2)}) collective-permute-start(bf16[256,768]{1,0:T(8,128)(2,1)S(1)} %get-tuple-element.21.near_ref), channel_id=1, source_target_pairs={{0,1},{1,0},{2,3},{3,2},{4,5},{5,4},{6,7},{7,6},{8,9},{9,8},{10,11... | collective-permute-start | bytes 1179656 | tf_op jit(solution)/shard_map/ppermute | solution.py:322
  27.5 5.9 %collective-permute-done.5.fourth_out_ref = bf16[192,768]{1,0:T(8,128)(2,1)S(1)} collective-permute-done((bf16[192,768]{1,0:T(8,128)(2,1)S(1)}, bf16[192,768]{1,0:T(8,128)(2,1)S(1)}, u32[]{:S(2)}, u32[]{:S(2)}) %collective-permute-start.5) | collective-permute-done | bytes 294944 | tf_op jit(solution)/shard_map/ppermute | solution.py:322
  36.9 5.1 %collective-permute-done.near_pair_ref = bf16[256,768]{1,0:T(8,128)(2,1)S(1)} collective-permute-done((bf16[256,768]{1,0:T(8,128)(2,1)S(1)}, bf16[256,768]{1,0:T(8,128)(2,1)S(1)}, u32[]{:S(2)}, u32[]{:S(2)}) %collective-permute-start) | collective-permute-done | bytes 393248 | tf_op jit(solution)/shard_map/ppermute | solution.py:322
  45.7 22.0 %attend.1 = (bf16[256,768]{1,0:T(8,128)(2,1)S(1)}, bf16[1,256,768]{2,1,0:T(8,128)(2,1)}, f32[512,768]{1,0:T(8,128)}, f32[256,768]{1,0:T(8,128)}, bf16[256,768]{1...) custom-call(bf16[1,256,768]{2,1,0:T(8,128)(2,1)S(1)} %copy-done.27, ...), custom_call_target="tpu_custom_call" | custom-call | flops 9663676416 | bytes 4718592 | tf_op jit(solution)/shard_map/attend/pallas_call | solution.py:195
  67.7 1.3 %collective-permute-start.8 = (bf16[256,768]{1,0:T(8,128)(2,1)S(1)}, bf16[256,768]{1,0:T(8,128)(2,1)S(1)}, u32[]{:S(2)}, u32[]{:S(2)}) collective-permute-start(bf16[256,768]{1,0:T(8,128)(2,1)S(1)} %get-tuple-element.29), channel_id=1, source_target_pairs={{0,1},{3,2},{4,5},{7,6},{8,9},{11,10},{12,13},{15,14},{16,17},{19,... | collective-permute-start | bytes 1179656 | tf_op jit(solution)/shard_map/ppermute | solution.py:340
  71.2 3.9 %collective-permute-start.15 = (bf16[768,384]{1,0:T(8,128)(2,1)}, bf16[768,384]{1,0:T(8,128)(2,1)}, u32[]{:S(2)}, u32[]{:S(2)}) collective-permute-start(bf16[768,384]{1,0:T(8,128)(2,1)} %fusion.2), channel_id=1, source_target_pairs={{0,64},{64,0},{128,192},{192,128},{1,65},{65,1},{129,193},{193,129... | collective-permute-start | bytes 1769480 | tf_op jit(solution)/shard_map/ppermute | solution.py:295
  77.2 1.5 %collective-permute-start.9 = (bf16[256,768]{1,0:T(8,128)(2,1)}, bf16[256,768]{1,0:T(8,128)(2,1)}, u32[]{:S(2)}, u32[]{:S(2)}) collective-permute-start(bf16[256,768]{1,0:T(8,128)(2,1)} %add_convert_fusion), channel_id=1, source_target_pairs={{1,2},{2,1},{5,6},{6,5},{9,10},{10,9},{13,14},{14,13},{17,18},{18,... | collective-permute-start | bytes 1179656 | tf_op jit(solution)/shard_map/ppermute | solution.py:340
  78.7 1.6 %fusion.1 = bf16[768,384]{1,0:T(8,128)(2,1)S(1)} fusion(bf16[768,384]{1,0:T(8,128)(2,1)} %collective-permute-done.15, f32[768,768]{0,1:T(8,128)} %copy-done.31, s32[]{:T(128)S(6)} %select_n.51), kind=kLoop, calls=%fused_computation.4 | loop fusion | flops 884736 | bytes 2359300 | tf_op jit(solution)/shard_map/convert_element_type | solution.py:295
  80.4 2.8 %collective-permute-start.18 = (bf16[192,384]{1,0:T(8,128)(2,1)S(1)}, bf16[192,384]{1,0:T(8,128)(2,1)S(1)}, u32[]{:S(2)}, u32[]{:S(2)}) collective-permute-start(bf16[192,384]{1,0:T(8,128)(2,1)S(1)} %get-tuple-element.38), channel_id=1, source_target_pairs={{0,32},{1,33},{2,34},{3,35},{4,36},{5,37},{6,38},{7,39},{8,40},{9,... | collective-permute-start | bytes 442376 | tf_op jit(solution)/shard_map/ppermute | solution.py:305
  84.1 1.9 %collective-permute-done.11 = bf16[256,768]{1,0:T(8,128)(2,1)S(1)} collective-permute-done((bf16[256,768]{1,0:T(8,128)(2,1)}, bf16[256,768]{1,0:T(8,128)(2,1)S(1)}, u32[]{:S(2)}, u32[]{:S(2)}) %collective-permute-start.11) | collective-permute-done | bytes 393248 | tf_op jit(solution)/shard_map/ppermute | solution.py:340
  87.3 4.7 %collective-permute-start.12 = (bf16[128,768]{1,0:T(8,128)(2,1)S(1)}, bf16[128,768]{1,0:T(8,128)(2,1)}, u32[]{:S(2)}, u32[]{:S(2)}) collective-permute-start(bf16[128,768]{1,0:T(8,128)(2,1)S(1)} %add_convert_fusion.2), channel_id=1, source_target_pairs={{0,1},{3,2},{4,5},{7,6},{8,9},{11,10},{12,13},{15,14},{16,17},{19,... | collective-permute-start | bytes 589832 | tf_op jit(solution)/shard_map/ppermute | solution.py:340
  92.9 6.3 %all-to-all-start = ((bf16[16,12,384]{2,1,0:T(8,128)(2,1)}), bf16[16,12,384]{2,1,0:T(8,128)(2,1)S(1)}, u32[]{:S(2)}, u32[]{:S(2)}) async-start(bf16[16,12,384]{2,1,0:T(8,128)(2,1)} %reshape.13), calls=%async_computation | async-start | bytes 393216 | tf_op jit(solution)/shard_map/all_to_all | solution.py:308
  99.1 1.6 %add_convert_fusion.1 = bf16[128,768]{1,0:T(8,128)(2,1)} fusion(bf16[128,768]{1,0:T(8,128)(2,1)} %collective-permute-done.12, bf16[128,768]{1,0:T(8,128)(2,1)S(1)} %add_convert_fusion.2), kind=kLoop, calls=%fused_computation.12 | loop fusion | flops 393216 | bytes 589824 | tf_op jit(solution)/shard_map/convert_element_type | solution.py:352
  100.8 1.3 %collective-permute-start.13 = (bf16[128,768]{1,0:T(8,128)(2,1)}, bf16[128,768]{1,0:T(8,128)(2,1)}, u32[]{:S(2)}, u32[]{:S(2)}) collective-permute-start(bf16[128,768]{1,0:T(8,128)(2,1)} %add_convert_fusion.1), channel_id=1, source_target_pairs={{1,2},{2,1},{5,6},{6,5},{9,10},{10,9},{13,14},{14,13},{17,18},{18,... | collective-permute-start | bytes 589832 | tf_op jit(solution)/shard_map/ppermute | solution.py:340
  103.1 3.4 %collective-permute-start.10 = (bf16[128,768]{1,0:T(8,128)(2,1)S(1)}, bf16[128,768]{1,0:T(8,128)(2,1)S(1)}, u32[]{:S(2)}, u32[]{:S(2)}) collective-permute-start(bf16[128,768]{1,0:T(8,128)(2,1)S(1)} %add_convert_fusion.3), channel_id=1, source_target_pairs={{0,1},{1,0},{2,3},{3,2},{4,5},{5,4},{6,7},{7,6},{8,9},{9,8},{10,11... | collective-permute-start | bytes 589832 | tf_op jit(solution)/shard_map/ppermute | solution.py:340
  106.8 4.8 %collective-permute-start.19 = (bf16[12,384]{1,0:T(8,128)(2,1)S(1)}, bf16[12,384]{1,0:T(8,128)(2,1)S(1)}, u32[]{:S(2)}, u32[]{:S(2)}) collective-permute-start(bf16[12,384]{1,0:T(8,128)(2,1)S(1)} %reduce_sum.12), channel_id=1, source_target_pairs={{0,128},{64,192},{128,0},{192,64},{1,129},{65,193},{129,1},{193,65... | collective-permute-start | bytes 27656 | tf_op jit(solution)/shard_map/ppermute | solution.py:310
  113.7 2.1 %collective-permute-done.19 = bf16[12,384]{1,0:T(8,128)(2,1)S(1)} collective-permute-done((bf16[12,384]{1,0:T(8,128)(2,1)S(1)}, bf16[12,384]{1,0:T(8,128)(2,1)S(1)}, u32[]{:S(2)}, u32[]{:S(2)}) %collective-permute-start.19) | collective-permute-done | bytes 9248 | tf_op jit(solution)/shard_map/ppermute | solution.py:310
  115.8 7.3 %collective-permute-start.20 = (bf16[12,384]{1,0:T(8,128)(2,1)S(1)}, bf16[12,384]{1,0:T(8,128)(2,1)S(1)}, u32[]{:S(2)}, u32[]{:S(2)}) collective-permute-start(bf16[12,384]{1,0:T(8,128)(2,1)S(1)} %multiply_convert_fusion), channel_id=1, source_target_pairs={{0,64},{64,0},{128,192},{192,128},{1,65},{65,1},{129,193},{193,129... | collective-permute-start | bytes 27656 | tf_op jit(solution)/shard_map/ppermute | solution.py:312
  126.2 3.8 %spread_rows.1 = (bf16[1,256,768]{2,1,0:T(8,128)(2,1)}, bf16[1,256,768]{2,1,0:T(8,128)(2,1)}) custom-call(s32[3,12]{1,0:T(4,128)S(1)} %copy-done.26, f32[512,768]{1,0:T(8,128)S(1)} %copy-done.1, f32[256,768]{1,0:T(8,128)S(1)} %copy-done.2, bf16[256,768]{1,0:T(8,128)(2,1)S(1)} %collective-permute-done.7.back1_ref, f32[128,768]{1,0:T(8,128)S(1)} %get-tuple-element.28.own2_ref, ...), custom_call_target="tpu_custom_call" | custom-call | tf_op jit(solution)/shard_map/spread_rows/pallas_call | solution.py:259
  (118 shorter events, 25.6 us)
Async XLA Ops:
  0.6 35.0 %copy-start = (bf16[768,768]{1,0:T(8,128)(2,1)S(1)}, bf16[768,768]{1,0:T(8,128)(2,1)}, u32[]{:S(2)}) copy-start(bf16[768,768]{1,0:T(8,128)(2,1)} %param.9) | copy-start | bytes 3538948
  5.7 36.2 %copy-start.30 = (bf16[256,768]{1,0:T(8,128)(2,1)}, bf16[256,768]{1,0:T(8,128)(2,1)S(1)}, u32[]{:S(2)}) copy-start(bf16[256,768]{1,0:T(8,128)(2,1)S(1)} %get-tuple-element.21.near_ref) | copy-start | bytes 1179652
  5.7 8.2 %collective-permute-start.1 = (bf16[192,768]{1,0:T(8,128)(2,1)S(1)}, bf16[192,768]{1,0:T(8,128)(2,1)S(1)}, u32[]{:S(2)}, u32[]{:S(2)}) collective-permute-start(bf16[192,768]{1,0:T(8,128)(2,1)S(1)} %get-tuple-element.22.far_ref), channel_id=1, source_target_pairs={{0,1},{1,0},{2,3},{3,2},{4,5},{5,4},{6,7},{7,6},{8,9},{9,8},{10,11... | collective-permute-start | bytes 884744 | tf_op jit(solution)/shard_map/ppermute | solution.py:322
  8.3 6.4 %collective-permute-start.2 = (bf16[192,768]{1,0:T(8,128)(2,1)S(1)}, bf16[192,768]{1,0:T(8,128)(2,1)S(1)}, u32[]{:S(2)}, u32[]{:S(2)}) collective-permute-start(bf16[192,768]{1,0:T(8,128)(2,1)S(1)} %get-tuple-element.22.far_ref), channel_id=1, source_target_pairs={{1,2},{2,1},{5,6},{6,5},{9,10},{10,9},{13,14},{14,13},{17,18},{18,... | collective-permute-start | bytes 884744 | tf_op jit(solution)/shard_map/ppermute | solution.py:322
  14.0 2.0 %collective-permute-start.4 = (bf16[192,768]{1,0:T(8,128)(2,1)S(1)}, bf16[192,768]{1,0:T(8,128)(2,1)S(1)}, u32[]{:S(2)}, u32[]{:S(2)}) collective-permute-start(bf16[192,768]{1,0:T(8,128)(2,1)S(1)} %collective-permute-done.1.far_pair_ref), channel_id=1, source_target_pairs={{1,2},{2,1},{5,6},{6,5},{9,10},{10,9},{13,14},{14,13},{17,18},{18,... | collective-permute-start | bytes 884744 | tf_op jit(solution)/shard_map/ppermute | solution.py:322
  14.7 12.8 %collective-permute-start.3 = (bf16[192,768]{1,0:T(8,128)(2,1)S(1)}, bf16[192,768]{1,0:T(8,128)(2,1)S(1)}, u32[]{:S(2)}, u32[]{:S(2)}) collective-permute-start(bf16[192,768]{1,0:T(8,128)(2,1)S(1)} %collective-permute-done.2.third_in_ref), channel_id=1, source_target_pairs={{1,0},{2,3},{5,4},{6,7},{9,8},{10,11},{13,12},{14,15},{17,16},{18,... | collective-permute-start | bytes 884744 | tf_op jit(solution)/shard_map/ppermute | solution.py:322
  16.0 17.5 %collective-permute-start.5 = (bf16[192,768]{1,0:T(8,128)(2,1)S(1)}, bf16[192,768]{1,0:T(8,128)(2,1)S(1)}, u32[]{:S(2)}, u32[]{:S(2)}) collective-permute-start(bf16[192,768]{1,0:T(8,128)(2,1)S(1)} %collective-permute-done.4.fourth_in_ref), channel_id=1, source_target_pairs={{1,0},{2,3},{5,4},{6,7},{9,8},{10,11},{13,12},{14,15},{17,16},{18,... | collective-permute-start | bytes 884744 | tf_op jit(solution)/shard_map/ppermute | solution.py:322
  17.3 24.7 %collective-permute-start = (bf16[256,768]{1,0:T(8,128)(2,1)S(1)}, bf16[256,768]{1,0:T(8,128)(2,1)S(1)}, u32[]{:S(2)}, u32[]{:S(2)}) collective-permute-start(bf16[256,768]{1,0:T(8,128)(2,1)S(1)} %get-tuple-element.21.near_ref), channel_id=1, source_target_pairs={{0,1},{1,0},{2,3},{3,2},{4,5},{5,4},{6,7},{7,6},{8,9},{9,8},{10,11... | collective-permute-start | bytes 1179656 | tf_op jit(solution)/shard_map/ppermute | solution.py:322
  34.3 8.4 %collective-permute-start.6 = (bf16[256,768]{1,0:T(8,128)(2,1)}, bf16[256,768]{1,0:T(8,128)(2,1)}, u32[]{:S(2)}, u32[]{:S(2)}) collective-permute-start(bf16[256,768]{1,0:T(8,128)(2,1)} %pad_maximum_fusion), channel_id=1, source_target_pairs={{0,4},{1,5},{2,6},{3,7},{4,0},{5,1},{6,2},{7,3},{8,12},{9,13},{10,... | collective-permute-start | bytes 1179656 | tf_op jit(solution)/shard_map/ppermute | solution.py:322
  67.7 8.6 %collective-permute-start.8 = (bf16[256,768]{1,0:T(8,128)(2,1)S(1)}, bf16[256,768]{1,0:T(8,128)(2,1)S(1)}, u32[]{:S(2)}, u32[]{:S(2)}) collective-permute-start(bf16[256,768]{1,0:T(8,128)(2,1)S(1)} %get-tuple-element.29), channel_id=1, source_target_pairs={{0,1},{3,2},{4,5},{7,6},{8,9},{11,10},{12,13},{15,14},{16,17},{19,... | collective-permute-start | bytes 1179656 | tf_op jit(solution)/shard_map/ppermute | solution.py:340
  71.2 7.6 %collective-permute-start.15 = (bf16[768,384]{1,0:T(8,128)(2,1)}, bf16[768,384]{1,0:T(8,128)(2,1)}, u32[]{:S(2)}, u32[]{:S(2)}) collective-permute-start(bf16[768,384]{1,0:T(8,128)(2,1)} %fusion.2), channel_id=1, source_target_pairs={{0,64},{64,0},{128,192},{192,128},{1,65},{65,1},{129,193},{193,129... | collective-permute-start | bytes 1769480 | tf_op jit(solution)/shard_map/ppermute | solution.py:295
  75.0 51.1 %collective-permute-start.7 = (bf16[256,768]{1,0:T(8,128)(2,1)}, bf16[256,768]{1,0:T(8,128)(2,1)S(1)}, u32[]{:S(2)}, u32[]{:S(2)}) collective-permute-start(bf16[256,768]{1,0:T(8,128)(2,1)} %copy-done.28), channel_id=1, source_target_pairs={{0,1},{1,0},{2,3},{3,2},{4,5},{5,4},{6,7},{7,6},{8,9},{9,8},{10,11... | collective-permute-start | bytes 1179656 | tf_op jit(solution)/shard_map/ppermute | solution.py:340
  75.0 11.0 %collective-permute-start.11 = (bf16[256,768]{1,0:T(8,128)(2,1)}, bf16[256,768]{1,0:T(8,128)(2,1)S(1)}, u32[]{:S(2)}, u32[]{:S(2)}) collective-permute-start(bf16[256,768]{1,0:T(8,128)(2,1)} %copy-done.29), channel_id=1, source_target_pairs={{0,4},{1,5},{2,6},{3,7},{4,0},{5,1},{6,2},{7,3},{8,12},{9,13},{10,... | collective-permute-start | bytes 1179656 | tf_op jit(solution)/shard_map/ppermute | solution.py:340
  77.2 24.9 %collective-permute-start.9 = (bf16[256,768]{1,0:T(8,128)(2,1)}, bf16[256,768]{1,0:T(8,128)(2,1)}, u32[]{:S(2)}, u32[]{:S(2)}) collective-permute-start(bf16[256,768]{1,0:T(8,128)(2,1)} %add_convert_fusion), channel_id=1, source_target_pairs={{1,2},{2,1},{5,6},{6,5},{9,10},{10,9},{13,14},{14,13},{17,18},{18,... | collective-permute-start | bytes 1179656 | tf_op jit(solution)/shard_map/ppermute | solution.py:340
  80.4 6.9 %collective-permute-start.18 = (bf16[192,384]{1,0:T(8,128)(2,1)S(1)}, bf16[192,384]{1,0:T(8,128)(2,1)S(1)}, u32[]{:S(2)}, u32[]{:S(2)}) collective-permute-start(bf16[192,384]{1,0:T(8,128)(2,1)S(1)} %get-tuple-element.38), channel_id=1, source_target_pairs={{0,32},{1,33},{2,34},{3,35},{4,36},{5,37},{6,38},{7,39},{8,40},{9,... | collective-permute-start | bytes 442376 | tf_op jit(solution)/shard_map/ppermute | solution.py:305
  83.2 8.8 %collective-permute-start.17 = (bf16[192,384]{1,0:T(8,128)(2,1)S(1)}, bf16[192,384]{1,0:T(8,128)(2,1)S(1)}, u32[]{:S(2)}, u32[]{:S(2)}) collective-permute-start(bf16[192,384]{1,0:T(8,128)(2,1)S(1)} %get-tuple-element.39), channel_id=1, source_target_pairs={{0,48},{1,49},{2,50},{3,51},{4,52},{5,53},{6,54},{7,55},{8,56},{9,... | collective-permute-start | bytes 442376 | tf_op jit(solution)/shard_map/ppermute | solution.py:305
  86.0 6.0 %collective-permute-start.16 = (bf16[192,384]{1,0:T(8,128)(2,1)S(1)}, bf16[192,384]{1,0:T(8,128)(2,1)S(1)}, u32[]{:S(2)}, u32[]{:S(2)}) collective-permute-start(bf16[192,384]{1,0:T(8,128)(2,1)S(1)} %get-tuple-element.37), channel_id=1, source_target_pairs={{0,16},{1,17},{2,18},{3,19},{4,20},{5,21},{6,22},{7,23},{8,24},{9,... | collective-permute-start | bytes 442376 | tf_op jit(solution)/shard_map/ppermute | solution.py:305
  87.3 11.8 %collective-permute-start.12 = (bf16[128,768]{1,0:T(8,128)(2,1)S(1)}, bf16[128,768]{1,0:T(8,128)(2,1)}, u32[]{:S(2)}, u32[]{:S(2)}) collective-permute-start(bf16[128,768]{1,0:T(8,128)(2,1)S(1)} %add_convert_fusion.2), channel_id=1, source_target_pairs={{0,1},{3,2},{4,5},{7,6},{8,9},{11,10},{12,13},{15,14},{16,17},{19,... | collective-permute-start | bytes 589832 | tf_op jit(solution)/shard_map/ppermute | solution.py:340
  92.9 13.9 %all-to-all-start = ((bf16[16,12,384]{2,1,0:T(8,128)(2,1)}), bf16[16,12,384]{2,1,0:T(8,128)(2,1)S(1)}, u32[]{:S(2)}, u32[]{:S(2)}) async-start(bf16[16,12,384]{2,1,0:T(8,128)(2,1)} %reshape.13), calls=%async_computation | async-start | bytes 393216 | tf_op jit(solution)/shard_map/all_to_all | solution.py:308
  100.8 10.9 %collective-permute-start.13 = (bf16[128,768]{1,0:T(8,128)(2,1)}, bf16[128,768]{1,0:T(8,128)(2,1)}, u32[]{:S(2)}, u32[]{:S(2)}) collective-permute-start(bf16[128,768]{1,0:T(8,128)(2,1)} %add_convert_fusion.1), channel_id=1, source_target_pairs={{1,2},{2,1},{5,6},{6,5},{9,10},{10,9},{13,14},{14,13},{17,18},{18,... | collective-permute-start | bytes 589832 | tf_op jit(solution)/shard_map/ppermute | solution.py:340
  103.1 23.1 %collective-permute-start.10 = (bf16[128,768]{1,0:T(8,128)(2,1)S(1)}, bf16[128,768]{1,0:T(8,128)(2,1)S(1)}, u32[]{:S(2)}, u32[]{:S(2)}) collective-permute-start(bf16[128,768]{1,0:T(8,128)(2,1)S(1)} %add_convert_fusion.3), channel_id=1, source_target_pairs={{0,1},{1,0},{2,3},{3,2},{4,5},{5,4},{6,7},{7,6},{8,9},{9,8},{10,11... | collective-permute-start | bytes 589832 | tf_op jit(solution)/shard_map/ppermute | solution.py:340
  106.8 8.9 %collective-permute-start.19 = (bf16[12,384]{1,0:T(8,128)(2,1)S(1)}, bf16[12,384]{1,0:T(8,128)(2,1)S(1)}, u32[]{:S(2)}, u32[]{:S(2)}) collective-permute-start(bf16[12,384]{1,0:T(8,128)(2,1)S(1)} %reduce_sum.12), channel_id=1, source_target_pairs={{0,128},{64,192},{128,0},{192,64},{1,129},{65,193},{129,1},{193,65... | collective-permute-start | bytes 27656 | tf_op jit(solution)/shard_map/ppermute | solution.py:310
  112.7 13.5 %collective-permute-start.14 = (bf16[64,768]{1,0:T(8,128)(2,1)S(1)}, bf16[64,768]{1,0:T(8,128)(2,1)S(1)}, u32[]{:S(2)}, u32[]{:S(2)}) collective-permute-start(bf16[64,768]{1,0:T(8,128)(2,1)S(1)} %get-tuple-element.40), channel_id=1, source_target_pairs={{0,1},{1,0},{2,3},{3,2},{4,5},{5,4},{6,7},{7,6},{8,9},{9,8},{10,11... | collective-permute-start | bytes 294920 | tf_op jit(solution)/shard_map/ppermute | solution.py:340
  115.8 14.2 %collective-permute-start.20 = (bf16[12,384]{1,0:T(8,128)(2,1)S(1)}, bf16[12,384]{1,0:T(8,128)(2,1)S(1)}, u32[]{:S(2)}, u32[]{:S(2)}) collective-permute-start(bf16[12,384]{1,0:T(8,128)(2,1)S(1)} %multiply_convert_fusion), channel_id=1, source_target_pairs={{0,64},{64,0},{128,192},{192,128},{1,65},{65,1},{129,193},{193,129... | collective-permute-start | bytes 27656 | tf_op jit(solution)/shard_map/ppermute | solution.py:312
  (34 other events, 303.6 us)

commit v2 on v0

v2 whole, which is shorter than its diff:
```python
import functools
import math

import jax
import jax.numpy as jnp
from jax import lax
from jax.experimental import pallas as pl
from jax.experimental.pallas import tpu as pltpu
from jax.sharding import PartitionSpec as P

HEADS = 12
HEAD_DIM = 64
LEVELS = 3
PAIR = 2 * HEAD_DIM
VMEM_LIMIT = 60 * 1024 * 1024
LOG2E = 1.0 / math.log(2.0)
GROUPS = ((0, HEADS // 2),)
PICK_PAIRS = 3
SPREAD_PAIRS = 3
CORE_RATE = 10**9
RUN = 4
F32 = jnp.float32
BF16 = jnp.bfloat16


def lane_masks(row_count):
    lane = lax.broadcasted_iota(jnp.int32, (row_count, PAIR), 1)
    return lane < HEAD_DIM, lane >= HEAD_DIM


def selection(offsets_ref, head, rows_dev, transposed):
    picked_count = rows_dev // 2 + rows_dev // 4 + rows_dev // 8
    shape = (rows_dev, picked_count) if transposed else (picked_count, rows_dev)
    slot = lax.broadcasted_iota(jnp.int32, shape, 1 if transposed else 0)
    row = lax.broadcasted_iota(jnp.int32, shape, 0 if transposed else 1)
    first, second = rows_dev // 2, rows_dev // 2 + rows_dev // 4
    target = jnp.where(
        slot < first,
        2 * slot + offsets_ref[0, head],
        jnp.where(
            slot < second,
            4 * (slot - first) + offsets_ref[1, head],
            8 * (slot - second) + offsets_ref[2, head],
        ),
    )
    return (row == target).astype(F32).astype(BF16)


def lanes(pair):
    return slice(pair * PAIR, (pair + 1) * PAIR)


def pick_kernel(offsets_ref, key_ref, value_ref, far_ref, near_ref, mid_ref):
    rows_dev = key_ref.shape[1]
    n1, n2, n3 = rows_dev // 2, rows_dev // 4, rows_dev // 8
    for pair in range(PICK_PAIRS):
        head = 2 * (PICK_PAIRS * pl.program_id(0) + pair)
        at = lanes(pair)
        both = jnp.concatenate([key_ref[0, :, at], value_ref[0, :, at]], axis=1)
        rows = [
            jnp.dot(selection(offsets_ref, head + side, rows_dev, False), both, preferred_element_type=F32)
            for side in range(2)
        ]
        low, _ = lane_masks(rows[0].shape[0])
        key_rows = jnp.where(low, rows[0][:, :PAIR], rows[1][:, :PAIR]).astype(BF16)
        value_rows = jnp.where(low, rows[0][:, PAIR:], rows[1][:, PAIR:]).astype(BF16)
        near_ref[:n1, at] = key_rows[:n1]
        near_ref[n1 : 2 * n1, at] = value_rows[:n1]
        near_ref[2 * n1 : 2 * n1 + n2, at] = key_rows[n1 : n1 + n2]
        near_ref[2 * n1 + n2 :, at] = value_rows[n1 : n1 + n2]
        mid_ref[:n2, at] = key_rows[n1 : n1 + n2]
        mid_ref[n2:, at] = value_rows[n1 : n1 + n2]
        far_ref[:n3, at] = key_rows[n1 + n2 :]
        far_ref[n3:, at] = value_rows[n1 + n2 :]


def pick(offsets, keys, values):
    rows_dev, feature = keys.shape[1:]
    width = PICK_PAIRS * PAIR
    whole = pl.BlockSpec((1, rows_dev, width), lambda i: (0, 0, i))
    rows = (rows_dev // 4, 3 * rows_dev // 2, rows_dev // 2)
    return pl.pallas_call(
        pick_kernel,
        grid=(feature // width,),
        in_specs=[pl.BlockSpec(memory_space=pltpu.SMEM), whole, whole],
        out_specs=[pl.BlockSpec((count, width), lambda i: (0, i)) for count in rows],
        out_shape=[jax.ShapeDtypeStruct((count, feature), BF16) for count in rows],
        compiler_params=pltpu.CompilerParams(vmem_limit_bytes=VMEM_LIMIT),
        cost_estimate=pl.CostEstimate(flops=2 * CORE_RATE, bytes_accessed=2 * 10**6, transcendentals=0),
        name="pick_rows",
    )(offsets, keys, values)


def sides(block):
    return [jnp.where(mask, block, jnp.zeros_like(block)) for mask in lane_masks(block.shape[0])]


def head_rows(side):
    return slice(side * HEAD_DIM, (side + 1) * HEAD_DIM)


NT = (((1,), (1,)), ((), ()))


def fill_sets(key_set_ref, value_set_ref, key_ref, value_ref, near_ref, gathered_refs):
    near_pair_ref, mid2_ref, mid3_ref, far0_ref, far1_ref, far2_ref, far3_ref, cross_ref = gathered_refs
    rows_dev = key_ref.shape[1]
    n1, n2, n3 = rows_dev // 2, rows_dev // 4, rows_dev // 8
    key_set_ref[:rows_dev] = key_ref[0]
    value_set_ref[:rows_dev] = value_ref[0]
    sources = [(near_ref, 0, n1), (near_pair_ref, 0, n1)]
    sources += [(near_ref, 2 * n1, n2), (near_pair_ref, 2 * n1, n2), (mid2_ref, 0, n2), (mid3_ref, 0, n2)]
    sources += [(ref, 0, n3) for ref in (far0_ref, far1_ref, far2_ref, far3_ref)]
    sources += [(cross_ref, 2 * n3 * idx, n3) for idx in range(4)]
    at = rows_dev
    for ref, base, count in sources:
        key_set_ref[at : at + count] = ref[base : base + count]
        value_set_ref[at : at + count] = ref[base + count : base + 2 * count]
        at += count


def weights_of(query_sides, keys):
    scores = [lax.dot_general(keys, side, NT, preferred_element_type=F32) for side in query_sides]
    raw, inverse = [], []
    for block in scores:
        row_max = jnp.max(block, axis=0, keepdims=True)
        weights = jnp.exp2(block * LOG2E - row_max * LOG2E)
        inverse.append(1.0 / jnp.sum(weights, axis=0, keepdims=True))
        raw.append(weights.astype(BF16))
    return raw, inverse


def attended_of(values_t, raw, inverse):
    return [
        (jnp.dot(values_t[head_rows(side)], raw[side], preferred_element_type=F32) * inverse[side]).astype(BF16)
        for side in range(2)
    ]


def backward_of(query_sides, grad, attended_t, keys_t, values, raw, raw_pair, inverse, query_grad_ref, out_refs, sums):
    local_ref, own1_ref, own2_ref, far_ref, back_ref, send1_ref, send2_ref, send3_ref = out_refs
    key_sum, value_sum = sums
    rows_dev = grad.shape[0]
    n1, n2, n3 = rows_dev // 2, rows_dev // 4, rows_dev // 8
    grad_t = grad.T.astype(F32)
    normed_t = jnp.concatenate([grad_t[head_rows(side)] * inverse[side] for side in range(2)], axis=0)
    grad_sides = sides(normed_t.astype(BF16).T)
    score_grads = []
    for side in range(2):
        prob_grad = lax.dot_general(values, grad_sides[side], NT, preferred_element_type=F32)
        delta = inverse[side] * jnp.sum(
            grad_t[head_rows(side)] * attended_t[side].astype(F32), axis=0, keepdims=True
        )
        score_grads.append((raw[side].astype(F32) * (prob_grad - delta)).astype(BF16))
    query_t = jnp.concatenate(
        [jnp.dot(keys_t[head_rows(side)], score_grads[side], preferred_element_type=F32) for side in range(2)],
        axis=0,
    )
    query_grad_ref[0] = (query_t * (1.0 / math.sqrt(HEAD_DIM))).astype(BF16).T
    key_sum[...] = jnp.dot(
        jnp.concatenate(score_grads, axis=1), jnp.concatenate(query_sides, axis=0), preferred_element_type=F32
    )
    value_sum[...] = jnp.dot(raw_pair, jnp.concatenate(grad_sides, axis=0), preferred_element_type=F32)
    targets = [(local_ref, 0, rows_dev), (own1_ref, 0, n1), (send1_ref, 0, n1)]
    targets += [(own2_ref, 0, n2), (send1_ref, 2 * n1, n2), (send2_ref, 0, n2), (send3_ref, 0, n2)]
    targets += [(far_ref, 2 * n3 * idx, n3) for idx in range(4)]
    targets += [(back_ref, 2 * n3 * idx, n3) for idx in range(4)]
    at = 0
    for ref, base, count in targets:
        ref[base : base + count] = key_sum[at : at + count].astype(ref.dtype)
        ref[base + count : base + 2 * count] = value_sum[at : at + count].astype(ref.dtype)
        at += count


def scaled_sides(query_ref):
    return sides((query_ref[0].astype(F32) * (1.0 / math.sqrt(HEAD_DIM))).astype(BF16))


def both_kernel(query_ref, key_ref, value_ref, near_ref, *refs):
    gathered, grad_ref, attended_ref, query_grad_ref = refs[:8], refs[8], refs[9], refs[10]
    outs, (key_set, value_set, key_sum, value_sum) = refs[11:-4], refs[-4:]
    fill_sets(key_set, value_set, key_ref, value_ref, near_ref, gathered)
    query_sides = scaled_sides(query_ref)
    raw, inverse = weights_of(query_sides, key_set[...])
    attended_t = attended_of(value_set[...].T, raw, inverse)
    attended_ref[...] = jnp.concatenate(attended_t, axis=0).T
    backward_of(
        query_sides, grad_ref[...], attended_t, key_set[...].T, value_set[...], raw,
        jnp.concatenate(raw, axis=1), inverse, query_grad_ref, outs, (key_sum, value_sum),
    )


class Layout:
    def __init__(self, group, rows_dev, feature):
        self.first, self.count = group
        self.rows_dev, self.feature, self.width = rows_dev, feature, group[1] * PAIR
        self.set_rows = 4 * rows_dev
        self.given = pl.BlockSpec((1, rows_dev, PAIR), lambda i: (0, 0, group[0] + i))
        self.sums = [pltpu.VMEM((self.set_rows, PAIR), F32)] * 2
        self.sets = [pltpu.VMEM((self.set_rows, PAIR), BF16)] * 2

    def whole(self, rows):
        return pl.BlockSpec((rows, PAIR), lambda i: (0, self.first + i))

    def part(self, rows):
        return pl.BlockSpec((rows, PAIR), lambda i: (0, i))

    def of(self, block):
        return self.part(block.shape[0]) if block.shape[1] == self.width else self.whole(block.shape[0])

    def gradient_outs(self):
        rows, shape = self.rows_dev, jax.ShapeDtypeStruct
        wide = [(2 * rows, F32), (rows, F32), (rows // 2, F32), (rows, F32)]
        narrow = [rows, 3 * rows // 2, rows // 2, rows // 2]
        specs = [self.given] + [self.whole(count) for count, _ in wide] + [self.part(count) for count in narrow]
        shapes = [shape((1, rows, self.feature), BF16)]
        shapes += [shape((count, self.feature), kind) for count, kind in wide]
        shapes += [shape((count, self.width), BF16) for count in narrow]
        return specs, shapes

    def call(self, kernel, name, operands, in_specs, out_specs, out_shapes, scratch, micros, before=()):
        return pl.pallas_call(
            kernel,
            grid=(self.count,),
            in_specs=list(in_specs) + [pl.BlockSpec(memory_space=pl.ANY)] * len(before),
            out_specs=out_specs,
            out_shape=out_shapes,
            input_output_aliases={len(operands) + idx: idx for idx in range(len(before))},
            scratch_shapes=scratch,
            compiler_params=pltpu.CompilerParams(vmem_limit_bytes=VMEM_LIMIT),
            cost_estimate=pl.CostEstimate(
                flops=int(micros * self.count * CORE_RATE), bytes_accessed=10**6, transcendentals=0
            ),
            name=name,
        )(*operands, *before)


def attend_both(group, queries, keys, values, grads, near, gathered):
    rows_dev, feature = queries.shape[1:]
    lay = Layout(group, rows_dev, feature)
    specs, shapes = lay.gradient_outs()
    operands = (queries, keys, values, near) + tuple(gathered) + (grads,)
    return lay.call(
        both_kernel, "attend_both", operands, [lay.given] * 3 + [lay.of(block) for block in operands[3:]],
        [lay.whole(rows_dev)] + specs, [jax.ShapeDtypeStruct((rows_dev, feature), BF16)] + shapes,
        lay.sets + lay.sums, 2.6,
    )


def spread_kernel(groups, offsets_ref, local_ref, own1_ref, own2_ref, own3_ref, far1_ref, far2_ref, far3_ref, *refs):
    key_ref, value_ref = refs[-2:]
    rows_dev = local_ref.shape[0] // 2

    def wide(ref, at, rows=slice(None)):
        return ref[rows, at].astype(F32)

    def run(part_refs):
        pair_ref, mid2_ref, mid3_ref = part_refs
        for pair in range(SPREAD_PAIRS):
            head = 2 * (SPREAD_PAIRS * pl.program_id(0) + pair)
            at = lanes(pair)
            totals = (
                own1_ref[:, at] + wide(pair_ref, at, slice(0, rows_dev)),
                own2_ref[:, at] + wide(pair_ref, at, slice(rows_dev, None)) + wide(mid2_ref, at) + wide(mid3_ref, at),
                own3_ref[:, at] + sum(wide(ref, at, slice(0, own3_ref.shape[0])) for ref in (far1_ref, far2_ref, far3_ref)),
            )
            key_rows = jnp.concatenate([t[: t.shape[0] // 2] for t in totals], axis=0)
            value_rows = jnp.concatenate([t[t.shape[0] // 2 :] for t in totals], axis=0)
            both = jnp.concatenate([key_rows, value_rows], axis=1).astype(BF16)
            spread = [
                jnp.dot(selection(offsets_ref, head + side, rows_dev, True), both, preferred_element_type=F32)
                for side in range(2)
            ]
            low, _ = lane_masks(rows_dev)
            key_ref[0, :, at] = (
                local_ref[:rows_dev, at] + jnp.where(low, spread[0][:, :PAIR], spread[1][:, :PAIR])
            ).astype(BF16)
            value_ref[0, :, at] = (
                local_ref[rows_dev:, at] + jnp.where(low, spread[0][:, PAIR:], spread[1][:, PAIR:])
            ).astype(BF16)

    for idx, (first, count) in enumerate(groups):
        step = pl.program_id(0) * SPREAD_PAIRS

        @pl.when((step >= first) & (step < first + count))
        def _():
            run(refs[3 * idx : 3 * idx + 3])


def spread(offsets, local, owns, fars, returned):
    rows_dev, feature = local.shape[0] // 2, local.shape[1]
    width = SPREAD_PAIRS * PAIR
    out = pl.BlockSpec((1, rows_dev, width), lambda i: (0, 0, i))
    shape = jax.ShapeDtypeStruct((1, rows_dev, feature), BF16)
    specs = [pl.BlockSpec((part.shape[0], width), lambda i: (0, i)) for part in (local,) + owns + fars]
    parts = []
    for (first, count), blocks in zip(GROUPS, returned):
        start, last = first // SPREAD_PAIRS, count // SPREAD_PAIRS - 1
        for block in blocks:
            parts.append(block)
            specs.append(
                pl.BlockSpec(
                    (block.shape[0], width),
                    functools.partial(lambda start, last, i: (0, jnp.clip(i - start, 0, last)), start, last),
                )
            )
    return pl.pallas_call(
        functools.partial(spread_kernel, GROUPS),
        grid=(feature // width,),
        in_specs=[pl.BlockSpec(memory_space=pltpu.SMEM)] + specs,
        out_specs=[out, out],
        out_shape=[shape, shape],
        compiler_params=pltpu.CompilerParams(vmem_limit_bytes=VMEM_LIMIT),
        cost_estimate=pl.CostEstimate(flops=3 * CORE_RATE, bytes_accessed=4 * 10**6, transcendentals=0),
        name="spread_rows",
    )(offsets, local, *owns, *fars, *parts)


def swap(block, bits):
    return lax.ppermute(block, "seq", [(i, i ^ bits) for i in range(lax.axis_size("seq"))])


def slide_swap(block, bits):
    return lax.ppermute(block, "dp", [(i, i ^ bits) for i in range(lax.axis_size("dp"))])


def after(block, others):
    tied = lax.optimization_barrier((block,) + tuple(others))
    return tied[0], list(tied[1:])


def plane_share(cotangent, attended):
    core = lax.axis_index("dp") % 2
    half = attended.shape[1] // 2

    def columns(which):
        block = lax.dynamic_slice_in_dim(attended, which * half, half, 1)
        return lax.dot_general(cotangent, block, (((0,), (0,)), ((), ())), preferred_element_type=F32)

    sent = slide_swap(columns(1 - core).astype(BF16), 1)
    total = (columns(core) + sent.astype(F32)).astype(BF16)
    planes = lax.axis_size("seq") // RUN
    groups = [[RUN * place + z for place in range(planes)] for z in range(RUN)]
    shares = lax.all_to_all(total, "seq", 0, 0, axis_index_groups=groups, tiled=True)
    return jnp.sum(shares.reshape(planes, -1, half).astype(F32), axis=0).astype(BF16)


def slides_total(share, norm_factor):
    parts = [slide_swap(share, bits) for bits in (1, 2, 3)]
    mine = ((share.astype(F32) + parts[1].astype(F32)) * norm_factor).astype(BF16)
    other = ((parts[0].astype(F32) + parts[2].astype(F32)) * norm_factor).astype(BF16)
    return jnp.where(
        lax.axis_index("dp") % 2 == 0, jnp.concatenate([mine, other], 1), jnp.concatenate([other, mine], 1)
    )


def shards(queries, keys, values, out_weight, out_cotangent, offsets):
    rows_dev, feature = queries.shape[1:]
    cotangent = out_cotangent[0]
    n3 = rows_dev // 4
    far, near, mid = pick(offsets, keys, values)
    fars = [far] + [swap(far, bits) for bits in (1, 2, 3)]
    cross = swap(jnp.concatenate(fars, axis=0), 4)
    grads = jnp.dot(cotangent, out_weight, preferred_element_type=F32).astype(BF16)
    gathered = [swap(near, 1), swap(mid, 2), swap(mid, 3)] + fars + [cross]
    results = attend_both(GROUPS[0], queries, keys, values, grads, near, gathered)
    attended, query_grad, local, own1, own2, far_grad, back = results[:7]
    cross_back = swap(back, 4)
    back1, back2, back3 = [swap(block, bits) for bits, block in zip((1, 2, 3), results[7:])]
    share = plane_share(cotangent, attended)
    share, (back2, back3) = after(share, [back2, back3])
    far_grad = far_grad + cross_back.astype(F32)
    far_parts = [far_grad[bits * n3 : (bits + 1) * n3] for bits in range(4)]
    rows, half = share.shape[0] // RUN, share.shape[1]
    place = lax.axis_index("seq") % RUN
    share_parts = [lax.dynamic_slice_in_dim(share, (place ^ bits) * rows, rows, 0) for bits in range(4)]
    total = share_parts[0].astype(F32)
    far_back = []
    for bits in (1, 2, 3):
        padded = jnp.pad(share_parts[bits], ((0, -rows % 16), (0, feature - half)))
        arrived = swap(jnp.concatenate([far_parts[bits].astype(BF16), padded], axis=0), bits)
        far_back.append(arrived)
        total = total + arrived[n3 : n3 + rows, :half].astype(F32)
    tiles = lax.axis_size("dp") * lax.axis_size("seq") * rows_dev
    total, (back1,) = after(total.astype(BF16), [back1])
    weight_grad = slides_total(total, 1.0 / math.sqrt(tiles))
    key_grad, value_grad = spread(
        offsets, local, (own1, own2, far_parts[0]), tuple(far_back), [[back1, back2, back3]]
    )
    mixed = lax.dot_general(
        attended, out_weight, (((1,), (1,)), ((), ())), preferred_element_type=F32
    ).astype(BF16)
    return mixed[None], query_grad, key_grad, value_grad, weight_grad


def solution(mesh):
    split = P("dp", "seq", None)
    return jax.shard_map(
        shards,
        mesh=mesh,
        in_specs=(split, split, split, P(), split, P()),
        out_specs=(split, split, split, split, P("seq", None)),
        check_vma=False,
    )
```

time: 649 us -> 115 us (0.18)
  blocking collectives: 439 us -> 0 us
  local copies, waits for them, and re-layouts: 99.5 us -> 3.41 us
  other arithmetic: 45 us -> 2.94 us
  starting transfers between devices: 12.6 us -> 39.7 us
  matrix products: 26.9 us -> 4.19 us
  Pallas kernels: 0 us -> 22.4 us
  waiting for transfers between devices: 21 us -> 41 us
    unnamed x1 -> x0, blocking collectives: 359 us -> none
    psum x1 -> x0, blocking collectives: 80.5 us -> none  [shards(): summed = lax.psum(shares.astype(jnp.bfloat16), 'dp').astype(jnp.float32)]
    dynamic_slice x24 -> x1, local copies, waits for them, and re-layouts: 28.8 us -> 0.03 us  [shards(): lax.dynamic_slice_in_dim(share, (place ^ bits) * rows, rows, 0)]
    mul x18 -> x0, local copies, waits for them, and re-layouts: 25 us -> none  [spread_rows(): source.reshape(row_count, 1, HEADS, feature // HEADS)]
    pallas_call x0 -> x3, Pallas kernels: none -> 22.4 us  [the longest x1 16.4 us: call(): pl.pallas_call(kernel, grid=(self.count,), in_specs=list(in_specs) + [pl....]
    ppermute x12 -> x18, starting transfers between devices: 12.6 us -> 33 us  [the longest x14 24.6 us: swap(): lax.ppermute(block, 'seq', [(i, i ^ bits) for i in range(lax.axis_size('s...]
    ppermute x12 -> x18, waiting for transfers between devices: 21 us -> 35.5 us  [the longest x14 32.5 us: swap(): lax.ppermute(block, 'seq', [(i, i ^ bits) for i in range(lax.axis_size('s...]
    convert_element_type x18 -> x3, other arithmetic: 11.9 us -> 0.03 us  [the longest x1 0.02 us: shards(): total, (back1,) = after(total.astype(BF16), [back1])]
  transfers between devices with their start and end apart: 12 -> 19, of which waited for: 3 -> 10; matrix products, arithmetic and copies ran while one was open for 10% -> 6% of each run, Pallas kernels for 0% -> 3%
where the time goes in v2:
time: 115 us; the launch traced here: 114 us
  waiting for transfers between devices  41 us (36%)
  starting transfers between devices  39.7 us (35%)
  Pallas kernels  22.4 us (19%)
  matrix products  4.19 us (4%)
  local copies, waits for them, and re-layouts  3.41 us (3%)
  other arithmetic  2.94 us (3%)
    ppermute x14, waiting for transfers between devices, swap(): lax.ppermute(block, 'seq', [(i, i ^ bits) for i in range(lax.axis_size('s...  32.5 us
    ppermute x14, starting transfers between devices, swap(): lax.ppermute(block, 'seq', [(i, i ^ bits) for i in range(lax.axis_size('s...  24.6 us
    pallas_call x1, Pallas kernels, call(): pl.pallas_call(kernel, grid=(self.count,), in_specs=list(in_specs) + [pl....  16.4 us
    ppermute x4, starting transfers between devices, slide_swap(): lax.ppermute(block, 'dp', [(i, i ^ bits) for i in range(lax.axis_size('dp...  8.42 us
    all_to_all x1, starting transfers between devices, plane_share(): lax.all_to_all(total, 'seq', 0, 0, axis_index_groups=groups, tiled=True)  6.75 us
    all_to_all x1, waiting for transfers between devices, plane_share(): lax.all_to_all(total, 'seq', 0, 0, axis_index_groups=groups, tiled=True)  5.42 us
    pallas_call x1, Pallas kernels, spread(): pl.pallas_call(functools.partial(spread_kernel, GROUPS), grid=(feature //...  3.4 us
    ppermute x4, waiting for transfers between devices, slide_swap(): lax.ppermute(block, 'dp', [(i, i ^ bits) for i in range(lax.axis_size('dp...  3.04 us
  transfers between devices with their start and end apart: 19, of which 10 were waited for; matrix products, arithmetic and copies ran while one was open for 6% of the time, Pallas kernels for 3%

profile of v2, /device:TPU:1, one launch (start us, length us, event | category | flops | bytes accessed | tf_op | source)
XLA Modules:
  0.0 114.5 jit_solution(15603436567449331391)
XLA Ops:
  0.7 2.6 %pick_rows.1 = (bf16[64,768]{1,0:T(8,128)(2,1)}, bf16[384,768]{1,0:T(8,128)(2,1)}, bf16[128,768]{1,0:T(8,128)(2,1)}) custom-call(s32[3,12]{1,0:T(4,128)} %offsets_ref.3, bf16[1,256,768]{2,1,0:T(8,128)(2,1)} %key_ref.3, bf16[1,256,768]{2,1,0:T(8,128)(2,1)} %value_ref.3), custom_call_target="tpu_custom_call" | custom-call | flops 2000000000 | bytes 2000000 | tf_op jit(solution)/shard_map/pick_rows/pallas_call | solution.py:82
  3.3 2.5 %collective-permute-start.3 = (bf16[64,768]{1,0:T(8,128)(2,1)}, bf16[64,768]{1,0:T(8,128)(2,1)S(1)}, u32[]{:S(2)}, u32[]{:S(2)}) collective-permute-start(bf16[64,768]{1,0:T(8,128)(2,1)} %get-tuple-element.27.refs_3_), channel_id=1, source_target_pairs={{0,1},{1,0},{2,3},{3,2},{4,5},{5,4},{6,7},{7,6},{8,9},{9,8},{10,11... | collective-permute-start | bytes 294920 | tf_op jit(solution)/shard_map/ppermute | solution.py:320
  5.8 3.0 %collective-permute-start.4 = (bf16[64,768]{1,0:T(8,128)(2,1)}, bf16[64,768]{1,0:T(8,128)(2,1)S(1)}, u32[]{:S(2)}, u32[]{:S(2)}) collective-permute-start(bf16[64,768]{1,0:T(8,128)(2,1)} %get-tuple-element.27.refs_3_), channel_id=1, source_target_pairs={{0,2},{1,3},{2,0},{3,1},{4,6},{5,7},{6,4},{7,5},{8,10},{9,11},{10,... | collective-permute-start | bytes 294920 | tf_op jit(solution)/shard_map/ppermute | solution.py:320
  9.1 2.6 %collective-permute-done.4.refs_5_ = bf16[64,768]{1,0:T(8,128)(2,1)S(1)} collective-permute-done((bf16[64,768]{1,0:T(8,128)(2,1)}, bf16[64,768]{1,0:T(8,128)(2,1)S(1)}, u32[]{:S(2)}, u32[]{:S(2)}) %collective-permute-start.4) | collective-permute-done | bytes 98336 | tf_op jit(solution)/shard_map/ppermute | solution.py:320
  11.6 3.5 %collective-permute-done.5.refs_6_ = bf16[64,768]{1,0:T(8,128)(2,1)S(1)} collective-permute-done((bf16[64,768]{1,0:T(8,128)(2,1)}, bf16[64,768]{1,0:T(8,128)(2,1)S(1)}, u32[]{:S(2)}, u32[]{:S(2)}) %collective-permute-start.5) | collective-permute-done | bytes 98336 | tf_op jit(solution)/shard_map/ppermute | solution.py:320
  16.1 1.5 %collective-permute-start.6 = (bf16[256,768]{1,0:T(8,128)(2,1)S(1)}, bf16[256,768]{1,0:T(8,128)(2,1)S(1)}, u32[]{:S(2)}, u32[]{:S(2)}) collective-permute-start(bf16[256,768]{1,0:T(8,128)(2,1)S(1)} %pad_maximum_fusion), channel_id=1, source_target_pairs={{0,4},{1,5},{2,6},{3,7},{4,0},{5,1},{6,2},{7,3},{8,12},{9,13},{10,... | collective-permute-start | bytes 1179656 | tf_op jit(solution)/shard_map/ppermute | solution.py:320
  17.6 3.5 %collective-permute-start.1 = (bf16[128,768]{1,0:T(8,128)(2,1)}, bf16[128,768]{1,0:T(8,128)(2,1)S(1)}, u32[]{:S(2)}, u32[]{:S(2)}) collective-permute-start(bf16[128,768]{1,0:T(8,128)(2,1)} %get-tuple-element.26), channel_id=1, source_target_pairs={{0,2},{1,3},{2,0},{3,1},{4,6},{5,7},{6,4},{7,5},{8,10},{9,11},{10,... | collective-permute-start | bytes 589832 | tf_op jit(solution)/shard_map/ppermute | solution.py:320
  23.6 5.7 %collective-permute-done.1.refs_1_ = bf16[128,768]{1,0:T(8,128)(2,1)S(1)} collective-permute-done((bf16[128,768]{1,0:T(8,128)(2,1)}, bf16[128,768]{1,0:T(8,128)(2,1)S(1)}, u32[]{:S(2)}, u32[]{:S(2)}) %collective-permute-start.1) | collective-permute-done | bytes 196640 | tf_op jit(solution)/shard_map/ppermute | solution.py:320
  29.3 7.2 %collective-permute-done.2.refs_2_ = bf16[128,768]{1,0:T(8,128)(2,1)} collective-permute-done((bf16[128,768]{1,0:T(8,128)(2,1)}, bf16[128,768]{1,0:T(8,128)(2,1)}, u32[]{:S(2)}, u32[]{:S(2)}) %collective-permute-start.2) | collective-permute-done | bytes 196640 | tf_op jit(solution)/shard_map/ppermute | solution.py:320
  38.0 16.4 %attend_both.1 = (bf16[256,768]{1,0:T(8,128)(2,1)}, bf16[1,256,768]{2,1,0:T(8,128)(2,1)}, f32[512,768]{1,0:T(8,128)}, f32[256,768]{1,0:T(8,128)}, f32[128,768]{1...) custom-call(bf16[1,256,768]{2,1,0:T(8,128)(2,1)} %query_ref.1, ...), custom_call_target="tpu_custom_call" | custom-call | flops 15600000000 | bytes 1000000 | tf_op jit(solution)/shard_map/attend_both/pallas_call | solution.py:222
  54.4 1.3 %fusion.2 = bf16[768,384]{0,1:T(8,128)(2,1)S(1)} fusion(bf16[1,256,768]{2,1,0:T(8,128)(2,1)S(1)} %copy-done.1, bf16[256,768]{1,0:T(8,128)(2,1)} %get-tuple-element.28, s32[]{:T(128)S(6)} %select_n.41), kind=kOutput, calls=%fused_computation.4 | convolution fusion | flops 151289856 | bytes 1179652 | tf_op jit(solution)/shard_map/dot_general | solution.py:338
  55.8 1.6 %collective-permute-start.8 = (bf16[768,384]{0,1:T(8,128)(2,1)S(1)}, bf16[768,384]{0,1:T(8,128)(2,1)S(1)}, u32[]{:S(2)}, u32[]{:S(2)}) collective-permute-start(bf16[768,384]{0,1:T(8,128)(2,1)S(1)} %fusion.2), channel_id=1, source_target_pairs={{0,64},{64,0},{128,192},{192,128},{1,65},{65,1},{129,193},{193,129... | collective-permute-start | bytes 1769480 | tf_op jit(solution)/shard_map/ppermute | solution.py:324
  60.4 6.8 %all-to-all-start = ((bf16[16,48,384]{2,1,0:T(8,128)(2,1)}), bf16[16,48,384]{2,1,0:T(8,128)(2,1)S(1)}, u32[]{:S(2)}, u32[]{:S(2)}) async-start(bf16[16,48,384]{2,1,0:T(8,128)(2,1)} %bitcast.4), calls=%async_computation | async-start | bytes 1179648 | tf_op jit(solution)/shard_map/all_to_all | solution.py:344
  67.2 2.2 %collective-permute-start.9 = (bf16[128,768]{1,0:T(8,128)(2,1)}, bf16[128,768]{1,0:T(8,128)(2,1)}, u32[]{:S(2)}, u32[]{:S(2)}) collective-permute-start(bf16[128,768]{1,0:T(8,128)(2,1)} %get-tuple-element.35), channel_id=1, source_target_pairs={{0,2},{1,3},{2,0},{3,1},{4,6},{5,7},{6,4},{7,5},{8,10},{9,11},{10,... | collective-permute-start | bytes 589832 | tf_op jit(solution)/shard_map/ppermute | solution.py:320
  69.4 2.0 %collective-permute-start.10 = (bf16[128,768]{1,0:T(8,128)(2,1)}, bf16[128,768]{1,0:T(8,128)(2,1)}, u32[]{:S(2)}, u32[]{:S(2)}) collective-permute-start(bf16[128,768]{1,0:T(8,128)(2,1)} %get-tuple-element.36), channel_id=1, source_target_pairs={{0,3},{1,2},{2,1},{3,0},{4,7},{5,6},{6,5},{7,4},{8,11},{9,10},{10,... | collective-permute-start | bytes 589832 | tf_op jit(solution)/shard_map/ppermute | solution.py:320
  72.6 5.4 %all-to-all-done = bf16[16,48,384]{2,1,0:T(8,128)(2,1)S(1)} async-done(((bf16[16,48,384]{2,1,0:T(8,128)(2,1)}), bf16[16,48,384]{2,1,0:T(8,128)(2,1)S(1)}, u32[]{:S(2)}, u32[]{:S(2)}) %all-to-all-start) | async-done | bytes 589856 | tf_op jit(solution)/shard_map/all_to_all | solution.py:344
  78.2 4.7 %collective-permute-done.9.refs_1_ = bf16[128,768]{1,0:T(8,128)(2,1)} collective-permute-done((bf16[128,768]{1,0:T(8,128)(2,1)}, bf16[128,768]{1,0:T(8,128)(2,1)}, u32[]{:S(2)}, u32[]{:S(2)}) %collective-permute-start.9) | collective-permute-done | bytes 196640 | tf_op jit(solution)/shard_map/ppermute | solution.py:320
  82.9 4.6 %collective-permute-start.11 = (bf16[80,768]{1,0:T(8,128)(2,1)S(1)}, bf16[80,768]{1,0:T(8,128)(2,1)S(1)}, u32[]{:S(2)}, u32[]{:S(2)}) collective-permute-start(bf16[80,768]{1,0:T(8,128)(2,1)S(1)} %fusion.12), channel_id=1, source_target_pairs={{0,1},{1,0},{2,3},{3,2},{4,5},{5,4},{6,7},{7,6},{8,9},{9,8},{10,11... | collective-permute-start | bytes 368648 | tf_op jit(solution)/shard_map/ppermute | solution.py:320
  88.4 1.5 %collective-permute-start.13 = (bf16[80,768]{1,0:T(8,128)(2,1)S(1)}, bf16[80,768]{1,0:T(8,128)(2,1)S(1)}, u32[]{:S(2)}, u32[]{:S(2)}) collective-permute-start(bf16[80,768]{1,0:T(8,128)(2,1)S(1)} %fusion.14), channel_id=1, source_target_pairs={{0,3},{1,2},{2,1},{3,0},{4,7},{5,6},{6,5},{7,4},{8,11},{9,10},{10,... | collective-permute-start | bytes 368648 | tf_op jit(solution)/shard_map/ppermute | solution.py:320
  91.9 5.3 %collective-permute-done.11.far1_ref = bf16[80,768]{1,0:T(8,128)(2,1)S(1)} collective-permute-done((bf16[80,768]{1,0:T(8,128)(2,1)S(1)}, bf16[80,768]{1,0:T(8,128)(2,1)S(1)}, u32[]{:S(2)}, u32[]{:S(2)}) %collective-permute-start.11) | collective-permute-done | bytes 122912 | tf_op jit(solution)/shard_map/ppermute | solution.py:320
  97.2 3.6 %collective-permute-done.13.far3_ref = bf16[80,768]{1,0:T(8,128)(2,1)S(1)} collective-permute-done((bf16[80,768]{1,0:T(8,128)(2,1)S(1)}, bf16[80,768]{1,0:T(8,128)(2,1)S(1)}, u32[]{:S(2)}, u32[]{:S(2)}) %collective-permute-start.13) | collective-permute-done | bytes 122912 | tf_op jit(solution)/shard_map/ppermute | solution.py:320
  100.9 6.5 %collective-permute-start.17 = (bf16[12,384]{1,0:T(8,128)(2,1)S(1)}, bf16[12,384]{1,0:T(8,128)(2,1)S(1)}, u32[]{:S(2)}, u32[]{:S(2)}) collective-permute-start(bf16[12,384]{1,0:T(8,128)(2,1)S(1)} %add_convert_fusion), channel_id=1, source_target_pairs={{0,192},{64,128},{128,64},{192,0},{1,193},{65,129},{129,65},{193,1... | collective-permute-start | bytes 27656 | tf_op jit(solution)/shard_map/ppermute | solution.py:324
  107.7 3.4 %spread_rows.1 = (bf16[1,256,768]{2,1,0:T(8,128)(2,1)}, bf16[1,256,768]{2,1,0:T(8,128)(2,1)}) custom-call(s32[3,12]{1,0:T(4,128)} %offsets_ref.3, f32[512,768]{1,0:T(8,128)} %get-tuple-element.30.local_ref, f32[256,768]{1,0:T(8,128)} %get-tuple-element.31.own1_ref, f32[128,768]{1,0:T(8,128)} %get-tuple-element.32.own2_ref, f32[64,768]{1,0:T(8,128)} %slice.31.own3_ref, ...), custom_call_target="tpu_custom_call" | custom-call | flops 3000000000 | bytes 4000000 | tf_op jit(solution)/shard_map/spread_rows/pallas_call | solution.py:307
  111.1 2.7 %collective-permute-done.15 = bf16[12,384]{1,0:T(8,128)(2,1)S(1)} collective-permute-done((bf16[12,384]{1,0:T(8,128)(2,1)S(1)}, bf16[12,384]{1,0:T(8,128)(2,1)S(1)}, u32[]{:S(2)}, u32[]{:S(2)}) %collective-permute-start.15) | collective-permute-done | bytes 9248 | tf_op jit(solution)/shard_map/ppermute | solution.py:324
  (59 shorter events, 13.7 us)
Async XLA Ops:
  0.6 21.8 %copy-start = (bf16[768,768]{1,0:T(8,128)(2,1)S(1)}, bf16[768,768]{1,0:T(8,128)(2,1)}, u32[]{:S(2)}) copy-start(bf16[768,768]{1,0:T(8,128)(2,1)} %param.9) | copy-start | bytes 3538948
  0.6 21.7 %copy-start.1 = (bf16[1,256,768]{2,1,0:T(8,128)(2,1)S(1)}, bf16[1,256,768]{2,1,0:T(8,128)(2,1)}, u32[]{:S(2)}) copy-start(bf16[1,256,768]{2,1,0:T(8,128)(2,1)} %param.10) | copy-start | bytes 1179652
  3.3 5.7 %collective-permute-start.3 = (bf16[64,768]{1,0:T(8,128)(2,1)}, bf16[64,768]{1,0:T(8,128)(2,1)S(1)}, u32[]{:S(2)}, u32[]{:S(2)}) collective-permute-start(bf16[64,768]{1,0:T(8,128)(2,1)} %get-tuple-element.27.refs_3_), channel_id=1, source_target_pairs={{0,1},{1,0},{2,3},{3,2},{4,5},{5,4},{6,7},{7,6},{8,9},{9,8},{10,11... | collective-permute-start | bytes 294920 | tf_op jit(solution)/shard_map/ppermute | solution.py:320
  5.8 5.8 %collective-permute-start.4 = (bf16[64,768]{1,0:T(8,128)(2,1)}, bf16[64,768]{1,0:T(8,128)(2,1)S(1)}, u32[]{:S(2)}, u32[]{:S(2)}) collective-permute-start(bf16[64,768]{1,0:T(8,128)(2,1)} %get-tuple-element.27.refs_3_), channel_id=1, source_target_pairs={{0,2},{1,3},{2,0},{3,1},{4,6},{5,7},{6,4},{7,5},{8,10},{9,11},{10,... | collective-permute-start | bytes 294920 | tf_op jit(solution)/shard_map/ppermute | solution.py:320
  8.8 6.3 %collective-permute-start.5 = (bf16[64,768]{1,0:T(8,128)(2,1)}, bf16[64,768]{1,0:T(8,128)(2,1)S(1)}, u32[]{:S(2)}, u32[]{:S(2)}) collective-permute-start(bf16[64,768]{1,0:T(8,128)(2,1)} %get-tuple-element.27.refs_3_), channel_id=1, source_target_pairs={{0,3},{1,2},{2,1},{3,0},{4,7},{5,6},{6,5},{7,4},{8,11},{9,10},{10,... | collective-permute-start | bytes 294920 | tf_op jit(solution)/shard_map/ppermute | solution.py:320
  8.8 27.7 %collective-permute-start = (bf16[384,768]{1,0:T(8,128)(2,1)}, bf16[384,768]{1,0:T(8,128)(2,1)S(1)}, u32[]{:S(2)}, u32[]{:S(2)}) collective-permute-start(bf16[384,768]{1,0:T(8,128)(2,1)} %get-tuple-element.25.near_ref), channel_id=1, source_target_pairs={{0,1},{1,0},{2,3},{3,2},{4,5},{5,4},{6,7},{7,6},{8,9},{9,8},{10,11... | collective-permute-start | bytes 1769480 | tf_op jit(solution)/shard_map/ppermute | solution.py:320
  9.1 14.6 %copy-start.3 = (bf16[64,768]{1,0:T(8,128)(2,1)}, bf16[64,768]{1,0:T(8,128)(2,1)S(1)}, u32[]{:S(2)}) copy-start(bf16[64,768]{1,0:T(8,128)(2,1)S(1)} %collective-permute-done.3.refs_4_) | copy-start | bytes 294916
  11.6 12.0 %copy-start.4 = (bf16[64,768]{1,0:T(8,128)(2,1)}, bf16[64,768]{1,0:T(8,128)(2,1)S(1)}, u32[]{:S(2)}) copy-start(bf16[64,768]{1,0:T(8,128)(2,1)S(1)} %collective-permute-done.4.refs_5_) | copy-start | bytes 294916
  16.1 20.4 %collective-permute-start.6 = (bf16[256,768]{1,0:T(8,128)(2,1)S(1)}, bf16[256,768]{1,0:T(8,128)(2,1)S(1)}, u32[]{:S(2)}, u32[]{:S(2)}) collective-permute-start(bf16[256,768]{1,0:T(8,128)(2,1)S(1)} %pad_maximum_fusion), channel_id=1, source_target_pairs={{0,4},{1,5},{2,6},{3,7},{4,0},{5,1},{6,2},{7,3},{8,12},{9,13},{10,... | collective-permute-start | bytes 1179656 | tf_op jit(solution)/shard_map/ppermute | solution.py:320
  17.6 11.7 %collective-permute-start.1 = (bf16[128,768]{1,0:T(8,128)(2,1)}, bf16[128,768]{1,0:T(8,128)(2,1)S(1)}, u32[]{:S(2)}, u32[]{:S(2)}) collective-permute-start(bf16[128,768]{1,0:T(8,128)(2,1)} %get-tuple-element.26), channel_id=1, source_target_pairs={{0,2},{1,3},{2,0},{3,1},{4,6},{5,7},{6,4},{7,5},{8,10},{9,11},{10,... | collective-permute-start | bytes 589832 | tf_op jit(solution)/shard_map/ppermute | solution.py:320
  21.1 15.4 %collective-permute-start.2 = (bf16[128,768]{1,0:T(8,128)(2,1)}, bf16[128,768]{1,0:T(8,128)(2,1)}, u32[]{:S(2)}, u32[]{:S(2)}) collective-permute-start(bf16[128,768]{1,0:T(8,128)(2,1)} %get-tuple-element.26), channel_id=1, source_target_pairs={{0,3},{1,2},{2,1},{3,0},{4,7},{5,6},{6,5},{7,4},{8,11},{9,10},{10,... | collective-permute-start | bytes 589832 | tf_op jit(solution)/shard_map/ppermute | solution.py:320
  55.8 3.2 %collective-permute-start.8 = (bf16[768,384]{0,1:T(8,128)(2,1)S(1)}, bf16[768,384]{0,1:T(8,128)(2,1)S(1)}, u32[]{:S(2)}, u32[]{:S(2)}) collective-permute-start(bf16[768,384]{0,1:T(8,128)(2,1)S(1)} %fusion.2), channel_id=1, source_target_pairs={{0,64},{64,0},{128,192},{192,128},{1,65},{65,1},{129,193},{193,129... | collective-permute-start | bytes 1769480 | tf_op jit(solution)/shard_map/ppermute | solution.py:324
  57.4 14.0 %collective-permute-start.7 = (bf16[256,768]{1,0:T(8,128)(2,1)}, bf16[256,768]{1,0:T(8,128)(2,1)S(1)}, u32[]{:S(2)}, u32[]{:S(2)}) collective-permute-start(bf16[256,768]{1,0:T(8,128)(2,1)} %get-tuple-element.34), channel_id=1, source_target_pairs={{0,4},{1,5},{2,6},{3,7},{4,0},{5,1},{6,2},{7,3},{8,12},{9,13},{10,... | collective-permute-start | bytes 1179656 | tf_op jit(solution)/shard_map/ppermute | solution.py:320
  60.4 17.6 %all-to-all-start = ((bf16[16,48,384]{2,1,0:T(8,128)(2,1)}), bf16[16,48,384]{2,1,0:T(8,128)(2,1)S(1)}, u32[]{:S(2)}, u32[]{:S(2)}) async-start(bf16[16,48,384]{2,1,0:T(8,128)(2,1)} %bitcast.4), calls=%async_computation | async-start | bytes 1179648 | tf_op jit(solution)/shard_map/all_to_all | solution.py:344
  67.2 15.6 %collective-permute-start.9 = (bf16[128,768]{1,0:T(8,128)(2,1)}, bf16[128,768]{1,0:T(8,128)(2,1)}, u32[]{:S(2)}, u32[]{:S(2)}) collective-permute-start(bf16[128,768]{1,0:T(8,128)(2,1)} %get-tuple-element.35), channel_id=1, source_target_pairs={{0,2},{1,3},{2,0},{3,1},{4,6},{5,7},{6,4},{7,5},{8,10},{9,11},{10,... | collective-permute-start | bytes 589832 | tf_op jit(solution)/shard_map/ppermute | solution.py:320
  69.4 13.4 %collective-permute-start.10 = (bf16[128,768]{1,0:T(8,128)(2,1)}, bf16[128,768]{1,0:T(8,128)(2,1)}, u32[]{:S(2)}, u32[]{:S(2)}) collective-permute-start(bf16[128,768]{1,0:T(8,128)(2,1)} %get-tuple-element.36), channel_id=1, source_target_pairs={{0,3},{1,2},{2,1},{3,0},{4,7},{5,6},{6,5},{7,4},{8,11},{9,10},{10,... | collective-permute-start | bytes 589832 | tf_op jit(solution)/shard_map/ppermute | solution.py:320
  71.4 29.5 %collective-permute-start.14 = (bf16[384,768]{1,0:T(8,128)(2,1)}, bf16[384,768]{1,0:T(8,128)(2,1)}, u32[]{:S(2)}, u32[]{:S(2)}) collective-permute-start(bf16[384,768]{1,0:T(8,128)(2,1)} %get-tuple-element.38), channel_id=1, source_target_pairs={{0,1},{1,0},{2,3},{3,2},{4,5},{5,4},{6,7},{7,6},{8,9},{9,8},{10,11... | collective-permute-start | bytes 1769480 | tf_op jit(solution)/shard_map/ppermute | solution.py:320
  82.9 14.3 %collective-permute-start.11 = (bf16[80,768]{1,0:T(8,128)(2,1)S(1)}, bf16[80,768]{1,0:T(8,128)(2,1)S(1)}, u32[]{:S(2)}, u32[]{:S(2)}) collective-permute-start(bf16[80,768]{1,0:T(8,128)(2,1)S(1)} %fusion.12), channel_id=1, source_target_pairs={{0,1},{1,0},{2,3},{3,2},{4,5},{5,4},{6,7},{7,6},{8,9},{9,8},{10,11... | collective-permute-start | bytes 368648 | tf_op jit(solution)/shard_map/ppermute | solution.py:320
  87.4 9.8 %collective-permute-start.12 = (bf16[80,768]{1,0:T(8,128)(2,1)S(1)}, bf16[80,768]{1,0:T(8,128)(2,1)S(1)}, u32[]{:S(2)}, u32[]{:S(2)}) collective-permute-start(bf16[80,768]{1,0:T(8,128)(2,1)S(1)} %fusion.13), channel_id=1, source_target_pairs={{0,2},{1,3},{2,0},{3,1},{4,6},{5,7},{6,4},{7,5},{8,10},{9,11},{10,... | collective-permute-start | bytes 368648 | tf_op jit(solution)/shard_map/ppermute | solution.py:320
  88.4 12.4 %collective-permute-start.13 = (bf16[80,768]{1,0:T(8,128)(2,1)S(1)}, bf16[80,768]{1,0:T(8,128)(2,1)S(1)}, u32[]{:S(2)}, u32[]{:S(2)}) collective-permute-start(bf16[80,768]{1,0:T(8,128)(2,1)S(1)} %fusion.14), channel_id=1, source_target_pairs={{0,3},{1,2},{2,1},{3,0},{4,7},{5,6},{6,5},{7,4},{8,11},{9,10},{10,... | collective-permute-start | bytes 368648 | tf_op jit(solution)/shard_map/ppermute | solution.py:320
  97.2 10.5 %copy-start.6 = (bf16[80,768]{1,0:T(8,128)(2,1)}, bf16[80,768]{1,0:T(8,128)(2,1)S(1)}, u32[]{:S(2)}) copy-start(bf16[80,768]{1,0:T(8,128)(2,1)S(1)} %collective-permute-done.11.far1_ref) | copy-start | bytes 368644
  100.9 13.0 %collective-permute-start.17 = (bf16[12,384]{1,0:T(8,128)(2,1)S(1)}, bf16[12,384]{1,0:T(8,128)(2,1)S(1)}, u32[]{:S(2)}, u32[]{:S(2)}) collective-permute-start(bf16[12,384]{1,0:T(8,128)(2,1)S(1)} %add_convert_fusion), channel_id=1, source_target_pairs={{0,192},{64,128},{128,64},{192,0},{1,193},{65,129},{129,65},{193,1... | collective-permute-start | bytes 27656 | tf_op jit(solution)/shard_map/ppermute | solution.py:324
  107.3 6.5 %collective-permute-start.16 = (bf16[12,384]{1,0:T(8,128)(2,1)S(1)}, bf16[12,384]{1,0:T(8,128)(2,1)S(1)}, u32[]{:S(2)}, u32[]{:S(2)}) collective-permute-start(bf16[12,384]{1,0:T(8,128)(2,1)S(1)} %add_convert_fusion), channel_id=1, source_target_pairs={{0,64},{64,0},{128,192},{192,128},{1,65},{65,1},{129,193},{193,129... | collective-permute-start | bytes 27656 | tf_op jit(solution)/shard_map/ppermute | solution.py:324
  107.3 6.5 %collective-permute-start.15 = (bf16[12,384]{1,0:T(8,128)(2,1)S(1)}, bf16[12,384]{1,0:T(8,128)(2,1)S(1)}, u32[]{:S(2)}, u32[]{:S(2)}) collective-permute-start(bf16[12,384]{1,0:T(8,128)(2,1)S(1)} %add_convert_fusion), channel_id=1, source_target_pairs={{0,128},{64,192},{128,0},{192,64},{1,129},{65,193},{129,1},{193,65... | collective-permute-start | bytes 27656 | tf_op jit(solution)/shard_map/ppermute | solution.py:324
  (7 other events, 39.2 us)

commit v3 on v2

--- a/solution.py
+++ b/solution.py
@@ -137,9 +137,8 @@
     ]
 
 
-def backward_of(query_sides, grad, attended_t, keys_t, values, raw, raw_pair, inverse, query_grad_ref, out_refs, sums):
+def backward_of(query_sides, grad, attended_t, keys_t, values, raw, raw_pair, inverse, query_grad_ref, out_refs):
     local_ref, own1_ref, own2_ref, far_ref, back_ref, send1_ref, send2_ref, send3_ref = out_refs
-    key_sum, value_sum = sums
     rows_dev = grad.shape[0]
     n1, n2, n3 = rows_dev // 2, rows_dev // 4, rows_dev // 8
     grad_t = grad.T.astype(F32)
@@ -157,10 +156,10 @@
         axis=0,
     )
     query_grad_ref[0] = (query_t * (1.0 / math.sqrt(HEAD_DIM))).astype(BF16).T
-    key_sum[...] = jnp.dot(
+    key_sum = jnp.dot(
         jnp.concatenate(score_grads, axis=1), jnp.concatenate(query_sides, axis=0), preferred_element_type=F32
     )
-    value_sum[...] = jnp.dot(raw_pair, jnp.concatenate(grad_sides, axis=0), preferred_element_type=F32)
+    value_sum = jnp.dot(raw_pair, jnp.concatenate(grad_sides, axis=0), preferred_element_type=F32)
     targets = [(local_ref, 0, rows_dev), (own1_ref, 0, n1), (send1_ref, 0, n1)]
     targets += [(own2_ref, 0, n2), (send1_ref, 2 * n1, n2), (send2_ref, 0, n2), (send3_ref, 0, n2)]
     targets += [(far_ref, 2 * n3 * idx, n3) for idx in range(4)]
@@ -178,7 +177,7 @@
 
 def both_kernel(query_ref, key_ref, value_ref, near_ref, *refs):
     gathered, grad_ref, attended_ref, query_grad_ref = refs[:8], refs[8], refs[9], refs[10]
-    outs, (key_set, value_set, key_sum, value_sum) = refs[11:-4], refs[-4:]
+    outs, (key_set, value_set) = refs[11:-2], refs[-2:]
     fill_sets(key_set, value_set, key_ref, value_ref, near_ref, gathered)
     query_sides = scaled_sides(query_ref)
     raw, inverse = weights_of(query_sides, key_set[...])
@@ -186,7 +185,7 @@
     attended_ref[...] = jnp.concatenate(attended_t, axis=0).T
     backward_of(
         query_sides, grad_ref[...], attended_t, key_set[...].T, value_set[...], raw,
-        jnp.concatenate(raw, axis=1), inverse, query_grad_ref, outs, (key_sum, value_sum),
+        jnp.concatenate(raw, axis=1), inverse, query_grad_ref, outs,
     )
 
 
@@ -196,7 +195,6 @@
         self.rows_dev, self.feature, self.width = rows_dev, feature, group[1] * PAIR
         self.set_rows = 4 * rows_dev
         self.given = pl.BlockSpec((1, rows_dev, PAIR), lambda i: (0, 0, group[0] + i))
-        self.sums = [pltpu.VMEM((self.set_rows, PAIR), F32)] * 2
         self.sets = [pltpu.VMEM((self.set_rows, PAIR), BF16)] * 2
 
     def whole(self, rows):
@@ -210,7 +208,7 @@
 
     def gradient_outs(self):
         rows, shape = self.rows_dev, jax.ShapeDtypeStruct
-        wide = [(2 * rows, F32), (rows, F32), (rows // 2, F32), (rows, F32)]
+        wide = [(2 * rows, F32), (rows, F32), (rows // 2, F32), (rows, BF16)]
         narrow = [rows, 3 * rows // 2, rows // 2, rows // 2]
         specs = [self.given] + [self.whole(count) for count, _ in wide] + [self.part(count) for count in narrow]
         shapes = [shape((1, rows, self.feature), BF16)]
@@ -243,7 +241,7 @@
     return lay.call(
         both_kernel, "attend_both", operands, [lay.given] * 3 + [lay.of(block) for block in operands[3:]],
         [lay.whole(rows_dev)] + specs, [jax.ShapeDtypeStruct((rows_dev, feature), BF16)] + shapes,
-        lay.sets + lay.sums, 2.6,
+        lay.sets, 2.6,
     )
 
 
@@ -262,7 +260,7 @@
             totals = (
                 own1_ref[:, at] + wide(pair_ref, at, slice(0, rows_dev)),
                 own2_ref[:, at] + wide(pair_ref, at, slice(rows_dev, None)) + wide(mid2_ref, at) + wide(mid3_ref, at),
-                own3_ref[:, at] + sum(wide(ref, at, slice(0, own3_ref.shape[0])) for ref in (far1_ref, far2_ref, far3_ref)),
+                wide(own3_ref, at) + sum(wide(ref, at, slice(0, own3_ref.shape[0])) for ref in (far1_ref, far2_ref, far3_ref)),
             )
             key_rows = jnp.concatenate([t[: t.shape[0] // 2] for t in totals], axis=0)
             value_rows = jnp.concatenate([t[t.shape[0] // 2 :] for t in totals], axis=0)
@@ -293,6 +291,7 @@
     out = pl.BlockSpec((1, rows_dev, width), lambda i: (0, 0, i))
     shape = jax.ShapeDtypeStruct((1, rows_dev, feature), BF16)
     specs = [pl.BlockSpec((part.shape[0], width), lambda i: (0, i)) for part in (local,) + owns + fars]
+    specs[3] = pl.BlockSpec((rows_dev // 4, width), lambda i: (0, i))
     parts = []
     for (first, count), blocks in zip(GROUPS, returned):
         start, last = first // SPREAD_PAIRS, count // SPREAD_PAIRS - 1
@@ -342,13 +341,12 @@
     planes = lax.axis_size("seq") // RUN
     groups = [[RUN * place + z for place in range(planes)] for z in range(RUN)]
     shares = lax.all_to_all(total, "seq", 0, 0, axis_index_groups=groups, tiled=True)
-    return jnp.sum(shares.reshape(planes, -1, half).astype(F32), axis=0).astype(BF16)
+    return jnp.sum(shares.reshape(planes, -1, half).astype(F32), axis=0).astype(BF16), sent
 
 
 def slides_total(share, norm_factor):
-    parts = [slide_swap(share, bits) for bits in (1, 2, 3)]
-    mine = ((share.astype(F32) + parts[1].astype(F32)) * norm_factor).astype(BF16)
-    other = ((parts[0].astype(F32) + parts[2].astype(F32)) * norm_factor).astype(BF16)
+    mine = ((share.astype(F32) + slide_swap(share, 2).astype(F32)) * norm_factor).astype(BF16)
+    other = slide_swap(mine, 1)
     return jnp.where(
         lax.axis_index("dp") % 2 == 0, jnp.concatenate([mine, other], 1), jnp.concatenate([other, mine], 1)
     )
@@ -367,9 +365,13 @@
     attended, query_grad, local, own1, own2, far_grad, back = results[:7]
     cross_back = swap(back, 4)
     back1, back2, back3 = [swap(block, bits) for bits, block in zip((1, 2, 3), results[7:])]
-    share = plane_share(cotangent, attended)
-    share, (back2, back3) = after(share, [back2, back3])
-    far_grad = far_grad + cross_back.astype(F32)
+    mixed = lax.dot_general(
+        attended, out_weight, (((1,), (1,)), ((), ())), preferred_element_type=F32
+    ).astype(BF16)
+    share, sent = plane_share(cotangent, attended)
+    share, (mixed,) = after(share, [mixed])
+    far_grad, (back2, back3) = after(far_grad, [back2, back3])
+    far_grad = (far_grad.astype(F32) + cross_back.astype(F32)).astype(BF16)
     far_parts = [far_grad[bits * n3 : (bits + 1) * n3] for bits in range(4)]
     rows, half = share.shape[0] // RUN, share.shape[1]
     place = lax.axis_index("seq") % RUN
@@ -378,18 +380,15 @@
     far_back = []
     for bits in (1, 2, 3):
         padded = jnp.pad(share_parts[bits], ((0, -rows % 16), (0, feature - half)))
-        arrived = swap(jnp.concatenate([far_parts[bits].astype(BF16), padded], axis=0), bits)
+        arrived = swap(jnp.concatenate([far_parts[bits], padded], axis=0), bits)
         far_back.append(arrived)
         total = total + arrived[n3 : n3 + rows, :half].astype(F32)
     tiles = lax.axis_size("dp") * lax.axis_size("seq") * rows_dev
     total, (back1,) = after(total.astype(BF16), [back1])
     weight_grad = slides_total(total, 1.0 / math.sqrt(tiles))
     key_grad, value_grad = spread(
-        offsets, local, (own1, own2, far_parts[0]), tuple(far_back), [[back1, back2, back3]]
-    )
-    mixed = lax.dot_general(
-        attended, out_weight, (((1,), (1,)), ((), ())), preferred_element_type=F32
-    ).astype(BF16)
+        offsets, local, (own1, own2, far_grad), tuple(far_back), [[back1, back2, back3]]
+    )
     return mixed[None], query_grad, key_grad, value_grad, weight_grad
 
 

time: 115 us -> 107 us (0.930)
  starting transfers between devices: 39.7 us -> 36.5 us
  waiting for transfers between devices: 41 us -> 38.7 us
    ppermute x14, starting transfers between devices: 24.6 us -> 20.2 us  [swap(): lax.ppermute(block, 'seq', [(i, i ^ bits) for i in range(lax.axis_size('s...]
    ppermute x14, waiting for transfers between devices: 32.5 us -> 30 us  [swap(): lax.ppermute(block, 'seq', [(i, i ^ bits) for i in range(lax.axis_size('s...]
    all_to_all x1, waiting for transfers between devices: 5.42 us -> 7.54 us  [plane_share(): lax.all_to_all(total, 'seq', 0, 0, axis_index_groups=groups, tiled=True)]
    ppermute x4 -> x3, waiting for transfers between devices: 3.04 us -> 1.22 us  [slide_swap(): lax.ppermute(block, 'dp', [(i, i ^ bits) for i in range(lax.axis_size('dp...]
    another operation x1 -> x0, other arithmetic: 1.22 us -> none
    ppermute x4 -> x3, starting transfers between devices: 8.42 us -> 9.47 us  [slide_swap(): lax.ppermute(block, 'dp', [(i, i ^ bits) for i in range(lax.axis_size('dp...]
  transfers between devices with their start and end apart: 19 -> 18, of which waited for: 10 -> 9; matrix products, arithmetic and copies ran while one was open for 6% -> 5% of each run, Pallas kernels for 3% -> 3%
where the time goes in v3:
time: 107 us
  waiting for transfers between devices  38.7 us (36%)
  starting transfers between devices  36.5 us (34%)
  Pallas kernels  22.4 us (21%)
  matrix products  4.2 us (4%)
  local copies, waits for them, and re-layouts  2.71 us (3%)
  other arithmetic  1.81 us (2%)
    ppermute x14, waiting for transfers between devices, swap(): lax.ppermute(block, 'seq', [(i, i ^ bits) for i in range(lax.axis_size('s...  30 us
    ppermute x14, starting transfers between devices, swap(): lax.ppermute(block, 'seq', [(i, i ^ bits) for i in range(lax.axis_size('s...  20.2 us
    pallas_call x1, Pallas kernels, call(): pl.pallas_call(kernel, grid=(self.count,), in_specs=list(in_specs) + [pl....  16.3 us
    ppermute x3, starting transfers between devices, slide_swap(): lax.ppermute(block, 'dp', [(i, i ^ bits) for i in range(lax.axis_size('dp...  9.47 us
    all_to_all x1, waiting for transfers between devices, plane_share(): lax.all_to_all(total, 'seq', 0, 0, axis_index_groups=groups, tiled=True)  7.54 us
    all_to_all x1, starting transfers between devices, plane_share(): lax.all_to_all(total, 'seq', 0, 0, axis_index_groups=groups, tiled=True)  6.74 us
    pallas_call x1, Pallas kernels, spread(): pl.pallas_call(functools.partial(spread_kernel, GROUPS), grid=(feature //...  3.38 us
    pallas_call x1, Pallas kernels, pick(): pl.pallas_call(pick_kernel, grid=(feature // width,), in_specs=[pl.BlockS...  2.66 us
  transfers between devices with their start and end apart: 18, of which 9 were waited for; matrix products, arithmetic and copies ran while one was open for 5% of the time, Pallas kernels for 3%

profile of v3, /device:TPU:1, one launch (start us, length us, event | category | flops | bytes accessed | tf_op | source)
XLA Modules:
  0.0 107.1 jit_solution(1829167239212102509)
XLA Ops:
  0.7 2.7 %pick_rows.1 = (bf16[64,768]{1,0:T(8,128)(2,1)}, bf16[384,768]{1,0:T(8,128)(2,1)}, bf16[128,768]{1,0:T(8,128)(2,1)}) custom-call(s32[3,12]{1,0:T(4,128)} %offsets_ref.3, bf16[1,256,768]{2,1,0:T(8,128)(2,1)} %key_ref.3, bf16[1,256,768]{2,1,0:T(8,128)(2,1)} %value_ref.3), custom_call_target="tpu_custom_call" | custom-call | flops 2000000000 | bytes 2000000 | tf_op jit(solution)/shard_map/pick_rows/pallas_call | solution.py:82
  3.3 2.5 %collective-permute-start.3 = (bf16[64,768]{1,0:T(8,128)(2,1)}, bf16[64,768]{1,0:T(8,128)(2,1)S(1)}, u32[]{:S(2)}, u32[]{:S(2)}) collective-permute-start(bf16[64,768]{1,0:T(8,128)(2,1)} %get-tuple-element.29.refs_3_), channel_id=1, source_target_pairs={{0,1},{1,0},{2,3},{3,2},{4,5},{5,4},{6,7},{7,6},{8,9},{9,8},{10,11... | collective-permute-start | bytes 294920 | tf_op jit(solution)/shard_map/ppermute | solution.py:319
  5.8 3.0 %collective-permute-start.4 = (bf16[64,768]{1,0:T(8,128)(2,1)}, bf16[64,768]{1,0:T(8,128)(2,1)S(1)}, u32[]{:S(2)}, u32[]{:S(2)}) collective-permute-start(bf16[64,768]{1,0:T(8,128)(2,1)} %get-tuple-element.29.refs_3_), channel_id=1, source_target_pairs={{0,2},{1,3},{2,0},{3,1},{4,6},{5,7},{6,4},{7,5},{8,10},{9,11},{10,... | collective-permute-start | bytes 294920 | tf_op jit(solution)/shard_map/ppermute | solution.py:319
  9.1 2.6 %collective-permute-done.4.refs_5_ = bf16[64,768]{1,0:T(8,128)(2,1)S(1)} collective-permute-done((bf16[64,768]{1,0:T(8,128)(2,1)}, bf16[64,768]{1,0:T(8,128)(2,1)S(1)}, u32[]{:S(2)}, u32[]{:S(2)}) %collective-permute-start.4) | collective-permute-done | bytes 98336 | tf_op jit(solution)/shard_map/ppermute | solution.py:319
  11.6 3.6 %collective-permute-done.5.refs_6_ = bf16[64,768]{1,0:T(8,128)(2,1)S(1)} collective-permute-done((bf16[64,768]{1,0:T(8,128)(2,1)}, bf16[64,768]{1,0:T(8,128)(2,1)S(1)}, u32[]{:S(2)}, u32[]{:S(2)}) %collective-permute-start.5) | collective-permute-done | bytes 98336 | tf_op jit(solution)/shard_map/ppermute | solution.py:319
  16.2 1.4 %collective-permute-start.6 = (bf16[256,768]{1,0:T(8,128)(2,1)S(1)}, bf16[256,768]{1,0:T(8,128)(2,1)S(1)}, u32[]{:S(2)}, u32[]{:S(2)}) collective-permute-start(bf16[256,768]{1,0:T(8,128)(2,1)S(1)} %pad_maximum_fusion), channel_id=1, source_target_pairs={{0,4},{1,5},{2,6},{3,7},{4,0},{5,1},{6,2},{7,3},{8,12},{9,13},{10,... | collective-permute-start | bytes 1179656 | tf_op jit(solution)/shard_map/ppermute | solution.py:319
  17.6 3.5 %collective-permute-start.1 = (bf16[128,768]{1,0:T(8,128)(2,1)}, bf16[128,768]{1,0:T(8,128)(2,1)S(1)}, u32[]{:S(2)}, u32[]{:S(2)}) collective-permute-start(bf16[128,768]{1,0:T(8,128)(2,1)} %get-tuple-element.28), channel_id=1, source_target_pairs={{0,2},{1,3},{2,0},{3,1},{4,6},{5,7},{6,4},{7,5},{8,10},{9,11},{10,... | collective-permute-start | bytes 589832 | tf_op jit(solution)/shard_map/ppermute | solution.py:319
  23.6 5.7 %collective-permute-done.1.refs_1_ = bf16[128,768]{1,0:T(8,128)(2,1)S(1)} collective-permute-done((bf16[128,768]{1,0:T(8,128)(2,1)}, bf16[128,768]{1,0:T(8,128)(2,1)S(1)}, u32[]{:S(2)}, u32[]{:S(2)}) %collective-permute-start.1) | collective-permute-done | bytes 196640 | tf_op jit(solution)/shard_map/ppermute | solution.py:319
  29.3 7.2 %collective-permute-done.2.refs_2_ = bf16[128,768]{1,0:T(8,128)(2,1)} collective-permute-done((bf16[128,768]{1,0:T(8,128)(2,1)}, bf16[128,768]{1,0:T(8,128)(2,1)}, u32[]{:S(2)}, u32[]{:S(2)}) %collective-permute-start.2) | collective-permute-done | bytes 196640 | tf_op jit(solution)/shard_map/ppermute | solution.py:319
  38.1 16.3 %attend_both.1 = (bf16[256,768]{1,0:T(8,128)(2,1)}, bf16[1,256,768]{2,1,0:T(8,128)(2,1)}, f32[512,768]{1,0:T(8,128)}, f32[256,768]{1,0:T(8,128)}, f32[128,768]{1...) custom-call(bf16[1,256,768]{2,1,0:T(8,128)(2,1)} %query_ref.1, ...), custom_call_target="tpu_custom_call" | custom-call | flops 15600000000 | bytes 1000000 | tf_op jit(solution)/shard_map/attend_both/pallas_call | solution.py:220
  54.4 1.3 %fusion.2 = bf16[768,384]{0,1:T(8,128)(2,1)S(1)} fusion(bf16[1,256,768]{2,1,0:T(8,128)(2,1)S(1)} %copy-done.1, bf16[256,768]{1,0:T(8,128)(2,1)} %get-tuple-element.30, s32[]{:T(128)S(6)} %select_n.41), kind=kOutput, calls=%fused_computation.4 | convolution fusion | flops 151289856 | bytes 1179652 | tf_op jit(solution)/shard_map/dot_general | solution.py:337
  55.8 1.6 %collective-permute-start.7 = (bf16[768,384]{0,1:T(8,128)(2,1)S(1)}, bf16[768,384]{0,1:T(8,128)(2,1)S(1)}, u32[]{:S(2)}, u32[]{:S(2)}) collective-permute-start(bf16[768,384]{0,1:T(8,128)(2,1)S(1)} %fusion.2), channel_id=1, source_target_pairs={{0,64},{64,0},{128,192},{192,128},{1,65},{65,1},{129,193},{193,129... | collective-permute-start | bytes 1769480 | tf_op jit(solution)/shard_map/ppermute | solution.py:323
  57.4 2.4 %collective-permute-start.8 = (bf16[128,768]{1,0:T(8,128)(2,1)}, bf16[128,768]{1,0:T(8,128)(2,1)}, u32[]{:S(2)}, u32[]{:S(2)}) collective-permute-start(bf16[128,768]{1,0:T(8,128)(2,1)} %get-tuple-element.37), channel_id=1, source_target_pairs={{0,2},{1,3},{2,0},{3,1},{4,6},{5,7},{6,4},{7,5},{8,10},{9,11},{10,... | collective-permute-start | bytes 589832 | tf_op jit(solution)/shard_map/ppermute | solution.py:319
  59.7 2.0 %collective-permute-start.9 = (bf16[128,768]{1,0:T(8,128)(2,1)}, bf16[128,768]{1,0:T(8,128)(2,1)}, u32[]{:S(2)}, u32[]{:S(2)}) collective-permute-start(bf16[128,768]{1,0:T(8,128)(2,1)} %get-tuple-element.38), channel_id=1, source_target_pairs={{0,3},{1,2},{2,1},{3,0},{4,7},{5,6},{6,5},{7,4},{8,11},{9,10},{10,... | collective-permute-start | bytes 589832 | tf_op jit(solution)/shard_map/ppermute | solution.py:319
  63.3 6.7 %all-to-all-start = ((bf16[16,48,384]{2,1,0:T(8,128)(2,1)}), bf16[16,48,384]{2,1,0:T(8,128)(2,1)S(1)}, u32[]{:S(2)}, u32[]{:S(2)}) async-start(bf16[16,48,384]{2,1,0:T(8,128)(2,1)} %bitcast.3), calls=%async_computation | async-start | bytes 1179648 | tf_op jit(solution)/shard_map/all_to_all | solution.py:343
  71.3 2.0 %collective-permute-done.8.refs_1_ = bf16[128,768]{1,0:T(8,128)(2,1)} collective-permute-done((bf16[128,768]{1,0:T(8,128)(2,1)}, bf16[128,768]{1,0:T(8,128)(2,1)}, u32[]{:S(2)}, u32[]{:S(2)}) %collective-permute-start.8) | collective-permute-done | bytes 196640 | tf_op jit(solution)/shard_map/ppermute | solution.py:319
  73.5 7.5 %all-to-all-done = bf16[16,48,384]{2,1,0:T(8,128)(2,1)S(1)} async-done(((bf16[16,48,384]{2,1,0:T(8,128)(2,1)}), bf16[16,48,384]{2,1,0:T(8,128)(2,1)S(1)}, u32[]{:S(2)}, u32[]{:S(2)}) %all-to-all-start) | async-done | bytes 589856 | tf_op jit(solution)/shard_map/all_to_all | solution.py:343
  81.2 1.4 %collective-permute-start.13 = (bf16[80,768]{1,0:T(8,128)(2,1)S(1)}, bf16[80,768]{1,0:T(8,128)(2,1)S(1)}, u32[]{:S(2)}, u32[]{:S(2)}) collective-permute-start(bf16[80,768]{1,0:T(8,128)(2,1)S(1)} %fusion.13), channel_id=1, source_target_pairs={{0,3},{1,2},{2,1},{3,0},{4,7},{5,6},{6,5},{7,4},{8,11},{9,10},{10,... | collective-permute-start | bytes 368648 | tf_op jit(solution)/shard_map/ppermute | solution.py:319
  82.7 2.3 %collective-permute-start.11 = (bf16[80,768]{1,0:T(8,128)(2,1)S(1)}, bf16[80,768]{1,0:T(8,128)(2,1)S(1)}, u32[]{:S(2)}, u32[]{:S(2)}) collective-permute-start(bf16[80,768]{1,0:T(8,128)(2,1)S(1)} %fusion.11), channel_id=1, source_target_pairs={{0,1},{1,0},{2,3},{3,2},{4,5},{5,4},{6,7},{7,6},{8,9},{9,8},{10,11... | collective-permute-start | bytes 368648 | tf_op jit(solution)/shard_map/ppermute | solution.py:319
  85.0 2.9 %collective-permute-done.13.far3_ref = bf16[80,768]{1,0:T(8,128)(2,1)S(1)} collective-permute-done((bf16[80,768]{1,0:T(8,128)(2,1)S(1)}, bf16[80,768]{1,0:T(8,128)(2,1)S(1)}, u32[]{:S(2)}, u32[]{:S(2)}) %collective-permute-start.13) | collective-permute-done | bytes 122912 | tf_op jit(solution)/shard_map/ppermute | solution.py:319
  87.9 6.0 %collective-permute-done.12.far2_ref = bf16[80,768]{1,0:T(8,128)(2,1)S(1)} collective-permute-done((bf16[80,768]{1,0:T(8,128)(2,1)S(1)}, bf16[80,768]{1,0:T(8,128)(2,1)S(1)}, u32[]{:S(2)}, u32[]{:S(2)}) %collective-permute-start.12) | collective-permute-done | bytes 122912 | tf_op jit(solution)/shard_map/ppermute | solution.py:319
  94.0 5.3 %collective-permute-start.15 = (bf16[12,384]{1,0:T(8,128)(2,1)S(1)}, bf16[12,384]{1,0:T(8,128)(2,1)S(1)}, u32[]{:S(2)}, u32[]{:S(2)}) collective-permute-start(bf16[12,384]{1,0:T(8,128)(2,1)S(1)} %add_convert_fusion.1), channel_id=1, source_target_pairs={{0,128},{64,192},{128,0},{192,64},{1,129},{65,193},{129,1},{193,65... | collective-permute-start | bytes 27656 | tf_op jit(solution)/shard_map/ppermute | solution.py:323
  100.5 2.6 %collective-permute-start.16 = (bf16[12,384]{1,0:T(8,128)(2,1)S(1)}, bf16[12,384]{1,0:T(8,128)(2,1)S(1)}, u32[]{:S(2)}, u32[]{:S(2)}) collective-permute-start(bf16[12,384]{1,0:T(8,128)(2,1)S(1)} %multiply_convert_fusion), channel_id=1, source_target_pairs={{0,64},{64,0},{128,192},{192,128},{1,65},{65,1},{129,193},{193,129... | collective-permute-start | bytes 27656 | tf_op jit(solution)/shard_map/ppermute | solution.py:323
  103.1 3.4 %spread_rows.1 = (bf16[1,256,768]{2,1,0:T(8,128)(2,1)}, bf16[1,256,768]{2,1,0:T(8,128)(2,1)}) custom-call(s32[3,12]{1,0:T(4,128)} %offsets_ref.3, f32[512,768]{1,0:T(8,128)} %get-tuple-element.33.local_ref, f32[256,768]{1,0:T(8,128)} %get-tuple-element.34.own1_ref, f32[128,768]{1,0:T(8,128)} %get-tuple-element.35.own2_ref, bf16[256,768]{1,0:T(8,128)(2,1)} %copy-done.3, ...), custom_call_target="tpu_custom_call" | custom-call | flops 3000000000 | bytes 4000000 | tf_op jit(solution)/shard_map/spread_rows/pallas_call | solution.py:306
  (59 shorter events, 10.4 us)
Async XLA Ops:
  0.6 21.8 %copy-start = (bf16[768,768]{1,0:T(8,128)(2,1)S(1)}, bf16[768,768]{1,0:T(8,128)(2,1)}, u32[]{:S(2)}) copy-start(bf16[768,768]{1,0:T(8,128)(2,1)} %param.9) | copy-start | bytes 3538948
  0.6 21.8 %copy-start.1 = (bf16[1,256,768]{2,1,0:T(8,128)(2,1)S(1)}, bf16[1,256,768]{2,1,0:T(8,128)(2,1)}, u32[]{:S(2)}) copy-start(bf16[1,256,768]{2,1,0:T(8,128)(2,1)} %param.10) | copy-start | bytes 1179652
  3.3 5.8 %collective-permute-start.3 = (bf16[64,768]{1,0:T(8,128)(2,1)}, bf16[64,768]{1,0:T(8,128)(2,1)S(1)}, u32[]{:S(2)}, u32[]{:S(2)}) collective-permute-start(bf16[64,768]{1,0:T(8,128)(2,1)} %get-tuple-element.29.refs_3_), channel_id=1, source_target_pairs={{0,1},{1,0},{2,3},{3,2},{4,5},{5,4},{6,7},{7,6},{8,9},{9,8},{10,11... | collective-permute-start | bytes 294920 | tf_op jit(solution)/shard_map/ppermute | solution.py:319
  5.8 5.8 %collective-permute-start.4 = (bf16[64,768]{1,0:T(8,128)(2,1)}, bf16[64,768]{1,0:T(8,128)(2,1)S(1)}, u32[]{:S(2)}, u32[]{:S(2)}) collective-permute-start(bf16[64,768]{1,0:T(8,128)(2,1)} %get-tuple-element.29.refs_3_), channel_id=1, source_target_pairs={{0,2},{1,3},{2,0},{3,1},{4,6},{5,7},{6,4},{7,5},{8,10},{9,11},{10,... | collective-permute-start | bytes 294920 | tf_op jit(solution)/shard_map/ppermute | solution.py:319
  8.8 6.5 %collective-permute-start.5 = (bf16[64,768]{1,0:T(8,128)(2,1)}, bf16[64,768]{1,0:T(8,128)(2,1)S(1)}, u32[]{:S(2)}, u32[]{:S(2)}) collective-permute-start(bf16[64,768]{1,0:T(8,128)(2,1)} %get-tuple-element.29.refs_3_), channel_id=1, source_target_pairs={{0,3},{1,2},{2,1},{3,0},{4,7},{5,6},{6,5},{7,4},{8,11},{9,10},{10,... | collective-permute-start | bytes 294920 | tf_op jit(solution)/shard_map/ppermute | solution.py:319
  8.8 27.7 %collective-permute-start = (bf16[384,768]{1,0:T(8,128)(2,1)}, bf16[384,768]{1,0:T(8,128)(2,1)S(1)}, u32[]{:S(2)}, u32[]{:S(2)}) collective-permute-start(bf16[384,768]{1,0:T(8,128)(2,1)} %get-tuple-element.27.near_ref), channel_id=1, source_target_pairs={{0,1},{1,0},{2,3},{3,2},{4,5},{5,4},{6,7},{7,6},{8,9},{9,8},{10,11... | collective-permute-start | bytes 1769480 | tf_op jit(solution)/shard_map/ppermute | solution.py:319
  9.1 14.6 %copy-start.5 = (bf16[64,768]{1,0:T(8,128)(2,1)}, bf16[64,768]{1,0:T(8,128)(2,1)S(1)}, u32[]{:S(2)}) copy-start(bf16[64,768]{1,0:T(8,128)(2,1)S(1)} %collective-permute-done.3.refs_4_) | copy-start | bytes 294916
  11.6 12.0 %copy-start.6 = (bf16[64,768]{1,0:T(8,128)(2,1)}, bf16[64,768]{1,0:T(8,128)(2,1)S(1)}, u32[]{:S(2)}) copy-start(bf16[64,768]{1,0:T(8,128)(2,1)S(1)} %collective-permute-done.4.refs_5_) | copy-start | bytes 294916
  16.2 20.3 %collective-permute-start.6 = (bf16[256,768]{1,0:T(8,128)(2,1)S(1)}, bf16[256,768]{1,0:T(8,128)(2,1)S(1)}, u32[]{:S(2)}, u32[]{:S(2)}) collective-permute-start(bf16[256,768]{1,0:T(8,128)(2,1)S(1)} %pad_maximum_fusion), channel_id=1, source_target_pairs={{0,4},{1,5},{2,6},{3,7},{4,0},{5,1},{6,2},{7,3},{8,12},{9,13},{10,... | collective-permute-start | bytes 1179656 | tf_op jit(solution)/shard_map/ppermute | solution.py:319
  17.6 11.7 %collective-permute-start.1 = (bf16[128,768]{1,0:T(8,128)(2,1)}, bf16[128,768]{1,0:T(8,128)(2,1)S(1)}, u32[]{:S(2)}, u32[]{:S(2)}) collective-permute-start(bf16[128,768]{1,0:T(8,128)(2,1)} %get-tuple-element.28), channel_id=1, source_target_pairs={{0,2},{1,3},{2,0},{3,1},{4,6},{5,7},{6,4},{7,5},{8,10},{9,11},{10,... | collective-permute-start | bytes 589832 | tf_op jit(solution)/shard_map/ppermute | solution.py:319
  21.1 15.4 %collective-permute-start.2 = (bf16[128,768]{1,0:T(8,128)(2,1)}, bf16[128,768]{1,0:T(8,128)(2,1)}, u32[]{:S(2)}, u32[]{:S(2)}) collective-permute-start(bf16[128,768]{1,0:T(8,128)(2,1)} %get-tuple-element.28), channel_id=1, source_target_pairs={{0,3},{1,2},{2,1},{3,0},{4,7},{5,6},{6,5},{7,4},{8,11},{9,10},{10,... | collective-permute-start | bytes 589832 | tf_op jit(solution)/shard_map/ppermute | solution.py:319
  55.8 6.1 %collective-permute-start.7 = (bf16[768,384]{0,1:T(8,128)(2,1)S(1)}, bf16[768,384]{0,1:T(8,128)(2,1)S(1)}, u32[]{:S(2)}, u32[]{:S(2)}) collective-permute-start(bf16[768,384]{0,1:T(8,128)(2,1)S(1)} %fusion.2), channel_id=1, source_target_pairs={{0,64},{64,0},{128,192},{192,128},{1,65},{65,1},{129,193},{193,129... | collective-permute-start | bytes 1769480 | tf_op jit(solution)/shard_map/ppermute | solution.py:323
  57.4 16.0 %collective-permute-start.8 = (bf16[128,768]{1,0:T(8,128)(2,1)}, bf16[128,768]{1,0:T(8,128)(2,1)}, u32[]{:S(2)}, u32[]{:S(2)}) collective-permute-start(bf16[128,768]{1,0:T(8,128)(2,1)} %get-tuple-element.37), channel_id=1, source_target_pairs={{0,2},{1,3},{2,0},{3,1},{4,6},{5,7},{6,4},{7,5},{8,10},{9,11},{10,... | collective-permute-start | bytes 589832 | tf_op jit(solution)/shard_map/ppermute | solution.py:319
  59.7 13.6 %collective-permute-start.9 = (bf16[128,768]{1,0:T(8,128)(2,1)}, bf16[128,768]{1,0:T(8,128)(2,1)}, u32[]{:S(2)}, u32[]{:S(2)}) collective-permute-start(bf16[128,768]{1,0:T(8,128)(2,1)} %get-tuple-element.38), channel_id=1, source_target_pairs={{0,3},{1,2},{2,1},{3,0},{4,7},{5,6},{6,5},{7,4},{8,11},{9,10},{10,... | collective-permute-start | bytes 589832 | tf_op jit(solution)/shard_map/ppermute | solution.py:319
  61.7 11.6 %collective-permute-start.10 = (bf16[256,768]{1,0:T(8,128)(2,1)}, bf16[256,768]{1,0:T(8,128)(2,1)S(1)}, u32[]{:S(2)}, u32[]{:S(2)}) collective-permute-start(bf16[256,768]{1,0:T(8,128)(2,1)} %get-tuple-element.40), channel_id=1, source_target_pairs={{0,4},{1,5},{2,6},{3,7},{4,0},{5,1},{6,2},{7,3},{8,12},{9,13},{10,... | collective-permute-start | bytes 1179656 | tf_op jit(solution)/shard_map/ppermute | solution.py:319
  63.3 17.7 %all-to-all-start = ((bf16[16,48,384]{2,1,0:T(8,128)(2,1)}), bf16[16,48,384]{2,1,0:T(8,128)(2,1)S(1)}, u32[]{:S(2)}, u32[]{:S(2)}) async-start(bf16[16,48,384]{2,1,0:T(8,128)(2,1)} %bitcast.3), calls=%async_computation | async-start | bytes 1179648 | tf_op jit(solution)/shard_map/all_to_all | solution.py:343
  71.3 22.6 %collective-permute-start.14 = (bf16[384,768]{1,0:T(8,128)(2,1)}, bf16[384,768]{1,0:T(8,128)(2,1)}, u32[]{:S(2)}, u32[]{:S(2)}) collective-permute-start(bf16[384,768]{1,0:T(8,128)(2,1)} %get-tuple-element.42), channel_id=1, source_target_pairs={{0,1},{1,0},{2,3},{3,2},{4,5},{5,4},{6,7},{7,6},{8,9},{9,8},{10,11... | collective-permute-start | bytes 1769480 | tf_op jit(solution)/shard_map/ppermute | solution.py:319
  73.5 29.6 %copy-start.3 = (bf16[256,768]{1,0:T(8,128)(2,1)}, bf16[256,768]{1,0:T(8,128)(2,1)S(1)}, u32[]{:S(2)}) copy-start(bf16[256,768]{1,0:T(8,128)(2,1)S(1)} %add_convert_fusion.own3_ref) | copy-start | bytes 1179652
  81.2 6.7 %collective-permute-start.13 = (bf16[80,768]{1,0:T(8,128)(2,1)S(1)}, bf16[80,768]{1,0:T(8,128)(2,1)S(1)}, u32[]{:S(2)}, u32[]{:S(2)}) collective-permute-start(bf16[80,768]{1,0:T(8,128)(2,1)S(1)} %fusion.13), channel_id=1, source_target_pairs={{0,3},{1,2},{2,1},{3,0},{4,7},{5,6},{6,5},{7,4},{8,11},{9,10},{10,... | collective-permute-start | bytes 368648 | tf_op jit(solution)/shard_map/ppermute | solution.py:319
  82.6 11.4 %collective-permute-start.12 = (bf16[80,768]{1,0:T(8,128)(2,1)S(1)}, bf16[80,768]{1,0:T(8,128)(2,1)S(1)}, u32[]{:S(2)}, u32[]{:S(2)}) collective-permute-start(bf16[80,768]{1,0:T(8,128)(2,1)S(1)} %fusion.12), channel_id=1, source_target_pairs={{0,2},{1,3},{2,0},{3,1},{4,6},{5,7},{6,4},{7,5},{8,10},{9,11},{10,... | collective-permute-start | bytes 368648 | tf_op jit(solution)/shard_map/ppermute | solution.py:319
  82.7 11.2 %collective-permute-start.11 = (bf16[80,768]{1,0:T(8,128)(2,1)S(1)}, bf16[80,768]{1,0:T(8,128)(2,1)S(1)}, u32[]{:S(2)}, u32[]{:S(2)}) collective-permute-start(bf16[80,768]{1,0:T(8,128)(2,1)S(1)} %fusion.11), channel_id=1, source_target_pairs={{0,1},{1,0},{2,3},{3,2},{4,5},{5,4},{6,7},{7,6},{8,9},{9,8},{10,11... | collective-permute-start | bytes 368648 | tf_op jit(solution)/shard_map/ppermute | solution.py:319
  87.9 15.2 %copy-start.8 = (bf16[80,768]{1,0:T(8,128)(2,1)}, bf16[80,768]{1,0:T(8,128)(2,1)S(1)}, u32[]{:S(2)}) copy-start(bf16[80,768]{1,0:T(8,128)(2,1)S(1)} %collective-permute-done.13.far3_ref) | copy-start | bytes 368644
  94.0 6.5 %collective-permute-start.15 = (bf16[12,384]{1,0:T(8,128)(2,1)S(1)}, bf16[12,384]{1,0:T(8,128)(2,1)S(1)}, u32[]{:S(2)}, u32[]{:S(2)}) collective-permute-start(bf16[12,384]{1,0:T(8,128)(2,1)S(1)} %add_convert_fusion.1), channel_id=1, source_target_pairs={{0,128},{64,192},{128,0},{192,64},{1,129},{65,193},{129,1},{193,65... | collective-permute-start | bytes 27656 | tf_op jit(solution)/shard_map/ppermute | solution.py:323
  100.5 5.9 %collective-permute-start.16 = (bf16[12,384]{1,0:T(8,128)(2,1)S(1)}, bf16[12,384]{1,0:T(8,128)(2,1)S(1)}, u32[]{:S(2)}, u32[]{:S(2)}) collective-permute-start(bf16[12,384]{1,0:T(8,128)(2,1)S(1)} %multiply_convert_fusion), channel_id=1, source_target_pairs={{0,64},{64,0},{128,192},{192,128},{1,65},{65,1},{129,193},{193,129... | collective-permute-start | bytes 27656 | tf_op jit(solution)/shard_map/ppermute | solution.py:323
  (8 other events, 46.2 us)

commit v4 on v3

v4 whole, which is shorter than its diff:
```python
import functools
import math

import jax
import jax.numpy as jnp
from jax import lax
from jax.experimental import pallas as pl
from jax.experimental.pallas import tpu as pltpu
from jax.sharding import PartitionSpec as P

HEADS = 12
HEAD_DIM = 64
LEVELS = 3
PAIR = 2 * HEAD_DIM
VMEM_LIMIT = 60 * 1024 * 1024
LOG2E = 1.0 / math.log(2.0)
GROUPS = ((0, HEADS // 2),)
PICK_PAIRS = 3
SPREAD_PAIRS = 3
CORE_RATE = 10**9
RUN = 4
F32 = jnp.float32
BF16 = jnp.bfloat16


def lane_masks(row_count):
    lane = lax.broadcasted_iota(jnp.int32, (row_count, PAIR), 1)
    return lane < HEAD_DIM, lane >= HEAD_DIM


def selection(offsets_ref, head, rows_dev, levels, transposed):
    counts = [rows_dev >> (level + 1) for level in levels]
    shape = (rows_dev, sum(counts)) if transposed else (sum(counts), rows_dev)
    slot = lax.broadcasted_iota(jnp.int32, shape, 1 if transposed else 0)
    row = lax.broadcasted_iota(jnp.int32, shape, 0 if transposed else 1)
    target, start = None, 0
    for level, count in zip(levels, counts):
        found = (2 << level) * (slot - start) + offsets_ref[level, head]
        target = found if target is None else jnp.where(slot < start, target, found)
        start += count
    return (row == target).astype(F32).astype(BF16)


def lanes(pair):
    return slice(pair * PAIR, (pair + 1) * PAIR)


def pick_kernel(offsets_ref, key_ref, value_ref, far_ref, near_ref, mid_ref):
    rows_dev = key_ref.shape[1]
    n1, n2, n3 = rows_dev // 2, rows_dev // 4, rows_dev // 8
    for pair in range(PICK_PAIRS):
        head = 2 * (PICK_PAIRS * pl.program_id(0) + pair)
        at = lanes(pair)
        both = jnp.concatenate([key_ref[0, :, at], value_ref[0, :, at]], axis=1)
        rows = [
            jnp.dot(selection(offsets_ref, head + side, rows_dev, (0, 1, 2), False), both, preferred_element_type=F32)
            for side in range(2)
        ]
        low, _ = lane_masks(rows[0].shape[0])
        key_rows = jnp.where(low, rows[0][:, :PAIR], rows[1][:, :PAIR]).astype(BF16)
        value_rows = jnp.where(low, rows[0][:, PAIR:], rows[1][:, PAIR:]).astype(BF16)
        near_ref[:n1, at] = key_rows[:n1]
        near_ref[n1 : 2 * n1, at] = value_rows[:n1]
        near_ref[2 * n1 : 2 * n1 + n2, at] = key_rows[n1 : n1 + n2]
        near_ref[2 * n1 + n2 :, at] = value_rows[n1 : n1 + n2]
        mid_ref[:n2, at] = key_rows[n1 : n1 + n2]
        mid_ref[n2:, at] = value_rows[n1 : n1 + n2]
        far_ref[:n3, at] = key_rows[n1 + n2 :]
        far_ref[n3:, at] = value_rows[n1 + n2 :]


def pick(offsets, keys, values):
    rows_dev, feature = keys.shape[1:]
    width = PICK_PAIRS * PAIR
    whole = pl.BlockSpec((1, rows_dev, width), lambda i: (0, 0, i))
    rows = (rows_dev // 4, 3 * rows_dev // 2, rows_dev // 2)
    return pl.pallas_call(
        pick_kernel,
        grid=(feature // width,),
        in_specs=[pl.BlockSpec(memory_space=pltpu.SMEM), whole, whole],
        out_specs=[pl.BlockSpec((count, width), lambda i: (0, i)) for count in rows],
        out_shape=[jax.ShapeDtypeStruct((count, feature), BF16) for count in rows],
        compiler_params=pltpu.CompilerParams(vmem_limit_bytes=VMEM_LIMIT),
        cost_estimate=pl.CostEstimate(flops=2 * CORE_RATE, bytes_accessed=2 * 10**6, transcendentals=0),
        name="pick_rows",
    )(offsets, keys, values)


def sides(block):
    return [jnp.where(mask, block, jnp.zeros_like(block)) for mask in lane_masks(block.shape[0])]


def head_rows(side):
    return slice(side * HEAD_DIM, (side + 1) * HEAD_DIM)


NT = (((1,), (1,)), ((), ()))


def copy_rows(key_set, value_set, key_ref, value_ref, sources):
    at = 0
    if key_ref is not None:
        at = key_ref.shape[1]
        key_set[:at] = key_ref[0]
        value_set[:at] = value_ref[0]
    for ref, base, count in sources:
        key_set[at : at + count] = ref[base : base + count]
        value_set[at : at + count] = ref[base + count : base + 2 * count]
        at += count


def level_rows(rows_dev):
    return rows_dev // 2, rows_dev // 4, rows_dev // 8


def scaled_sides(query_ref):
    return sides((query_ref[0].astype(F32) * (1.0 / math.sqrt(HEAD_DIM))).astype(BF16))


def scores_of(keys, query_side):
    return lax.dot_general(keys, query_side, NT, preferred_element_type=F32)


def own_kernel(query_ref, key_ref, value_ref, near_ref, mid_ref, far_ref, raw_ref, stats_ref, part_ref, key_set, value_set):
    n1, n2, n3 = level_rows(query_ref.shape[1])
    copy_rows(key_set, value_set, key_ref, value_ref, [(near_ref, 0, n1), (mid_ref, 0, n2), (far_ref, 0, n3)])
    values_t = value_set[...].T
    rows_dev = query_ref.shape[1]
    for side, query_side in enumerate(scaled_sides(query_ref)):
        scores = scores_of(key_set[...], query_side)
        row_max = jnp.max(scores, axis=0, keepdims=True)
        weights = jnp.exp2(scores * LOG2E - row_max * LOG2E)
        raw = weights.astype(BF16)
        raw_ref[0, :, side * rows_dev : (side + 1) * rows_dev] = raw
        total = jnp.sum(weights, axis=0, keepdims=True)
        for place, row in enumerate((row_max, total)):
            first = 16 * side + 8 * place
            stats_ref[0, first : first + 8] = jnp.broadcast_to(row, (8, rows_dev))
        part_ref[0, head_rows(side)] = jnp.dot(values_t[head_rows(side)], raw, preferred_element_type=F32)


def both_kernel(query_ref, key_ref, value_ref, near_ref, *refs):
    (near_pair_ref, mid2_ref, mid3_ref, far0_ref, far1_ref, far2_ref, far3_ref, cross_ref,
     grad_ref, mid_ref, own_raw_ref, stats_ref, part_ref) = refs[:13]
    attended_ref, query_grad_ref = refs[13:15]
    local_ref, own1_ref, own2_ref, far_ref, back_ref, send1_ref, send2_ref, send3_ref = refs[15:-2]
    key_set, value_set = refs[-2:]
    rows_dev = query_ref.shape[1]
    n1, n2, n3 = level_rows(rows_dev)
    own = rows_dev + n1 + n2 + n3
    copy_rows(
        key_set, value_set, key_ref, value_ref,
        [(near_ref, 0, n1), (mid_ref, 0, n2), (far0_ref, 0, n3)]
        + [(near_pair_ref, 0, n1), (near_pair_ref, 2 * n1, n2), (mid2_ref, 0, n2), (mid3_ref, 0, n2)]
        + [(ref, 0, n3) for ref in (far1_ref, far2_ref, far3_ref)]
        + [(cross_ref, 2 * n3 * idx, n3) for idx in range(4)],
    )
    query_sides = scaled_sides(query_ref)
    scores = [scores_of(key_set[own:], side) for side in query_sides]
    far_values_t = value_set[own:].T
    raw, scales, attended_t = [], [], []
    for side in range(2):
        own_max, own_sum = (stats_ref[0, first : first + 1] for first in (16 * side, 16 * side + 8))
        row_max = jnp.maximum(own_max, jnp.max(scores[side], axis=0, keepdims=True))
        weights = jnp.exp2(scores[side] * LOG2E - row_max * LOG2E)
        own_factor = jnp.exp2((own_max - row_max) * LOG2E)
        inverse = 1.0 / (own_sum * own_factor + jnp.sum(weights, axis=0, keepdims=True))
        raw.append(weights.astype(BF16))
        scales.append((inverse * own_factor, inverse))
        rows = head_rows(side)
        product = jnp.dot(far_values_t[rows], raw[side], preferred_element_type=F32)
        attended_t.append(((part_ref[0, rows] * own_factor + product) * inverse).astype(BF16))
    attended_ref[...] = jnp.concatenate(attended_t, axis=0).T

    grad_t = grad_ref[...].T.astype(F32)
    own_raw = own_raw_ref[0]
    raws = [(own_raw[:, side * rows_dev : (side + 1) * rows_dev], raw[side]) for side in range(2)]
    deltas = [
        jnp.sum(grad_t[head_rows(side)] * attended_t[side].astype(F32), axis=0, keepdims=True) for side in range(2)
    ]
    score_grads = [[], []]
    value_sums = []
    for part, values in enumerate((value_set[:own], value_set[own:])):
        normed = [grad_t[head_rows(side)] * scales[side][part] for side in range(2)]
        grad_sides = sides(jnp.concatenate(normed, axis=0).astype(BF16).T)
        for side in range(2):
            prob_grad = scores_of(values, grad_sides[side])
            difference = prob_grad - deltas[side] * scales[side][part]
            score_grads[side].append((raws[side][part].astype(F32) * difference).astype(BF16))
        pair = own_raw if part == 0 else jnp.concatenate(raw, axis=1)
        value_sums.append(jnp.dot(pair, jnp.concatenate(grad_sides, axis=0), preferred_element_type=F32))
    value_sum = jnp.concatenate(value_sums, axis=0)
    score_grads = [jnp.concatenate(parts, axis=0) for parts in score_grads]
    keys_t = key_set[...].T
    query_t = jnp.concatenate(
        [jnp.dot(keys_t[head_rows(side)], score_grads[side], preferred_element_type=F32) for side in range(2)],
        axis=0,
    )
    query_grad_ref[0] = (query_t * (1.0 / math.sqrt(HEAD_DIM))).astype(BF16).T
    key_sum = jnp.dot(
        jnp.concatenate(score_grads, axis=1), jnp.concatenate(query_sides, axis=0), preferred_element_type=F32
    )
    targets = [(local_ref, 0, rows_dev), (own1_ref, 0, n1), (own2_ref, 0, n2), (far_ref, 0, n3)]
    targets += [(send1_ref, 0, n1), (send1_ref, 2 * n1, n2), (send2_ref, 0, n2), (send3_ref, 0, n2)]
    targets += [(far_ref, 2 * n3 * idx, n3) for idx in range(1, 4)]
    targets += [(back_ref, 2 * n3 * idx, n3) for idx in range(4)]
    at = 0
    for ref, base, count in targets:
        ref[base : base + count] = key_sum[at : at + count].astype(ref.dtype)
        ref[base + count : base + 2 * count] = value_sum[at : at + count].astype(ref.dtype)
        at += count


class Layout:
    def __init__(self, group, rows_dev, feature):
        self.first, self.count = group
        self.rows_dev, self.feature, self.width = rows_dev, feature, group[1] * PAIR
        self.set_rows = 4 * rows_dev
        self.given = pl.BlockSpec((1, rows_dev, PAIR), lambda i: (0, 0, group[0] + i))
        self.sets = [pltpu.VMEM((self.set_rows, PAIR), BF16)] * 2

    def whole(self, rows):
        return pl.BlockSpec((rows, PAIR), lambda i: (0, self.first + i))

    def part(self, rows):
        return pl.BlockSpec((rows, PAIR), lambda i: (0, i))

    def stacked(self, block):
        return pl.BlockSpec((1,) + block.shape[1:], lambda i: (i, 0, 0))

    def of(self, block):
        return self.part(block.shape[0]) if block.shape[1] == self.width else self.whole(block.shape[0])

    def gradient_outs(self):
        rows, shape = self.rows_dev, jax.ShapeDtypeStruct
        wide = [(2 * rows, F32), (rows, F32), (rows // 2, F32), (rows, BF16)]
        narrow = [rows, 3 * rows // 2, rows // 2, rows // 2]
        specs = [self.given] + [self.whole(count) for count, _ in wide] + [self.part(count) for count in narrow]
        shapes = [shape((1, rows, self.feature), BF16)]
        shapes += [shape((count, self.feature), kind) for count, kind in wide]
        shapes += [shape((count, self.width), BF16) for count in narrow]
        return specs, shapes

    def call(self, kernel, name, operands, in_specs, out_specs, out_shapes, scratch, micros, before=()):
        return pl.pallas_call(
            kernel,
            grid=(self.count,),
            in_specs=list(in_specs) + [pl.BlockSpec(memory_space=pl.ANY)] * len(before),
            out_specs=out_specs,
            out_shape=out_shapes,
            input_output_aliases={len(operands) + idx: idx for idx in range(len(before))},
            scratch_shapes=scratch,
            compiler_params=pltpu.CompilerParams(vmem_limit_bytes=VMEM_LIMIT),
            cost_estimate=pl.CostEstimate(
                flops=int(micros * self.count * CORE_RATE), bytes_accessed=10**6, transcendentals=0
            ),
            name=name,
        )(*operands, *before)


def attend_own(group, queries, keys, values, near, mid, far):
    rows_dev, feature = queries.shape[1:]
    lay = Layout(group, rows_dev, feature)
    own = rows_dev + sum(level_rows(rows_dev))
    shape = jax.ShapeDtypeStruct
    shapes = [
        shape((lay.count, own, 2 * rows_dev), BF16),
        shape((lay.count, 32, rows_dev), F32),
        shape((lay.count, PAIR, rows_dev), F32),
    ]
    operands = (queries, keys, values, near, mid, far)
    return lay.call(
        own_kernel, "attend_own", operands, [lay.given] * 3 + [lay.of(block) for block in operands[3:]],
        [lay.stacked(out) for out in shapes], shapes, [pltpu.VMEM((own, PAIR), BF16)] * 2, 0.1,
    )


def attend_both(group, queries, keys, values, grads, near, mid, gathered, own_parts):
    rows_dev, feature = queries.shape[1:]
    lay = Layout(group, rows_dev, feature)
    specs, shapes = lay.gradient_outs()
    operands = (queries, keys, values, near) + tuple(gathered) + (grads, mid) + tuple(own_parts)
    return lay.call(
        both_kernel, "attend_both", operands,
        [lay.given] * 3 + [lay.of(block) for block in operands[3:-3]] + [lay.stacked(block) for block in own_parts],
        [lay.whole(rows_dev)] + specs, [jax.ShapeDtypeStruct((rows_dev, feature), BF16)] + shapes,
        lay.sets, 2.6,
    )


def spread_kernel(levels, offsets_ref, key_base_ref, value_base_ref, *refs):
    key_ref, value_ref = refs[-2:]
    rows_dev = key_ref.shape[1]
    for pair in range(SPREAD_PAIRS):
        head = 2 * (SPREAD_PAIRS * pl.program_id(0) + pair)
        at = lanes(pair)
        key_rows, value_rows, used = [], [], 0
        for level, starts in levels:
            count = rows_dev >> (level + 1)
            total = sum(
                ref[start : start + 2 * count, at].astype(F32)
                for ref, start in zip(refs[used : used + len(starts)], starts)
            )
            used += len(starts)
            key_rows.append(total[:count])
            value_rows.append(total[count:])
        both = jnp.concatenate(
            [jnp.concatenate(key_rows, axis=0), jnp.concatenate(value_rows, axis=0)], axis=1
        ).astype(BF16)
        spread = [
            jnp.dot(
                selection(offsets_ref, head + side, rows_dev, [level for level, _ in levels], True),
                both,
                preferred_element_type=F32,
            )
            for side in range(2)
        ]
        low, _ = lane_masks(rows_dev)
        for half, (base_ref, ref) in enumerate(((key_base_ref, key_ref), (value_base_ref, value_ref))):
            columns = slice(half * PAIR, (half + 1) * PAIR)
            ref[0, :, at] = (
                base_ref[0, :, at] + jnp.where(low, spread[0][:, columns], spread[1][:, columns])
            ).astype(ref.dtype)


def spread(offsets, base, levels, kind):
    key_base, value_base = base
    rows_dev, feature = key_base.shape[1:]
    width = SPREAD_PAIRS * PAIR
    blocks = [block for _, parts in levels for block, _ in parts]
    out = pl.BlockSpec((1, rows_dev, width), lambda i: (0, 0, i))
    shape = jax.ShapeDtypeStruct((1, rows_dev, feature), kind)
    return pl.pallas_call(
        functools.partial(spread_kernel, [(level, [start for _, start in parts]) for level, parts in levels]),
        grid=(feature // width,),
        in_specs=[
            pl.BlockSpec(memory_space=pltpu.SMEM),
            pl.BlockSpec((1, rows_dev, width), lambda i: (0, 0, i)),
            pl.BlockSpec((1, rows_dev, width), lambda i: (int(key_base is value_base), 0, i)),
        ]
        + [pl.BlockSpec((block.shape[0], width), lambda i: (0, i)) for block in blocks],
        out_specs=[out, out],
        out_shape=[shape, shape],
        compiler_params=pltpu.CompilerParams(vmem_limit_bytes=VMEM_LIMIT),
        cost_estimate=pl.CostEstimate(flops=2 * CORE_RATE, bytes_accessed=4 * 10**6, transcendentals=0),
        name="spread_rows",
    )(offsets, key_base, value_base, *blocks)


def swap(block, bits):
    return lax.ppermute(block, "seq", [(i, i ^ bits) for i in range(lax.axis_size("seq"))])


def slide_swap(block, bits):
    return lax.ppermute(block, "dp", [(i, i ^ bits) for i in range(lax.axis_size("dp"))])


def after(block, others):
    tied = lax.optimization_barrier((block,) + tuple(others))
    return tied[0], list(tied[1:])


def plane_share(cotangent, attended):
    core = lax.axis_index("dp") % 2
    half = attended.shape[1] // 2

    def columns(which):
        block = lax.dynamic_slice_in_dim(attended, which * half, half, 1)
        return lax.dot_general(cotangent, block, (((0,), (0,)), ((), ())), preferred_element_type=F32)

    sent = slide_swap(columns(1 - core).astype(BF16), 1)
    total = (columns(core) + sent.astype(F32)).astype(BF16)
    planes = lax.axis_size("seq") // RUN
    groups = [[RUN * place + z for place in range(planes)] for z in range(RUN)]
    shares = lax.all_to_all(total, "seq", 0, 0, axis_index_groups=groups, tiled=True)
    return jnp.sum(shares.reshape(planes, -1, half).astype(F32), axis=0).astype(BF16), sent


def slides_total(share, norm_factor, others):
    mine = ((share.astype(F32) + slide_swap(share, 2).astype(F32)) * norm_factor).astype(BF16)
    mine, others = after(mine, others)
    other = slide_swap(mine, 1)
    whole = jnp.where(
        lax.axis_index("dp") % 2 == 0, jnp.concatenate([mine, other], 1), jnp.concatenate([other, mine], 1)
    )
    return whole, others


def shards(queries, keys, values, out_weight, out_cotangent, offsets):
    rows_dev, feature = queries.shape[1:]
    cotangent = out_cotangent[0]
    n3 = rows_dev // 4
    far, near, mid = pick(offsets, keys, values)
    fars = [far] + [swap(far, bits) for bits in (1, 2, 3)]
    cross = swap(jnp.concatenate(fars, axis=0), 4)
    near_pair, mid2, mid3 = swap(near, 1), swap(mid, 2), swap(mid, 3)
    grads = jnp.dot(cotangent, out_weight, preferred_element_type=F32).astype(BF16)
    gathered = [near_pair, mid2, mid3] + fars + [cross]
    own_parts = attend_own(GROUPS[0], queries, keys, values, near, mid, far)
    results = attend_both(GROUPS[0], queries, keys, values, grads, near, mid, gathered, own_parts)
    attended, query_grad, local, own1, own2, far_grad, back = results[:7]
    cross_back = swap(back, 4)
    back1, back2, back3 = [swap(block, bits) for bits, block in zip((1, 2, 3), results[7:])]
    mixed = lax.dot_general(
        attended, out_weight, (((1,), (1,)), ((), ())), preferred_element_type=F32
    ).astype(BF16)
    share, sent = plane_share(cotangent, attended)
    share, (mixed,) = after(share, [mixed])
    far_grad, (back2, back3) = after(far_grad, [back2, back3])
    far_grad = (far_grad.astype(F32) + cross_back.astype(F32)).astype(BF16)
    far_parts = [far_grad[bits * n3 : (bits + 1) * n3] for bits in range(4)]
    rows, half = share.shape[0] // RUN, share.shape[1]
    place = lax.axis_index("seq") % RUN
    share_parts = [lax.dynamic_slice_in_dim(share, (place ^ bits) * rows, rows, 0) for bits in range(4)]
    total = share_parts[0].astype(F32)
    far_back = []
    for bits in (1, 2, 3):
        padded = jnp.pad(share_parts[bits], ((0, -rows % 16), (0, feature - half)))
        arrived = swap(jnp.concatenate([far_parts[bits], padded], axis=0), bits)
        far_back.append(arrived)
        total = total + arrived[n3 : n3 + rows, :half].astype(F32)
    tiles = lax.axis_size("dp") * lax.axis_size("seq") * rows_dev
    local = local.reshape(2, rows_dev, feature)
    base = spread(
        offsets,
        (local, local),
        ((0, ((own1, 0), (back1, 0))), (1, ((own2, 0), (back1, rows_dev), (back2, 0), (back3, 0)))),
        F32,
    )
    total, base = after(total.astype(BF16), base)
    key_grad, value_grad = spread(
        offsets, base, ((2, tuple((block, 0) for block in [far_grad] + far_back)),), BF16
    )
    weight_grad, (key_grad, value_grad) = slides_total(
        total, 1.0 / math.sqrt(tiles), [key_grad, value_grad]
    )
    return mixed[None], query_grad, key_grad, value_grad, weight_grad


def solution(mesh):
    split = P("dp", "seq", None)
    return jax.shard_map(
        shards,
        mesh=mesh,
        in_specs=(split, split, split, P(), split, P()),
        out_specs=(split, split, split, split, P("seq", None)),
        check_vma=False,
    )
```

time: 107 us -> 102 us (0.953)
  waiting for transfers between devices: 38.7 us -> 25.4 us
  Pallas kernels: 22.4 us -> 30.5 us
    ppermute x14, waiting for transfers between devices: 30 us -> 17 us  [swap(): lax.ppermute(block, 'seq', [(i, i ^ bits) for i in range(lax.axis_size('s...]
    pallas_call x1 -> x2, Pallas kernels: 16.3 us -> 21.7 us  [call(): pl.pallas_call(kernel, grid=(self.count,), in_specs=list(in_specs) + [pl....]
    pallas_call x1 -> x2, Pallas kernels: 3.38 us -> 6.21 us  [spread(): pl.pallas_call(functools.partial(spread_kernel, [(level, [start for _, st...]
  transfers between devices with their start and end apart: 18 -> 18, of which waited for: 9 -> 9; matrix products, arithmetic and copies ran while one was open for 5% -> 5% of each run, Pallas kernels for 3% -> 14%
where the time goes in v4:
time: 102 us
  starting transfers between devices  36.9 us (36%)
  Pallas kernels  30.5 us (30%)
  waiting for transfers between devices  25.4 us (25%)
  matrix products  4.2 us (4%)
  local copies, waits for them, and re-layouts  2.15 us (2%)
  other arithmetic  1.81 us (2%)
    pallas_call x2, Pallas kernels, call(): pl.pallas_call(kernel, grid=(self.count,), in_specs=list(in_specs) + [pl....  21.7 us
    ppermute x14, starting transfers between devices, swap(): lax.ppermute(block, 'seq', [(i, i ^ bits) for i in range(lax.axis_size('s...  20.4 us
    ppermute x14, waiting for transfers between devices, swap(): lax.ppermute(block, 'seq', [(i, i ^ bits) for i in range(lax.axis_size('s...  17 us
    ppermute x3, starting transfers between devices, slide_swap(): lax.ppermute(block, 'dp', [(i, i ^ bits) for i in range(lax.axis_size('dp...  9.73 us
    all_to_all x1, waiting for transfers between devices, plane_share(): lax.all_to_all(total, 'seq', 0, 0, axis_index_groups=groups, tiled=True)  7.57 us
    all_to_all x1, starting transfers between devices, plane_share(): lax.all_to_all(total, 'seq', 0, 0, axis_index_groups=groups, tiled=True)  6.76 us
    pallas_call x2, Pallas kernels, spread(): pl.pallas_call(functools.partial(spread_kernel, [(level, [start for _, st...  6.21 us
    pallas_call x1, Pallas kernels, pick(): pl.pallas_call(pick_kernel, grid=(feature // width,), in_specs=[pl.BlockS...  2.67 us
  transfers between devices with their start and end apart: 18, of which 9 were waited for; matrix products, arithmetic and copies ran while one was open for 5% of the time, Pallas kernels for 14%

profile of v4, /device:TPU:1, one launch (start us, length us, event | category | flops | bytes accessed | tf_op | source)
XLA Modules:
  0.0 101.9 jit_solution(3684262067884864109)
XLA Ops:
  0.6 2.7 %pick_rows.1 = (bf16[64,768]{1,0:T(8,128)(2,1)}, bf16[384,768]{1,0:T(8,128)(2,1)}, bf16[128,768]{1,0:T(8,128)(2,1)}) custom-call(s32[3,12]{1,0:T(4,128)} %offsets_ref.5, bf16[1,256,768]{2,1,0:T(8,128)(2,1)} %key_ref.5, bf16[1,256,768]{2,1,0:T(8,128)(2,1)} %value_ref.5), custom_call_target="tpu_custom_call" | custom-call | flops 2000000000 | bytes 2000000 | tf_op jit(solution)/shard_map/pick_rows/pallas_call | solution.py:77
  3.3 2.5 %collective-permute-start.3 = (bf16[64,768]{1,0:T(8,128)(2,1)}, bf16[64,768]{1,0:T(8,128)(2,1)S(1)}, u32[]{:S(2)}, u32[]{:S(2)}) collective-permute-start(bf16[64,768]{1,0:T(8,128)(2,1)} %get-tuple-element.38.far_ref.refs_3_), channel_id=1, source_target_pairs={{0,1},{1,0},{2,3},{3,2},{4,5},{5,4},{6,7},{7,6},{8,9},{9,8},{10,11... | collective-permute-start | bytes 294920 | tf_op jit(solution)/shard_map/ppermute | solution.py:351
  5.8 3.0 %collective-permute-start.4 = (bf16[64,768]{1,0:T(8,128)(2,1)}, bf16[64,768]{1,0:T(8,128)(2,1)S(1)}, u32[]{:S(2)}, u32[]{:S(2)}) collective-permute-start(bf16[64,768]{1,0:T(8,128)(2,1)} %get-tuple-element.38.far_ref.refs_3_), channel_id=1, source_target_pairs={{0,2},{1,3},{2,0},{3,1},{4,6},{5,7},{6,4},{7,5},{8,10},{9,11},{10,... | collective-permute-start | bytes 294920 | tf_op jit(solution)/shard_map/ppermute | solution.py:351
  9.1 2.5 %collective-permute-done.4.refs_5_ = bf16[64,768]{1,0:T(8,128)(2,1)S(1)} collective-permute-done((bf16[64,768]{1,0:T(8,128)(2,1)}, bf16[64,768]{1,0:T(8,128)(2,1)S(1)}, u32[]{:S(2)}, u32[]{:S(2)}) %collective-permute-start.4) | collective-permute-done | bytes 98336 | tf_op jit(solution)/shard_map/ppermute | solution.py:351
  11.6 3.6 %collective-permute-done.5.refs_6_ = bf16[64,768]{1,0:T(8,128)(2,1)S(1)} collective-permute-done((bf16[64,768]{1,0:T(8,128)(2,1)}, bf16[64,768]{1,0:T(8,128)(2,1)S(1)}, u32[]{:S(2)}, u32[]{:S(2)}) %collective-permute-start.5) | collective-permute-done | bytes 98336 | tf_op jit(solution)/shard_map/ppermute | solution.py:351
  17.5 3.6 %collective-permute-start.1 = (bf16[128,768]{1,0:T(8,128)(2,1)}, bf16[128,768]{1,0:T(8,128)(2,1)S(1)}, u32[]{:S(2)}, u32[]{:S(2)}) collective-permute-start(bf16[128,768]{1,0:T(8,128)(2,1)} %get-tuple-element.37.mid_ref.refs_9_), channel_id=1, source_target_pairs={{0,2},{1,3},{2,0},{3,1},{4,6},{5,7},{6,4},{7,5},{8,10},{9,11},{10,... | collective-permute-start | bytes 589832 | tf_op jit(solution)/shard_map/ppermute | solution.py:351
  22.4 7.9 %attend_own.1 = (bf16[6,480,512]{2,1,0:T(8,128)(2,1)}, f32[6,32,256]{2,1,0:T(8,128)}, f32[6,128,256]{2,1,0:T(8,128)}) custom-call(bf16[1,256,768]{2,1,0:T(8,128)(2,1)} %query_ref.3, bf16[1,256,768]{2,1,0:T(8,128)(2,1)} %key_ref.5, bf16[1,256,768]{2,1,0:T(8,128)(2,1)} %value_ref.5, bf16[384,768]{1,0:T(8,128)(2,1)} %get-tuple-element.36.near_ref, ...), custom_call_target="tpu_custom_call" | custom-call | flops 600000000 | bytes 1000000 | tf_op jit(solution)/shard_map/attend_own/pallas_call | solution.py:245
  31.6 4.9 %collective-permute-done.2.refs_2_ = bf16[128,768]{1,0:T(8,128)(2,1)} collective-permute-done((bf16[128,768]{1,0:T(8,128)(2,1)}, bf16[128,768]{1,0:T(8,128)(2,1)}, u32[]{:S(2)}, u32[]{:S(2)}) %collective-permute-start.2) | collective-permute-done | bytes 196640 | tf_op jit(solution)/shard_map/ppermute | solution.py:351
  37.5 13.7 %attend_both.1 = (bf16[256,768]{1,0:T(8,128)(2,1)}, bf16[1,256,768]{2,1,0:T(8,128)(2,1)}, f32[512,768]{1,0:T(8,128)}, f32[256,768]{1,0:T(8,128)}, f32[128,768]{1...) custom-call(bf16[1,256,768]{2,1,0:T(8,128)(2,1)} %query_ref.3, ...), custom_call_target="tpu_custom_call" | custom-call | flops 15600000000 | bytes 1000000 | tf_op jit(solution)/shard_map/attend_both/pallas_call | solution.py:245
  51.2 1.3 %fusion.2 = bf16[768,384]{0,1:T(8,128)(2,1)S(1)} fusion(bf16[1,256,768]{2,1,0:T(8,128)(2,1)S(1)} %copy-done.1, bf16[256,768]{1,0:T(8,128)(2,1)} %get-tuple-element.42, s32[]{:T(128)S(6)} %select_n.41), kind=kOutput, calls=%fused_computation.4 | convolution fusion | flops 151289856 | bytes 1179652 | tf_op jit(solution)/shard_map/dot_general | solution.py:369
  52.6 1.6 %collective-permute-start.7 = (bf16[768,384]{0,1:T(8,128)(2,1)S(1)}, bf16[768,384]{0,1:T(8,128)(2,1)S(1)}, u32[]{:S(2)}, u32[]{:S(2)}) collective-permute-start(bf16[768,384]{0,1:T(8,128)(2,1)S(1)} %fusion.2), channel_id=1, source_target_pairs={{0,64},{64,0},{128,192},{192,128},{1,65},{65,1},{129,193},{193,129... | collective-permute-start | bytes 1769480 | tf_op jit(solution)/shard_map/ppermute | solution.py:355
  54.2 2.4 %collective-permute-start.8 = (bf16[128,768]{1,0:T(8,128)(2,1)}, bf16[128,768]{1,0:T(8,128)(2,1)}, u32[]{:S(2)}, u32[]{:S(2)}) collective-permute-start(bf16[128,768]{1,0:T(8,128)(2,1)} %get-tuple-element.47), channel_id=1, source_target_pairs={{0,2},{1,3},{2,0},{3,1},{4,6},{5,7},{6,4},{7,5},{8,10},{9,11},{10,... | collective-permute-start | bytes 589832 | tf_op jit(solution)/shard_map/ppermute | solution.py:351
  56.6 2.0 %collective-permute-start.9 = (bf16[128,768]{1,0:T(8,128)(2,1)}, bf16[128,768]{1,0:T(8,128)(2,1)}, u32[]{:S(2)}, u32[]{:S(2)}) collective-permute-start(bf16[128,768]{1,0:T(8,128)(2,1)} %get-tuple-element.48), channel_id=1, source_target_pairs={{0,3},{1,2},{2,1},{3,0},{4,7},{5,6},{6,5},{7,4},{8,11},{9,10},{10,... | collective-permute-start | bytes 589832 | tf_op jit(solution)/shard_map/ppermute | solution.py:351
  60.2 6.8 %all-to-all-start = ((bf16[16,48,384]{2,1,0:T(8,128)(2,1)}), bf16[16,48,384]{2,1,0:T(8,128)(2,1)S(1)}, u32[]{:S(2)}, u32[]{:S(2)}) async-start(bf16[16,48,384]{2,1,0:T(8,128)(2,1)} %bitcast.3), calls=%async_computation | async-start | bytes 1179648 | tf_op jit(solution)/shard_map/all_to_all | solution.py:375
  68.2 2.0 %collective-permute-done.8.refs_4_ = bf16[128,768]{1,0:T(8,128)(2,1)} collective-permute-done((bf16[128,768]{1,0:T(8,128)(2,1)}, bf16[128,768]{1,0:T(8,128)(2,1)}, u32[]{:S(2)}, u32[]{:S(2)}) %collective-permute-start.8) | collective-permute-done | bytes 196640 | tf_op jit(solution)/shard_map/ppermute | solution.py:351
  70.4 7.6 %all-to-all-done = bf16[16,48,384]{2,1,0:T(8,128)(2,1)S(1)} async-done(((bf16[16,48,384]{2,1,0:T(8,128)(2,1)}), bf16[16,48,384]{2,1,0:T(8,128)(2,1)S(1)}, u32[]{:S(2)}, u32[]{:S(2)}) %all-to-all-start) | async-done | bytes 589856 | tf_op jit(solution)/shard_map/all_to_all | solution.py:375
  78.4 1.6 %collective-permute-start.12 = (bf16[80,768]{1,0:T(8,128)(2,1)S(1)}, bf16[80,768]{1,0:T(8,128)(2,1)S(1)}, u32[]{:S(2)}, u32[]{:S(2)}) collective-permute-start(bf16[80,768]{1,0:T(8,128)(2,1)S(1)} %fusion.12), channel_id=1, source_target_pairs={{0,2},{1,3},{2,0},{3,1},{4,6},{5,7},{6,4},{7,5},{8,10},{9,11},{10,... | collective-permute-start | bytes 368648 | tf_op jit(solution)/shard_map/ppermute | solution.py:351
  80.0 2.1 %collective-permute-start.13 = (bf16[80,768]{1,0:T(8,128)(2,1)S(1)}, bf16[80,768]{1,0:T(8,128)(2,1)S(1)}, u32[]{:S(2)}, u32[]{:S(2)}) collective-permute-start(bf16[80,768]{1,0:T(8,128)(2,1)S(1)} %fusion.13), channel_id=1, source_target_pairs={{0,3},{1,2},{2,1},{3,0},{4,7},{5,6},{6,5},{7,4},{8,11},{9,10},{10,... | collective-permute-start | bytes 368648 | tf_op jit(solution)/shard_map/ppermute | solution.py:351
  82.2 3.5 %spread_rows.2 = (f32[1,256,768]{2,1,0:T(8,128)}, f32[1,256,768]{2,1,0:T(8,128)}) custom-call(s32[3,12]{1,0:T(4,128)} %offsets_ref.5, f32[2,256,768]{2,1,0:T(8,128)} %bitcast.22, f32[2,256,768]{2,1,0:T(8,128)} %bitcast.23, f32[256,768]{1,0:T(8,128)} %get-tuple-element.52.refs_0_, bf16[384,768]{1,0:T(8,128)(2,1)} %collective-permute-done.14.refs_1_.refs_3_, ...), custom_call_target="tpu_custom_call" | custom-call | flops 2000000000 | bytes 4000000 | tf_op jit(solution)/shard_map/spread_rows/pallas_call | solution.py:333
  85.7 1.5 %collective-permute-done.11.refs_1_ = bf16[80,768]{1,0:T(8,128)(2,1)S(1)} collective-permute-done((bf16[80,768]{1,0:T(8,128)(2,1)S(1)}, bf16[80,768]{1,0:T(8,128)(2,1)S(1)}, u32[]{:S(2)}, u32[]{:S(2)}) %collective-permute-start.11) | collective-permute-done | bytes 122912 | tf_op jit(solution)/shard_map/ppermute | solution.py:351
  87.1 2.4 %collective-permute-done.13.refs_3_ = bf16[80,768]{1,0:T(8,128)(2,1)S(1)} collective-permute-done((bf16[80,768]{1,0:T(8,128)(2,1)S(1)}, bf16[80,768]{1,0:T(8,128)(2,1)S(1)}, u32[]{:S(2)}, u32[]{:S(2)}) %collective-permute-start.13) | collective-permute-done | bytes 122912 | tf_op jit(solution)/shard_map/ppermute | solution.py:351
  89.6 5.4 %collective-permute-start.15 = (bf16[12,384]{1,0:T(8,128)(2,1)S(1)}, bf16[12,384]{1,0:T(8,128)(2,1)S(1)}, u32[]{:S(2)}, u32[]{:S(2)}) collective-permute-start(bf16[12,384]{1,0:T(8,128)(2,1)S(1)} %add_convert_fusion.1), channel_id=1, source_target_pairs={{0,128},{64,192},{128,0},{192,64},{1,129},{65,193},{129,1},{193,65... | collective-permute-start | bytes 27656 | tf_op jit(solution)/shard_map/ppermute | solution.py:355
  95.0 2.7 %spread_rows.3 = (bf16[1,256,768]{2,1,0:T(8,128)(2,1)}, bf16[1,256,768]{2,1,0:T(8,128)(2,1)}) custom-call(s32[3,12]{1,0:T(4,128)} %offsets_ref.5, f32[1,256,768]{2,1,0:T(8,128)} %get-tuple-element.60.key_base_ref, f32[1,256,768]{2,1,0:T(8,128)} %get-tuple-element.61.value_base_ref, bf16[256,768]{1,0:T(8,128)(2,1)} %copy-done.3, bf16[80,768]{1,0:T(8,128)(2,1)} %copy-done.8, ...), custom_call_target="tpu_custom_call" | custom-call | flops 2000000000 | bytes 4000000 | tf_op jit(solution)/shard_map/spread_rows/pallas_call | solution.py:333
  97.8 2.7 %collective-permute-start.16 = (bf16[12,384]{1,0:T(8,128)(2,1)S(1)}, bf16[12,384]{1,0:T(8,128)(2,1)S(1)}, u32[]{:S(2)}, u32[]{:S(2)}) collective-permute-start(bf16[12,384]{1,0:T(8,128)(2,1)S(1)} %multiply_convert_fusion), channel_id=1, source_target_pairs={{0,64},{64,0},{128,192},{192,128},{1,65},{65,1},{129,193},{193,129... | collective-permute-start | bytes 27656 | tf_op jit(solution)/shard_map/ppermute | solution.py:355
  (63 shorter events, 11.0 us)
Async XLA Ops:
  0.6 29.7 %copy-start = (bf16[768,768]{1,0:T(8,128)(2,1)S(1)}, bf16[768,768]{1,0:T(8,128)(2,1)}, u32[]{:S(2)}) copy-start(bf16[768,768]{1,0:T(8,128)(2,1)} %param.9) | copy-start | bytes 3538948
  3.3 5.7 %collective-permute-start.3 = (bf16[64,768]{1,0:T(8,128)(2,1)}, bf16[64,768]{1,0:T(8,128)(2,1)S(1)}, u32[]{:S(2)}, u32[]{:S(2)}) collective-permute-start(bf16[64,768]{1,0:T(8,128)(2,1)} %get-tuple-element.38.far_ref.refs_3_), channel_id=1, source_target_pairs={{0,1},{1,0},{2,3},{3,2},{4,5},{5,4},{6,7},{7,6},{8,9},{9,8},{10,11... | collective-permute-start | bytes 294920 | tf_op jit(solution)/shard_map/ppermute | solution.py:351
  5.8 5.8 %collective-permute-start.4 = (bf16[64,768]{1,0:T(8,128)(2,1)}, bf16[64,768]{1,0:T(8,128)(2,1)S(1)}, u32[]{:S(2)}, u32[]{:S(2)}) collective-permute-start(bf16[64,768]{1,0:T(8,128)(2,1)} %get-tuple-element.38.far_ref.refs_3_), channel_id=1, source_target_pairs={{0,2},{1,3},{2,0},{3,1},{4,6},{5,7},{6,4},{7,5},{8,10},{9,11},{10,... | collective-permute-start | bytes 294920 | tf_op jit(solution)/shard_map/ppermute | solution.py:351
  8.8 6.5 %collective-permute-start.5 = (bf16[64,768]{1,0:T(8,128)(2,1)}, bf16[64,768]{1,0:T(8,128)(2,1)S(1)}, u32[]{:S(2)}, u32[]{:S(2)}) collective-permute-start(bf16[64,768]{1,0:T(8,128)(2,1)} %get-tuple-element.38.far_ref.refs_3_), channel_id=1, source_target_pairs={{0,3},{1,2},{2,1},{3,0},{4,7},{5,6},{6,5},{7,4},{8,11},{9,10},{10,... | collective-permute-start | bytes 294920 | tf_op jit(solution)/shard_map/ppermute | solution.py:351
  8.8 27.7 %collective-permute-start = (bf16[384,768]{1,0:T(8,128)(2,1)}, bf16[384,768]{1,0:T(8,128)(2,1)S(1)}, u32[]{:S(2)}, u32[]{:S(2)}) collective-permute-start(bf16[384,768]{1,0:T(8,128)(2,1)} %get-tuple-element.36.near_ref), channel_id=1, source_target_pairs={{0,1},{1,0},{2,3},{3,2},{4,5},{5,4},{6,7},{7,6},{8,9},{9,8},{10,11... | collective-permute-start | bytes 1769480 | tf_op jit(solution)/shard_map/ppermute | solution.py:351
  9.1 21.3 %copy-start.5 = (bf16[64,768]{1,0:T(8,128)(2,1)}, bf16[64,768]{1,0:T(8,128)(2,1)S(1)}, u32[]{:S(2)}) copy-start(bf16[64,768]{1,0:T(8,128)(2,1)S(1)} %collective-permute-done.3.refs_4_) | copy-start | bytes 294916
  11.6 18.7 %copy-start.6 = (bf16[64,768]{1,0:T(8,128)(2,1)}, bf16[64,768]{1,0:T(8,128)(2,1)S(1)}, u32[]{:S(2)}) copy-start(bf16[64,768]{1,0:T(8,128)(2,1)S(1)} %collective-permute-done.4.refs_5_) | copy-start | bytes 294916
  15.3 15.1 %copy-start.7 = (bf16[64,768]{1,0:T(8,128)(2,1)}, bf16[64,768]{1,0:T(8,128)(2,1)S(1)}, u32[]{:S(2)}) copy-start(bf16[64,768]{1,0:T(8,128)(2,1)S(1)} %collective-permute-done.5.refs_6_) | copy-start | bytes 294916
  16.2 14.1 %copy-start.1 = (bf16[1,256,768]{2,1,0:T(8,128)(2,1)S(1)}, bf16[1,256,768]{2,1,0:T(8,128)(2,1)}, u32[]{:S(2)}) copy-start(bf16[1,256,768]{2,1,0:T(8,128)(2,1)} %param.10) | copy-start | bytes 1179652
  16.2 20.2 %collective-permute-start.6 = (bf16[256,768]{1,0:T(8,128)(2,1)S(1)}, bf16[256,768]{1,0:T(8,128)(2,1)S(1)}, u32[]{:S(2)}, u32[]{:S(2)}) collective-permute-start(bf16[256,768]{1,0:T(8,128)(2,1)S(1)} %pad_maximum_fusion), channel_id=1, source_target_pairs={{0,4},{1,5},{2,6},{3,7},{4,0},{5,1},{6,2},{7,3},{8,12},{9,13},{10,... | collective-permute-start | bytes 1179656 | tf_op jit(solution)/shard_map/ppermute | solution.py:351
  17.5 14.1 %collective-permute-start.1 = (bf16[128,768]{1,0:T(8,128)(2,1)}, bf16[128,768]{1,0:T(8,128)(2,1)S(1)}, u32[]{:S(2)}, u32[]{:S(2)}) collective-permute-start(bf16[128,768]{1,0:T(8,128)(2,1)} %get-tuple-element.37.mid_ref.refs_9_), channel_id=1, source_target_pairs={{0,2},{1,3},{2,0},{3,1},{4,6},{5,7},{6,4},{7,5},{8,10},{9,11},{10,... | collective-permute-start | bytes 589832 | tf_op jit(solution)/shard_map/ppermute | solution.py:351
  21.1 15.4 %collective-permute-start.2 = (bf16[128,768]{1,0:T(8,128)(2,1)}, bf16[128,768]{1,0:T(8,128)(2,1)}, u32[]{:S(2)}, u32[]{:S(2)}) collective-permute-start(bf16[128,768]{1,0:T(8,128)(2,1)} %get-tuple-element.37.mid_ref.refs_9_), channel_id=1, source_target_pairs={{0,3},{1,2},{2,1},{3,0},{4,7},{5,6},{6,5},{7,4},{8,11},{9,10},{10,... | collective-permute-start | bytes 589832 | tf_op jit(solution)/shard_map/ppermute | solution.py:351
  52.6 6.1 %collective-permute-start.7 = (bf16[768,384]{0,1:T(8,128)(2,1)S(1)}, bf16[768,384]{0,1:T(8,128)(2,1)S(1)}, u32[]{:S(2)}, u32[]{:S(2)}) collective-permute-start(bf16[768,384]{0,1:T(8,128)(2,1)S(1)} %fusion.2), channel_id=1, source_target_pairs={{0,64},{64,0},{128,192},{192,128},{1,65},{65,1},{129,193},{193,129... | collective-permute-start | bytes 1769480 | tf_op jit(solution)/shard_map/ppermute | solution.py:355
  54.2 16.0 %collective-permute-start.8 = (bf16[128,768]{1,0:T(8,128)(2,1)}, bf16[128,768]{1,0:T(8,128)(2,1)}, u32[]{:S(2)}, u32[]{:S(2)}) collective-permute-start(bf16[128,768]{1,0:T(8,128)(2,1)} %get-tuple-element.47), channel_id=1, source_target_pairs={{0,2},{1,3},{2,0},{3,1},{4,6},{5,7},{6,4},{7,5},{8,10},{9,11},{10,... | collective-permute-start | bytes 589832 | tf_op jit(solution)/shard_map/ppermute | solution.py:351
  56.6 13.6 %collective-permute-start.9 = (bf16[128,768]{1,0:T(8,128)(2,1)}, bf16[128,768]{1,0:T(8,128)(2,1)}, u32[]{:S(2)}, u32[]{:S(2)}) collective-permute-start(bf16[128,768]{1,0:T(8,128)(2,1)} %get-tuple-element.48), channel_id=1, source_target_pairs={{0,3},{1,2},{2,1},{3,0},{4,7},{5,6},{6,5},{7,4},{8,11},{9,10},{10,... | collective-permute-start | bytes 589832 | tf_op jit(solution)/shard_map/ppermute | solution.py:351
  58.6 11.7 %collective-permute-start.10 = (bf16[256,768]{1,0:T(8,128)(2,1)}, bf16[256,768]{1,0:T(8,128)(2,1)S(1)}, u32[]{:S(2)}, u32[]{:S(2)}) collective-permute-start(bf16[256,768]{1,0:T(8,128)(2,1)} %get-tuple-element.50), channel_id=1, source_target_pairs={{0,4},{1,5},{2,6},{3,7},{4,0},{5,1},{6,2},{7,3},{8,12},{9,13},{10,... | collective-permute-start | bytes 1179656 | tf_op jit(solution)/shard_map/ppermute | solution.py:351
  60.2 17.7 %all-to-all-start = ((bf16[16,48,384]{2,1,0:T(8,128)(2,1)}), bf16[16,48,384]{2,1,0:T(8,128)(2,1)S(1)}, u32[]{:S(2)}, u32[]{:S(2)}) async-start(bf16[16,48,384]{2,1,0:T(8,128)(2,1)} %bitcast.3), calls=%async_computation | async-start | bytes 1179648 | tf_op jit(solution)/shard_map/all_to_all | solution.py:375
  68.2 13.9 %collective-permute-start.14 = (bf16[384,768]{1,0:T(8,128)(2,1)S(1)}, bf16[384,768]{1,0:T(8,128)(2,1)}, u32[]{:S(2)}, u32[]{:S(2)}) collective-permute-start(bf16[384,768]{1,0:T(8,128)(2,1)S(1)} %copy-done.11), channel_id=1, source_target_pairs={{0,1},{1,0},{2,3},{3,2},{4,5},{5,4},{6,7},{7,6},{8,9},{9,8},{10,11... | collective-permute-start | bytes 1769480 | tf_op jit(solution)/shard_map/ppermute | solution.py:351
  70.3 15.3 %copy-start.3 = (bf16[256,768]{1,0:T(8,128)(2,1)}, bf16[256,768]{1,0:T(8,128)(2,1)S(1)}, u32[]{:S(2)}) copy-start(bf16[256,768]{1,0:T(8,128)(2,1)S(1)} %add_convert_fusion.refs_0_) | copy-start | bytes 1179652
  78.1 9.0 %collective-permute-start.11 = (bf16[80,768]{1,0:T(8,128)(2,1)S(1)}, bf16[80,768]{1,0:T(8,128)(2,1)S(1)}, u32[]{:S(2)}, u32[]{:S(2)}) collective-permute-start(bf16[80,768]{1,0:T(8,128)(2,1)S(1)} %fusion.11), channel_id=1, source_target_pairs={{0,1},{1,0},{2,3},{3,2},{4,5},{5,4},{6,7},{7,6},{8,9},{9,8},{10,11... | collective-permute-start | bytes 368648 | tf_op jit(solution)/shard_map/ppermute | solution.py:351
  78.4 8.7 %collective-permute-start.12 = (bf16[80,768]{1,0:T(8,128)(2,1)S(1)}, bf16[80,768]{1,0:T(8,128)(2,1)S(1)}, u32[]{:S(2)}, u32[]{:S(2)}) collective-permute-start(bf16[80,768]{1,0:T(8,128)(2,1)S(1)} %fusion.12), channel_id=1, source_target_pairs={{0,2},{1,3},{2,0},{3,1},{4,6},{5,7},{6,4},{7,5},{8,10},{9,11},{10,... | collective-permute-start | bytes 368648 | tf_op jit(solution)/shard_map/ppermute | solution.py:351
  80.0 9.6 %collective-permute-start.13 = (bf16[80,768]{1,0:T(8,128)(2,1)S(1)}, bf16[80,768]{1,0:T(8,128)(2,1)S(1)}, u32[]{:S(2)}, u32[]{:S(2)}) collective-permute-start(bf16[80,768]{1,0:T(8,128)(2,1)S(1)} %fusion.13), channel_id=1, source_target_pairs={{0,3},{1,2},{2,1},{3,0},{4,7},{5,6},{6,5},{7,4},{8,11},{9,10},{10,... | collective-permute-start | bytes 368648 | tf_op jit(solution)/shard_map/ppermute | solution.py:351
  89.6 8.2 %collective-permute-start.15 = (bf16[12,384]{1,0:T(8,128)(2,1)S(1)}, bf16[12,384]{1,0:T(8,128)(2,1)S(1)}, u32[]{:S(2)}, u32[]{:S(2)}) collective-permute-start(bf16[12,384]{1,0:T(8,128)(2,1)S(1)} %add_convert_fusion.1), channel_id=1, source_target_pairs={{0,128},{64,192},{128,0},{192,64},{1,129},{65,193},{129,1},{193,65... | collective-permute-start | bytes 27656 | tf_op jit(solution)/shard_map/ppermute | solution.py:355
  97.8 3.5 %collective-permute-start.16 = (bf16[12,384]{1,0:T(8,128)(2,1)S(1)}, bf16[12,384]{1,0:T(8,128)(2,1)S(1)}, u32[]{:S(2)}, u32[]{:S(2)}) collective-permute-start(bf16[12,384]{1,0:T(8,128)(2,1)S(1)} %multiply_convert_fusion), channel_id=1, source_target_pairs={{0,64},{64,0},{128,192},{192,128},{1,65},{65,1},{129,193},{193,129... | collective-permute-start | bytes 27656 | tf_op jit(solution)/shard_map/ppermute | solution.py:355
  (9 other events, 40.0 us)

commit v5 on v4

--- a/solution.py
+++ b/solution.py
@@ -175,18 +175,15 @@
     grad_t = grad_ref[...].T.astype(F32)
     own_raw = own_raw_ref[0]
     raws = [(own_raw[:, side * rows_dev : (side + 1) * rows_dev], raw[side]) for side in range(2)]
-    deltas = [
-        jnp.sum(grad_t[head_rows(side)] * attended_t[side].astype(F32), axis=0, keepdims=True) for side in range(2)
-    ]
     score_grads = [[], []]
     value_sums = []
     for part, values in enumerate((value_set[:own], value_set[own:])):
-        normed = [grad_t[head_rows(side)] * scales[side][part] for side in range(2)]
-        grad_sides = sides(jnp.concatenate(normed, axis=0).astype(BF16).T)
+        normed = [(grad_t[head_rows(side)] * scales[side][part]).astype(BF16) for side in range(2)]
+        grad_sides = sides(jnp.concatenate(normed, axis=0).T)
         for side in range(2):
             prob_grad = scores_of(values, grad_sides[side])
-            difference = prob_grad - deltas[side] * scales[side][part]
-            score_grads[side].append((raws[side][part].astype(F32) * difference).astype(BF16))
+            delta = jnp.sum(normed[side].astype(F32) * attended_t[side].astype(F32), axis=0, keepdims=True)
+            score_grads[side].append((raws[side][part].astype(F32) * (prob_grad - delta)).astype(BF16))
         pair = own_raw if part == 0 else jnp.concatenate(raw, axis=1)
         value_sums.append(jnp.dot(pair, jnp.concatenate(grad_sides, axis=0), preferred_element_type=F32))
     value_sum = jnp.concatenate(value_sums, axis=0)
@@ -295,13 +292,10 @@
         head = 2 * (SPREAD_PAIRS * pl.program_id(0) + pair)
         at = lanes(pair)
         key_rows, value_rows, used = [], [], 0
-        for level, starts in levels:
+        for level, blocks in levels:
             count = rows_dev >> (level + 1)
-            total = sum(
-                ref[start : start + 2 * count, at].astype(F32)
-                for ref, start in zip(refs[used : used + len(starts)], starts)
-            )
-            used += len(starts)
+            total = sum(ref[:, at].astype(F32) for ref in refs[used : used + blocks])
+            used += blocks
             key_rows.append(total[:count])
             value_rows.append(total[count:])
         both = jnp.concatenate(
@@ -327,18 +321,23 @@
     key_base, value_base = base
     rows_dev, feature = key_base.shape[1:]
     width = SPREAD_PAIRS * PAIR
-    blocks = [block for _, parts in levels for block, _ in parts]
+    blocks, specs = [], []
+    for level, parts in levels:
+        rows = 2 * (rows_dev >> (level + 1))
+        for block, start in parts:
+            blocks.append(block)
+            specs.append(pl.BlockSpec((rows, width), functools.partial(lambda first, i: (first, i), start // rows)))
     out = pl.BlockSpec((1, rows_dev, width), lambda i: (0, 0, i))
     shape = jax.ShapeDtypeStruct((1, rows_dev, feature), kind)
     return pl.pallas_call(
-        functools.partial(spread_kernel, [(level, [start for _, start in parts]) for level, parts in levels]),
+        functools.partial(spread_kernel, [(level, len(parts)) for level, parts in levels]),
         grid=(feature // width,),
         in_specs=[
             pl.BlockSpec(memory_space=pltpu.SMEM),
             pl.BlockSpec((1, rows_dev, width), lambda i: (0, 0, i)),
             pl.BlockSpec((1, rows_dev, width), lambda i: (int(key_base is value_base), 0, i)),
         ]
-        + [pl.BlockSpec((block.shape[0], width), lambda i: (0, i)) for block in blocks],
+        + specs,
         out_specs=[out, out],
         out_shape=[shape, shape],
         compiler_params=pltpu.CompilerParams(vmem_limit_bytes=VMEM_LIMIT),
@@ -380,9 +379,11 @@
     mine = ((share.astype(F32) + slide_swap(share, 2).astype(F32)) * norm_factor).astype(BF16)
     mine, others = after(mine, others)
     other = slide_swap(mine, 1)
-    whole = jnp.where(
-        lax.axis_index("dp") % 2 == 0, jnp.concatenate([mine, other], 1), jnp.concatenate([other, mine], 1)
-    )
+    half = mine.shape[1] // 2
+    low = lax.axis_index("dp") % 2 == 0
+    left, right = jnp.where(low, mine, other), jnp.where(low, other, mine)
+    rows = [jnp.concatenate([left[:, at], right[:, at]], axis=1) for at in (slice(0, half), slice(half, None))]
+    whole = jnp.concatenate(rows, axis=0)
     return whole, others
 
 
@@ -406,19 +407,23 @@
     ).astype(BF16)
     share, sent = plane_share(cotangent, attended)
     share, (mixed,) = after(share, [mixed])
-    far_grad, (back2, back3) = after(far_grad, [back2, back3])
+    far_grad, (back1, back2) = after(far_grad, [back1, back2])
     far_grad = (far_grad.astype(F32) + cross_back.astype(F32)).astype(BF16)
     far_parts = [far_grad[bits * n3 : (bits + 1) * n3] for bits in range(4)]
     rows, half = share.shape[0] // RUN, share.shape[1]
     place = lax.axis_index("seq") % RUN
-    share_parts = [lax.dynamic_slice_in_dim(share, (place ^ bits) * rows, rows, 0) for bits in range(4)]
+    packed = rows // 2
+    share_parts = []
+    for bits in range(4):
+        part = lax.dynamic_slice_in_dim(share, (place ^ bits) * rows, rows, 0)
+        share_parts.append(jnp.concatenate([part[:packed], part[packed:]], axis=1))
     total = share_parts[0].astype(F32)
     far_back = []
     for bits in (1, 2, 3):
-        padded = jnp.pad(share_parts[bits], ((0, -rows % 16), (0, feature - half)))
+        padded = jnp.pad(share_parts[bits], ((0, -packed % 8), (0, feature - 2 * half)))
         arrived = swap(jnp.concatenate([far_parts[bits], padded], axis=0), bits)
         far_back.append(arrived)
-        total = total + arrived[n3 : n3 + rows, :half].astype(F32)
+        total = total + arrived[n3 : n3 + packed, : 2 * half].astype(F32)
     tiles = lax.axis_size("dp") * lax.axis_size("seq") * rows_dev
     local = local.reshape(2, rows_dev, feature)
     base = spread(

time: 102 us -> 102 us (level)
    all_to_all x1, waiting for transfers between devices: 7.57 us -> 1.41 us  [plane_share(): lax.all_to_all(total, 'seq', 0, 0, axis_index_groups=groups, tiled=True)]
    ppermute x14, waiting for transfers between devices: 17 us -> 22.5 us  [swap(): lax.ppermute(block, 'seq', [(i, i ^ bits) for i in range(lax.axis_size('s...]
  transfers between devices with their start and end apart: 18 -> 18, of which waited for: 9 -> 8; matrix products, arithmetic and copies ran while one was open for 5% -> 5% of each run, Pallas kernels for 14% -> 14%
where the time goes in v5:
time: 102 us; the launch traced here: 101 us
  starting transfers between devices  37.2 us (36%)
  Pallas kernels  30.2 us (30%)
  waiting for transfers between devices  24.7 us (24%)
  matrix products  4.19 us (4%)
  local copies, waits for them, and re-layouts  2.21 us (2%)
  other arithmetic  1.84 us (2%)
    ppermute x14, waiting for transfers between devices, swap(): lax.ppermute(block, 'seq', [(i, i ^ bits) for i in range(lax.axis_size('s...  22.5 us
    pallas_call x2, Pallas kernels, call(): pl.pallas_call(kernel, grid=(self.count,), in_specs=list(in_specs) + [pl....  21.5 us
    ppermute x14, starting transfers between devices, swap(): lax.ppermute(block, 'seq', [(i, i ^ bits) for i in range(lax.axis_size('s...  20.8 us
    ppermute x3, starting transfers between devices, slide_swap(): lax.ppermute(block, 'dp', [(i, i ^ bits) for i in range(lax.axis_size('dp...  10 us
    all_to_all x1, starting transfers between devices, plane_share(): lax.all_to_all(total, 'seq', 0, 0, axis_index_groups=groups, tiled=True)  6.47 us
    pallas_call x2, Pallas kernels, spread(): pl.pallas_call(functools.partial(spread_kernel, [(level, len(parts)) for...  6.03 us
    pallas_call x1, Pallas kernels, pick(): pl.pallas_call(pick_kernel, grid=(feature // width,), in_specs=[pl.BlockS...  2.67 us
  transfers between devices with their start and end apart: 18, of which 8 were waited for; matrix products, arithmetic and copies ran while one was open for 5% of the time, Pallas kernels for 14%

profile of v5, /device:TPU:1, one launch (start us, length us, event | category | flops | bytes accessed | tf_op | source)
XLA Modules:
  0.0 101.3 jit_solution(13034800294665643642)
XLA Ops:
  0.6 2.7 %pick_rows.1 = (bf16[64,768]{1,0:T(8,128)(2,1)}, bf16[384,768]{1,0:T(8,128)(2,1)}, bf16[128,768]{1,0:T(8,128)(2,1)}) custom-call(s32[3,12]{1,0:T(4,128)} %offsets_ref.5, bf16[1,256,768]{2,1,0:T(8,128)(2,1)} %key_ref.5, bf16[1,256,768]{2,1,0:T(8,128)(2,1)} %value_ref.5), custom_call_target="tpu_custom_call" | custom-call | flops 2000000000 | bytes 2000000 | tf_op jit(solution)/shard_map/pick_rows/pallas_call | solution.py:77
  3.3 2.5 %collective-permute-start.3 = (bf16[64,768]{1,0:T(8,128)(2,1)}, bf16[64,768]{1,0:T(8,128)(2,1)S(1)}, u32[]{:S(2)}, u32[]{:S(2)}) collective-permute-start(bf16[64,768]{1,0:T(8,128)(2,1)} %get-tuple-element.38.far_ref.refs_3_), channel_id=1, source_target_pairs={{0,1},{1,0},{2,3},{3,2},{4,5},{5,4},{6,7},{7,6},{8,9},{9,8},{10,11... | collective-permute-start | bytes 294920 | tf_op jit(solution)/shard_map/ppermute | solution.py:350
  5.8 3.0 %collective-permute-start.4 = (bf16[64,768]{1,0:T(8,128)(2,1)}, bf16[64,768]{1,0:T(8,128)(2,1)S(1)}, u32[]{:S(2)}, u32[]{:S(2)}) collective-permute-start(bf16[64,768]{1,0:T(8,128)(2,1)} %get-tuple-element.38.far_ref.refs_3_), channel_id=1, source_target_pairs={{0,2},{1,3},{2,0},{3,1},{4,6},{5,7},{6,4},{7,5},{8,10},{9,11},{10,... | collective-permute-start | bytes 294920 | tf_op jit(solution)/shard_map/ppermute | solution.py:350
  9.1 2.5 %collective-permute-done.4.refs_5_ = bf16[64,768]{1,0:T(8,128)(2,1)S(1)} collective-permute-done((bf16[64,768]{1,0:T(8,128)(2,1)}, bf16[64,768]{1,0:T(8,128)(2,1)S(1)}, u32[]{:S(2)}, u32[]{:S(2)}) %collective-permute-start.4) | collective-permute-done | bytes 98336 | tf_op jit(solution)/shard_map/ppermute | solution.py:350
  11.6 3.6 %collective-permute-done.5.refs_6_ = bf16[64,768]{1,0:T(8,128)(2,1)S(1)} collective-permute-done((bf16[64,768]{1,0:T(8,128)(2,1)}, bf16[64,768]{1,0:T(8,128)(2,1)S(1)}, u32[]{:S(2)}, u32[]{:S(2)}) %collective-permute-start.5) | collective-permute-done | bytes 98336 | tf_op jit(solution)/shard_map/ppermute | solution.py:350
  17.5 3.6 %collective-permute-start.1 = (bf16[128,768]{1,0:T(8,128)(2,1)}, bf16[128,768]{1,0:T(8,128)(2,1)S(1)}, u32[]{:S(2)}, u32[]{:S(2)}) collective-permute-start(bf16[128,768]{1,0:T(8,128)(2,1)} %get-tuple-element.37.mid_ref.refs_9_), channel_id=1, source_target_pairs={{0,2},{1,3},{2,0},{3,1},{4,6},{5,7},{6,4},{7,5},{8,10},{9,11},{10,... | collective-permute-start | bytes 589832 | tf_op jit(solution)/shard_map/ppermute | solution.py:350
  21.1 1.3 %collective-permute-start.2 = (bf16[128,768]{1,0:T(8,128)(2,1)}, bf16[128,768]{1,0:T(8,128)(2,1)}, u32[]{:S(2)}, u32[]{:S(2)}) collective-permute-start(bf16[128,768]{1,0:T(8,128)(2,1)} %get-tuple-element.37.mid_ref.refs_9_), channel_id=1, source_target_pairs={{0,3},{1,2},{2,1},{3,0},{4,7},{5,6},{6,5},{7,4},{8,11},{9,10},{10,... | collective-permute-start | bytes 589832 | tf_op jit(solution)/shard_map/ppermute | solution.py:350
  22.4 7.9 %attend_own.1 = (bf16[6,480,512]{2,1,0:T(8,128)(2,1)}, f32[6,32,256]{2,1,0:T(8,128)}, f32[6,128,256]{2,1,0:T(8,128)}) custom-call(bf16[1,256,768]{2,1,0:T(8,128)(2,1)} %query_ref.3, bf16[1,256,768]{2,1,0:T(8,128)(2,1)} %key_ref.5, bf16[1,256,768]{2,1,0:T(8,128)(2,1)} %value_ref.5, bf16[384,768]{1,0:T(8,128)(2,1)} %get-tuple-element.36.near_ref, ...), custom_call_target="tpu_custom_call" | custom-call | flops 600000000 | bytes 1000000 | tf_op jit(solution)/shard_map/attend_own/pallas_call | solution.py:242
  31.6 4.9 %collective-permute-done.2.refs_2_ = bf16[128,768]{1,0:T(8,128)(2,1)} collective-permute-done((bf16[128,768]{1,0:T(8,128)(2,1)}, bf16[128,768]{1,0:T(8,128)(2,1)}, u32[]{:S(2)}, u32[]{:S(2)}) %collective-permute-start.2) | collective-permute-done | bytes 196640 | tf_op jit(solution)/shard_map/ppermute | solution.py:350
  37.5 13.7 %attend_both.1 = (bf16[256,768]{1,0:T(8,128)(2,1)}, bf16[1,256,768]{2,1,0:T(8,128)(2,1)}, f32[512,768]{1,0:T(8,128)}, f32[256,768]{1,0:T(8,128)}, f32[128,768]{1...) custom-call(bf16[1,256,768]{2,1,0:T(8,128)(2,1)} %query_ref.3, ...), custom_call_target="tpu_custom_call" | custom-call | flops 15600000000 | bytes 1000000 | tf_op jit(solution)/shard_map/attend_both/pallas_call | solution.py:242
  51.2 1.3 %fusion.2 = bf16[768,384]{0,1:T(8,128)(2,1)S(1)} fusion(bf16[1,256,768]{2,1,0:T(8,128)(2,1)S(1)} %copy-done.1, bf16[256,768]{1,0:T(8,128)(2,1)} %get-tuple-element.42, s32[]{:T(128)S(6)} %select_n.45), kind=kOutput, calls=%fused_computation.4 | convolution fusion | flops 151289856 | bytes 1179652 | tf_op jit(solution)/shard_map/dot_general | solution.py:368
  52.5 1.6 %collective-permute-start.7 = (bf16[768,384]{0,1:T(8,128)(2,1)S(1)}, bf16[768,384]{0,1:T(8,128)(2,1)S(1)}, u32[]{:S(2)}, u32[]{:S(2)}) collective-permute-start(bf16[768,384]{0,1:T(8,128)(2,1)S(1)} %fusion.2), channel_id=1, source_target_pairs={{0,64},{64,0},{128,192},{192,128},{1,65},{65,1},{129,193},{193,129... | collective-permute-start | bytes 1769480 | tf_op jit(solution)/shard_map/ppermute | solution.py:354
  54.2 2.3 %collective-permute-start.8 = (bf16[384,768]{1,0:T(8,128)(2,1)}, bf16[384,768]{1,0:T(8,128)(2,1)}, u32[]{:S(2)}, u32[]{:S(2)}) collective-permute-start(bf16[384,768]{1,0:T(8,128)(2,1)} %get-tuple-element.47), channel_id=1, source_target_pairs={{0,1},{1,0},{2,3},{3,2},{4,5},{5,4},{6,7},{7,6},{8,9},{9,8},{10,11... | collective-permute-start | bytes 1769480 | tf_op jit(solution)/shard_map/ppermute | solution.py:350
  58.6 6.5 %all-to-all-start = ((bf16[16,48,384]{2,1,0:T(8,128)(2,1)}), bf16[16,48,384]{2,1,0:T(8,128)(2,1)S(1)}, u32[]{:S(2)}, u32[]{:S(2)}) async-start(bf16[16,48,384]{2,1,0:T(8,128)(2,1)} %bitcast.3), calls=%async_computation | async-start | bytes 1179648 | tf_op jit(solution)/shard_map/all_to_all | solution.py:374
  66.4 1.8 %collective-permute-start.14 = (bf16[128,768]{1,0:T(8,128)(2,1)S(1)}, bf16[128,768]{1,0:T(8,128)(2,1)}, u32[]{:S(2)}, u32[]{:S(2)}) collective-permute-start(bf16[128,768]{1,0:T(8,128)(2,1)S(1)} %copy-done.13), channel_id=1, source_target_pairs={{0,3},{1,2},{2,1},{3,0},{4,7},{5,6},{6,5},{7,4},{8,11},{9,10},{10,... | collective-permute-start | bytes 589832 | tf_op jit(solution)/shard_map/ppermute | solution.py:350
  68.2 5.5 %collective-permute-done.9.refs_4_ = bf16[128,768]{1,0:T(8,128)(2,1)} collective-permute-done((bf16[128,768]{1,0:T(8,128)(2,1)}, bf16[128,768]{1,0:T(8,128)(2,1)}, u32[]{:S(2)}, u32[]{:S(2)}) %collective-permute-start.9) | collective-permute-done | bytes 196640 | tf_op jit(solution)/shard_map/ppermute | solution.py:350
  74.7 1.4 %all-to-all-done = bf16[16,48,384]{2,1,0:T(8,128)(2,1)S(1)} async-done(((bf16[16,48,384]{2,1,0:T(8,128)(2,1)}), bf16[16,48,384]{2,1,0:T(8,128)(2,1)S(1)}, u32[]{:S(2)}, u32[]{:S(2)}) %all-to-all-start) | async-done | bytes 589856 | tf_op jit(solution)/shard_map/all_to_all | solution.py:374
  76.3 1.6 %collective-permute-start.11 = (bf16[72,768]{1,0:T(8,128)(2,1)S(1)}, bf16[72,768]{1,0:T(8,128)(2,1)S(1)}, u32[]{:S(2)}, u32[]{:S(2)}) collective-permute-start(bf16[72,768]{1,0:T(8,128)(2,1)S(1)} %pad_maximum_fusion.1), channel_id=1, source_target_pairs={{0,1},{1,0},{2,3},{3,2},{4,5},{5,4},{6,7},{7,6},{8,9},{9,8},{10,11... | collective-permute-start | bytes 331784 | tf_op jit(solution)/shard_map/ppermute | solution.py:350
  78.9 1.5 %collective-permute-start.13 = (bf16[72,768]{1,0:T(8,128)(2,1)S(1)}, bf16[72,768]{1,0:T(8,128)(2,1)S(1)}, u32[]{:S(2)}, u32[]{:S(2)}) collective-permute-start(bf16[72,768]{1,0:T(8,128)(2,1)S(1)} %pad_maximum_fusion.3), channel_id=1, source_target_pairs={{0,3},{1,2},{2,1},{3,0},{4,7},{5,6},{6,5},{7,4},{8,11},{9,10},{10,... | collective-permute-start | bytes 331784 | tf_op jit(solution)/shard_map/ppermute | solution.py:350
  80.4 3.4 %spread_rows.2 = (f32[1,256,768]{2,1,0:T(8,128)}, f32[1,256,768]{2,1,0:T(8,128)}) custom-call(s32[3,12]{1,0:T(4,128)} %offsets_ref.5, f32[2,256,768]{2,1,0:T(8,128)} %bitcast.22, f32[2,256,768]{2,1,0:T(8,128)} %bitcast.23, f32[256,768]{1,0:T(8,128)} %get-tuple-element.52.refs_0_, bf16[384,768]{1,0:T(8,128)(2,1)} %collective-permute-done.8.refs_1_.refs_3_, ...), custom_call_target="tpu_custom_call" | custom-call | flops 2000000000 | bytes 4000000 | tf_op jit(solution)/shard_map/spread_rows/pallas_call | solution.py:332
  83.7 5.0 %collective-permute-done.12.refs_2_ = bf16[72,768]{1,0:T(8,128)(2,1)S(1)} collective-permute-done((bf16[72,768]{1,0:T(8,128)(2,1)S(1)}, bf16[72,768]{1,0:T(8,128)(2,1)S(1)}, u32[]{:S(2)}, u32[]{:S(2)}) %collective-permute-start.12) | collective-permute-done | bytes 110624 | tf_op jit(solution)/shard_map/ppermute | solution.py:350
  88.8 5.4 %collective-permute-start.15 = (bf16[6,768]{1,0:T(8,128)(2,1)S(1)}, bf16[6,768]{1,0:T(8,128)(2,1)S(1)}, u32[]{:S(2)}, u32[]{:S(2)}) collective-permute-start(bf16[6,768]{1,0:T(8,128)(2,1)S(1)} %add_convert_fusion.1), channel_id=1, source_target_pairs={{0,128},{64,192},{128,0},{192,64},{1,129},{65,193},{129,1},{193,65... | collective-permute-start | bytes 27656 | tf_op jit(solution)/shard_map/ppermute | solution.py:354
  94.2 2.7 %spread_rows.3 = (bf16[1,256,768]{2,1,0:T(8,128)(2,1)}, bf16[1,256,768]{2,1,0:T(8,128)(2,1)}) custom-call(s32[3,12]{1,0:T(4,128)} %offsets_ref.5, f32[1,256,768]{2,1,0:T(8,128)} %get-tuple-element.60.key_base_ref, f32[1,256,768]{2,1,0:T(8,128)} %get-tuple-element.61.value_base_ref, bf16[256,768]{1,0:T(8,128)(2,1)} %copy-done.3, bf16[72,768]{1,0:T(8,128)(2,1)} %copy-done.8, ...), custom_call_target="tpu_custom_call" | custom-call | flops 2000000000 | bytes 4000000 | tf_op jit(solution)/shard_map/spread_rows/pallas_call | solution.py:332
  96.9 2.9 %collective-permute-start.16 = (bf16[6,768]{1,0:T(8,128)(2,1)S(1)}, bf16[6,768]{1,0:T(8,128)(2,1)S(1)}, u32[]{:S(2)}, u32[]{:S(2)}) collective-permute-start(bf16[6,768]{1,0:T(8,128)(2,1)S(1)} %multiply_convert_fusion), channel_id=1, source_target_pairs={{0,64},{64,0},{128,192},{192,128},{1,65},{65,1},{129,193},{193,129... | collective-permute-start | bytes 27656 | tf_op jit(solution)/shard_map/ppermute | solution.py:354
  (68 shorter events, 11.8 us)
Async XLA Ops:
  0.6 29.7 %copy-start = (bf16[768,768]{1,0:T(8,128)(2,1)S(1)}, bf16[768,768]{1,0:T(8,128)(2,1)}, u32[]{:S(2)}) copy-start(bf16[768,768]{1,0:T(8,128)(2,1)} %param.9) | copy-start | bytes 3538948
  3.3 5.7 %collective-permute-start.3 = (bf16[64,768]{1,0:T(8,128)(2,1)}, bf16[64,768]{1,0:T(8,128)(2,1)S(1)}, u32[]{:S(2)}, u32[]{:S(2)}) collective-permute-start(bf16[64,768]{1,0:T(8,128)(2,1)} %get-tuple-element.38.far_ref.refs_3_), channel_id=1, source_target_pairs={{0,1},{1,0},{2,3},{3,2},{4,5},{5,4},{6,7},{7,6},{8,9},{9,8},{10,11... | collective-permute-start | bytes 294920 | tf_op jit(solution)/shard_map/ppermute | solution.py:350
  5.8 5.8 %collective-permute-start.4 = (bf16[64,768]{1,0:T(8,128)(2,1)}, bf16[64,768]{1,0:T(8,128)(2,1)S(1)}, u32[]{:S(2)}, u32[]{:S(2)}) collective-permute-start(bf16[64,768]{1,0:T(8,128)(2,1)} %get-tuple-element.38.far_ref.refs_3_), channel_id=1, source_target_pairs={{0,2},{1,3},{2,0},{3,1},{4,6},{5,7},{6,4},{7,5},{8,10},{9,11},{10,... | collective-permute-start | bytes 294920 | tf_op jit(solution)/shard_map/ppermute | solution.py:350
  8.8 6.5 %collective-permute-start.5 = (bf16[64,768]{1,0:T(8,128)(2,1)}, bf16[64,768]{1,0:T(8,128)(2,1)S(1)}, u32[]{:S(2)}, u32[]{:S(2)}) collective-permute-start(bf16[64,768]{1,0:T(8,128)(2,1)} %get-tuple-element.38.far_ref.refs_3_), channel_id=1, source_target_pairs={{0,3},{1,2},{2,1},{3,0},{4,7},{5,6},{6,5},{7,4},{8,11},{9,10},{10,... | collective-permute-start | bytes 294920 | tf_op jit(solution)/shard_map/ppermute | solution.py:350
  8.8 27.7 %collective-permute-start = (bf16[384,768]{1,0:T(8,128)(2,1)}, bf16[384,768]{1,0:T(8,128)(2,1)S(1)}, u32[]{:S(2)}, u32[]{:S(2)}) collective-permute-start(bf16[384,768]{1,0:T(8,128)(2,1)} %get-tuple-element.36.near_ref), channel_id=1, source_target_pairs={{0,1},{1,0},{2,3},{3,2},{4,5},{5,4},{6,7},{7,6},{8,9},{9,8},{10,11... | collective-permute-start | bytes 1769480 | tf_op jit(solution)/shard_map/ppermute | solution.py:350
  9.1 21.2 %copy-start.5 = (bf16[64,768]{1,0:T(8,128)(2,1)}, bf16[64,768]{1,0:T(8,128)(2,1)S(1)}, u32[]{:S(2)}) copy-start(bf16[64,768]{1,0:T(8,128)(2,1)S(1)} %collective-permute-done.3.refs_4_) | copy-start | bytes 294916
  11.6 18.7 %copy-start.6 = (bf16[64,768]{1,0:T(8,128)(2,1)}, bf16[64,768]{1,0:T(8,128)(2,1)S(1)}, u32[]{:S(2)}) copy-start(bf16[64,768]{1,0:T(8,128)(2,1)S(1)} %collective-permute-done.4.refs_5_) | copy-start | bytes 294916
  15.3 15.0 %copy-start.7 = (bf16[64,768]{1,0:T(8,128)(2,1)}, bf16[64,768]{1,0:T(8,128)(2,1)S(1)}, u32[]{:S(2)}) copy-start(bf16[64,768]{1,0:T(8,128)(2,1)S(1)} %collective-permute-done.5.refs_6_) | copy-start | bytes 294916
  16.2 14.1 %copy-start.1 = (bf16[1,256,768]{2,1,0:T(8,128)(2,1)S(1)}, bf16[1,256,768]{2,1,0:T(8,128)(2,1)}, u32[]{:S(2)}) copy-start(bf16[1,256,768]{2,1,0:T(8,128)(2,1)} %param.10) | copy-start | bytes 1179652
  16.2 20.2 %collective-permute-start.6 = (bf16[256,768]{1,0:T(8,128)(2,1)S(1)}, bf16[256,768]{1,0:T(8,128)(2,1)S(1)}, u32[]{:S(2)}, u32[]{:S(2)}) collective-permute-start(bf16[256,768]{1,0:T(8,128)(2,1)S(1)} %pad_maximum_fusion), channel_id=1, source_target_pairs={{0,4},{1,5},{2,6},{3,7},{4,0},{5,1},{6,2},{7,3},{8,12},{9,13},{10,... | collective-permute-start | bytes 1179656 | tf_op jit(solution)/shard_map/ppermute | solution.py:350
  17.5 14.1 %collective-permute-start.1 = (bf16[128,768]{1,0:T(8,128)(2,1)}, bf16[128,768]{1,0:T(8,128)(2,1)S(1)}, u32[]{:S(2)}, u32[]{:S(2)}) collective-permute-start(bf16[128,768]{1,0:T(8,128)(2,1)} %get-tuple-element.37.mid_ref.refs_9_), channel_id=1, source_target_pairs={{0,2},{1,3},{2,0},{3,1},{4,6},{5,7},{6,4},{7,5},{8,10},{9,11},{10,... | collective-permute-start | bytes 589832 | tf_op jit(solution)/shard_map/ppermute | solution.py:350
  21.1 15.4 %collective-permute-start.2 = (bf16[128,768]{1,0:T(8,128)(2,1)}, bf16[128,768]{1,0:T(8,128)(2,1)}, u32[]{:S(2)}, u32[]{:S(2)}) collective-permute-start(bf16[128,768]{1,0:T(8,128)(2,1)} %get-tuple-element.37.mid_ref.refs_9_), channel_id=1, source_target_pairs={{0,3},{1,2},{2,1},{3,0},{4,7},{5,6},{6,5},{7,4},{8,11},{9,10},{10,... | collective-permute-start | bytes 589832 | tf_op jit(solution)/shard_map/ppermute | solution.py:350
  52.5 4.7 %collective-permute-start.7 = (bf16[768,384]{0,1:T(8,128)(2,1)S(1)}, bf16[768,384]{0,1:T(8,128)(2,1)S(1)}, u32[]{:S(2)}, u32[]{:S(2)}) collective-permute-start(bf16[768,384]{0,1:T(8,128)(2,1)S(1)} %fusion.2), channel_id=1, source_target_pairs={{0,64},{64,0},{128,192},{192,128},{1,65},{65,1},{129,193},{193,129... | collective-permute-start | bytes 1769480 | tf_op jit(solution)/shard_map/ppermute | solution.py:354
  54.2 20.4 %collective-permute-start.8 = (bf16[384,768]{1,0:T(8,128)(2,1)}, bf16[384,768]{1,0:T(8,128)(2,1)}, u32[]{:S(2)}, u32[]{:S(2)}) collective-permute-start(bf16[384,768]{1,0:T(8,128)(2,1)} %get-tuple-element.47), channel_id=1, source_target_pairs={{0,1},{1,0},{2,3},{3,2},{4,5},{5,4},{6,7},{7,6},{8,9},{9,8},{10,11... | collective-permute-start | bytes 1769480 | tf_op jit(solution)/shard_map/ppermute | solution.py:350
  56.5 17.2 %collective-permute-start.9 = (bf16[128,768]{1,0:T(8,128)(2,1)}, bf16[128,768]{1,0:T(8,128)(2,1)}, u32[]{:S(2)}, u32[]{:S(2)}) collective-permute-start(bf16[128,768]{1,0:T(8,128)(2,1)} %get-tuple-element.48), channel_id=1, source_target_pairs={{0,2},{1,3},{2,0},{3,1},{4,6},{5,7},{6,4},{7,5},{8,10},{9,11},{10,... | collective-permute-start | bytes 589832 | tf_op jit(solution)/shard_map/ppermute | solution.py:350
  56.5 18.1 %collective-permute-start.10 = (bf16[256,768]{1,0:T(8,128)(2,1)}, bf16[256,768]{1,0:T(8,128)(2,1)S(1)}, u32[]{:S(2)}, u32[]{:S(2)}) collective-permute-start(bf16[256,768]{1,0:T(8,128)(2,1)} %get-tuple-element.50), channel_id=1, source_target_pairs={{0,4},{1,5},{2,6},{3,7},{4,0},{5,1},{6,2},{7,3},{8,12},{9,13},{10,... | collective-permute-start | bytes 1179656 | tf_op jit(solution)/shard_map/ppermute | solution.py:350
  58.6 17.5 %all-to-all-start = ((bf16[16,48,384]{2,1,0:T(8,128)(2,1)}), bf16[16,48,384]{2,1,0:T(8,128)(2,1)S(1)}, u32[]{:S(2)}, u32[]{:S(2)}) async-start(bf16[16,48,384]{2,1,0:T(8,128)(2,1)} %bitcast.3), calls=%async_computation | async-start | bytes 1179648 | tf_op jit(solution)/shard_map/all_to_all | solution.py:374
  66.4 14.0 %collective-permute-start.14 = (bf16[128,768]{1,0:T(8,128)(2,1)S(1)}, bf16[128,768]{1,0:T(8,128)(2,1)}, u32[]{:S(2)}, u32[]{:S(2)}) collective-permute-start(bf16[128,768]{1,0:T(8,128)(2,1)S(1)} %copy-done.13), channel_id=1, source_target_pairs={{0,3},{1,2},{2,1},{3,0},{4,7},{5,6},{6,5},{7,4},{8,11},{9,10},{10,... | collective-permute-start | bytes 589832 | tf_op jit(solution)/shard_map/ppermute | solution.py:350
  76.3 7.4 %collective-permute-start.11 = (bf16[72,768]{1,0:T(8,128)(2,1)S(1)}, bf16[72,768]{1,0:T(8,128)(2,1)S(1)}, u32[]{:S(2)}, u32[]{:S(2)}) collective-permute-start(bf16[72,768]{1,0:T(8,128)(2,1)S(1)} %pad_maximum_fusion.1), channel_id=1, source_target_pairs={{0,1},{1,0},{2,3},{3,2},{4,5},{5,4},{6,7},{7,6},{8,9},{9,8},{10,11... | collective-permute-start | bytes 331784 | tf_op jit(solution)/shard_map/ppermute | solution.py:350
  77.9 10.9 %collective-permute-start.12 = (bf16[72,768]{1,0:T(8,128)(2,1)S(1)}, bf16[72,768]{1,0:T(8,128)(2,1)S(1)}, u32[]{:S(2)}, u32[]{:S(2)}) collective-permute-start(bf16[72,768]{1,0:T(8,128)(2,1)S(1)} %pad_maximum_fusion.2), channel_id=1, source_target_pairs={{0,2},{1,3},{2,0},{3,1},{4,6},{5,7},{6,4},{7,5},{8,10},{9,11},{10,... | collective-permute-start | bytes 331784 | tf_op jit(solution)/shard_map/ppermute | solution.py:350
  78.9 9.9 %collective-permute-start.13 = (bf16[72,768]{1,0:T(8,128)(2,1)S(1)}, bf16[72,768]{1,0:T(8,128)(2,1)S(1)}, u32[]{:S(2)}, u32[]{:S(2)}) collective-permute-start(bf16[72,768]{1,0:T(8,128)(2,1)S(1)} %pad_maximum_fusion.3), channel_id=1, source_target_pairs={{0,3},{1,2},{2,1},{3,0},{4,7},{5,6},{6,5},{7,4},{8,11},{9,10},{10,... | collective-permute-start | bytes 331784 | tf_op jit(solution)/shard_map/ppermute | solution.py:350
  83.7 10.5 %copy-start.8 = (bf16[72,768]{1,0:T(8,128)(2,1)}, bf16[72,768]{1,0:T(8,128)(2,1)S(1)}, u32[]{:S(2)}) copy-start(bf16[72,768]{1,0:T(8,128)(2,1)S(1)} %collective-permute-done.11.refs_1_) | copy-start | bytes 331780
  88.8 8.1 %collective-permute-start.15 = (bf16[6,768]{1,0:T(8,128)(2,1)S(1)}, bf16[6,768]{1,0:T(8,128)(2,1)S(1)}, u32[]{:S(2)}, u32[]{:S(2)}) collective-permute-start(bf16[6,768]{1,0:T(8,128)(2,1)S(1)} %add_convert_fusion.1), channel_id=1, source_target_pairs={{0,128},{64,192},{128,0},{192,64},{1,129},{65,193},{129,1},{193,65... | collective-permute-start | bytes 27656 | tf_op jit(solution)/shard_map/ppermute | solution.py:354
  96.9 3.8 %collective-permute-start.16 = (bf16[6,768]{1,0:T(8,128)(2,1)S(1)}, bf16[6,768]{1,0:T(8,128)(2,1)S(1)}, u32[]{:S(2)}, u32[]{:S(2)}) collective-permute-start(bf16[6,768]{1,0:T(8,128)(2,1)S(1)} %multiply_convert_fusion), channel_id=1, source_target_pairs={{0,64},{64,0},{128,192},{192,128},{1,65},{65,1},{129,193},{193,129... | collective-permute-start | bytes 27656 | tf_op jit(solution)/shard_map/ppermute | solution.py:354
  (9 other events, 43.4 us)

commit v6 on v5

--- a/solution.py
+++ b/solution.py
@@ -395,7 +395,8 @@
     fars = [far] + [swap(far, bits) for bits in (1, 2, 3)]
     cross = swap(jnp.concatenate(fars, axis=0), 4)
     near_pair, mid2, mid3 = swap(near, 1), swap(mid, 2), swap(mid, 3)
-    grads = jnp.dot(cotangent, out_weight, preferred_element_type=F32).astype(BF16)
+    late_cotangent, (mid2,) = after(cotangent, [mid2])
+    grads = jnp.dot(late_cotangent, out_weight, preferred_element_type=F32).astype(BF16)
     gathered = [near_pair, mid2, mid3] + fars + [cross]
     own_parts = attend_own(GROUPS[0], queries, keys, values, near, mid, far)
     results = attend_both(GROUPS[0], queries, keys, values, grads, near, mid, gathered, own_parts)

time: 102 us -> 100 us (0.980)
  waiting for transfers between devices: 24.7 us -> 23 us
    ppermute x14, waiting for transfers between devices: 22.5 us -> 19.7 us  [swap(): lax.ppermute(block, 'seq', [(i, i ^ bits) for i in range(lax.axis_size('s...]
    all_to_all x1, waiting for transfers between devices: 1.41 us -> 2.43 us  [plane_share(): lax.all_to_all(total, 'seq', 0, 0, axis_index_groups=groups, tiled=True)]
where the time goes in v6:
time: 100 us; the launch traced here: 99.7 us
  starting transfers between devices  37.3 us (37%)
  Pallas kernels  30.3 us (30%)
  waiting for transfers between devices  23 us (23%)
  matrix products  4.19 us (4%)
  local copies, waits for them, and re-layouts  2.21 us (2%)
  other arithmetic  1.84 us (2%)
    pallas_call x2, Pallas kernels, call(): pl.pallas_call(kernel, grid=(self.count,), in_specs=list(in_specs) + [pl....  21.6 us
    ppermute x14, starting transfers between devices, swap(): lax.ppermute(block, 'seq', [(i, i ^ bits) for i in range(lax.axis_size('s...  20.1 us
    ppermute x14, waiting for transfers between devices, swap(): lax.ppermute(block, 'seq', [(i, i ^ bits) for i in range(lax.axis_size('s...  19.7 us
    ppermute x3, starting transfers between devices, slide_swap(): lax.ppermute(block, 'dp', [(i, i ^ bits) for i in range(lax.axis_size('dp...  10.8 us
    all_to_all x1, starting transfers between devices, plane_share(): lax.all_to_all(total, 'seq', 0, 0, axis_index_groups=groups, tiled=True)  6.42 us
    pallas_call x2, Pallas kernels, spread(): pl.pallas_call(functools.partial(spread_kernel, [(level, len(parts)) for...  6.03 us
    pallas_call x1, Pallas kernels, pick(): pl.pallas_call(pick_kernel, grid=(feature // width,), in_specs=[pl.BlockS...  2.67 us
    all_to_all x1, waiting for transfers between devices, plane_share(): lax.all_to_all(total, 'seq', 0, 0, axis_index_groups=groups, tiled=True)  2.43 us
  transfers between devices with their start and end apart: 18, of which 8 were waited for; matrix products, arithmetic and copies ran while one was open for 5% of the time, Pallas kernels for 14%

profile of v6, /device:TPU:1, one launch (start us, length us, event | category | flops | bytes accessed | tf_op | source)
XLA Modules:
  0.0 99.7 jit_solution(1088780495327821587)
XLA Ops:
  0.6 2.7 %pick_rows.1 = (bf16[64,768]{1,0:T(8,128)(2,1)}, bf16[384,768]{1,0:T(8,128)(2,1)}, bf16[128,768]{1,0:T(8,128)(2,1)}) custom-call(s32[3,12]{1,0:T(4,128)} %offsets_ref.5, bf16[1,256,768]{2,1,0:T(8,128)(2,1)} %key_ref.5, bf16[1,256,768]{2,1,0:T(8,128)(2,1)} %value_ref.5), custom_call_target="tpu_custom_call" | custom-call | flops 2000000000 | bytes 2000000 | tf_op jit(solution)/shard_map/pick_rows/pallas_call | solution.py:77
  3.3 2.5 %collective-permute-start.3 = (bf16[64,768]{1,0:T(8,128)(2,1)}, bf16[64,768]{1,0:T(8,128)(2,1)S(1)}, u32[]{:S(2)}, u32[]{:S(2)}) collective-permute-start(bf16[64,768]{1,0:T(8,128)(2,1)} %get-tuple-element.41.far_ref.refs_3_), channel_id=1, source_target_pairs={{0,1},{1,0},{2,3},{3,2},{4,5},{5,4},{6,7},{7,6},{8,9},{9,8},{10,11... | collective-permute-start | bytes 294920 | tf_op jit(solution)/shard_map/ppermute | solution.py:350
  5.8 3.0 %collective-permute-start.4 = (bf16[64,768]{1,0:T(8,128)(2,1)}, bf16[64,768]{1,0:T(8,128)(2,1)S(1)}, u32[]{:S(2)}, u32[]{:S(2)}) collective-permute-start(bf16[64,768]{1,0:T(8,128)(2,1)} %get-tuple-element.41.far_ref.refs_3_), channel_id=1, source_target_pairs={{0,2},{1,3},{2,0},{3,1},{4,6},{5,7},{6,4},{7,5},{8,10},{9,11},{10,... | collective-permute-start | bytes 294920 | tf_op jit(solution)/shard_map/ppermute | solution.py:350
  9.1 3.3 %collective-permute-start.1 = (bf16[128,768]{1,0:T(8,128)(2,1)}, bf16[128,768]{1,0:T(8,128)(2,1)S(1)}, u32[]{:S(2)}, u32[]{:S(2)}) collective-permute-start(bf16[128,768]{1,0:T(8,128)(2,1)} %get-tuple-element.39.mid_ref.refs_9_), channel_id=1, source_target_pairs={{0,2},{1,3},{2,0},{3,1},{4,6},{5,7},{6,4},{7,5},{8,10},{9,11},{10,... | collective-permute-start | bytes 589832 | tf_op jit(solution)/shard_map/ppermute | solution.py:350
  12.3 2.9 %collective-permute-done.5.refs_6_ = bf16[64,768]{1,0:T(8,128)(2,1)S(1)} collective-permute-done((bf16[64,768]{1,0:T(8,128)(2,1)}, bf16[64,768]{1,0:T(8,128)(2,1)S(1)}, u32[]{:S(2)}, u32[]{:S(2)}) %collective-permute-start.5) | collective-permute-done | bytes 98336 | tf_op jit(solution)/shard_map/ppermute | solution.py:350
  18.4 7.9 %attend_own.1 = (bf16[6,480,512]{2,1,0:T(8,128)(2,1)}, f32[6,32,256]{2,1,0:T(8,128)}, f32[6,128,256]{2,1,0:T(8,128)}) custom-call(bf16[1,256,768]{2,1,0:T(8,128)(2,1)} %query_ref.3, bf16[1,256,768]{2,1,0:T(8,128)(2,1)} %key_ref.5, bf16[1,256,768]{2,1,0:T(8,128)(2,1)} %value_ref.5, bf16[384,768]{1,0:T(8,128)(2,1)} %get-tuple-element.38.near_ref, ...), custom_call_target="tpu_custom_call" | custom-call | flops 600000000 | bytes 1000000 | tf_op jit(solution)/shard_map/attend_own/pallas_call | solution.py:242
  26.3 3.0 %collective-permute-done.1.refs_1_ = bf16[128,768]{1,0:T(8,128)(2,1)S(1)} collective-permute-done((bf16[128,768]{1,0:T(8,128)(2,1)}, bf16[128,768]{1,0:T(8,128)(2,1)S(1)}, u32[]{:S(2)}, u32[]{:S(2)}) %collective-permute-start.1) | collective-permute-done | bytes 196640 | tf_op jit(solution)/shard_map/ppermute | solution.py:350
  30.6 5.9 %collective-permute-done.2.refs_2_ = bf16[128,768]{1,0:T(8,128)(2,1)} collective-permute-done((bf16[128,768]{1,0:T(8,128)(2,1)}, bf16[128,768]{1,0:T(8,128)(2,1)}, u32[]{:S(2)}, u32[]{:S(2)}) %collective-permute-start.2) | collective-permute-done | bytes 196640 | tf_op jit(solution)/shard_map/ppermute | solution.py:350
  37.4 13.7 %attend_both.1 = (bf16[256,768]{1,0:T(8,128)(2,1)}, bf16[1,256,768]{2,1,0:T(8,128)(2,1)}, f32[512,768]{1,0:T(8,128)}, f32[256,768]{1,0:T(8,128)}, f32[128,768]{1...) custom-call(bf16[1,256,768]{2,1,0:T(8,128)(2,1)} %query_ref.3, ...), custom_call_target="tpu_custom_call" | custom-call | flops 15600000000 | bytes 1000000 | tf_op jit(solution)/shard_map/attend_both/pallas_call | solution.py:242
  51.2 1.3 %fusion.2 = bf16[768,384]{0,1:T(8,128)(2,1)S(1)} fusion(bf16[256,768]{1,0:T(8,128)(2,1)} %get-tuple-element.46, s32[]{:T(128)S(6)} %select_n.45, bf16[1,256,768]{2,1,0:T(8,128)(2,1)S(1)} %copy-done.1), kind=kOutput, calls=%fused_computation.4 | convolution fusion | flops 151289856 | bytes 1179652 | tf_op jit(solution)/shard_map/dot_general | solution.py:368
  52.5 1.5 %collective-permute-start.7 = (bf16[768,384]{0,1:T(8,128)(2,1)S(1)}, bf16[768,384]{0,1:T(8,128)(2,1)S(1)}, u32[]{:S(2)}, u32[]{:S(2)}) collective-permute-start(bf16[768,384]{0,1:T(8,128)(2,1)S(1)} %fusion.2), channel_id=1, source_target_pairs={{0,64},{64,0},{128,192},{192,128},{1,65},{65,1},{129,193},{193,129... | collective-permute-start | bytes 1769480 | tf_op jit(solution)/shard_map/ppermute | solution.py:354
  54.0 1.9 %collective-permute-start.9 = (bf16[128,768]{1,0:T(8,128)(2,1)}, bf16[128,768]{1,0:T(8,128)(2,1)}, u32[]{:S(2)}, u32[]{:S(2)}) collective-permute-start(bf16[128,768]{1,0:T(8,128)(2,1)} %get-tuple-element.52), channel_id=1, source_target_pairs={{0,2},{1,3},{2,0},{3,1},{4,6},{5,7},{6,4},{7,5},{8,10},{9,11},{10,... | collective-permute-start | bytes 589832 | tf_op jit(solution)/shard_map/ppermute | solution.py:350
  58.6 6.4 %all-to-all-start = ((bf16[16,48,384]{2,1,0:T(8,128)(2,1)}), bf16[16,48,384]{2,1,0:T(8,128)(2,1)S(1)}, u32[]{:S(2)}, u32[]{:S(2)}) async-start(bf16[16,48,384]{2,1,0:T(8,128)(2,1)} %bitcast.3), calls=%async_computation | async-start | bytes 1179648 | tf_op jit(solution)/shard_map/all_to_all | solution.py:374
  66.3 1.8 %collective-permute-start.14 = (bf16[128,768]{1,0:T(8,128)(2,1)S(1)}, bf16[128,768]{1,0:T(8,128)(2,1)}, u32[]{:S(2)}, u32[]{:S(2)}) collective-permute-start(bf16[128,768]{1,0:T(8,128)(2,1)S(1)} %copy-done.13), channel_id=1, source_target_pairs={{0,3},{1,2},{2,1},{3,0},{4,7},{5,6},{6,5},{7,4},{8,11},{9,10},{10,... | collective-permute-start | bytes 589832 | tf_op jit(solution)/shard_map/ppermute | solution.py:350
  68.1 3.3 %collective-permute-done.9.refs_4_ = bf16[128,768]{1,0:T(8,128)(2,1)} collective-permute-done((bf16[128,768]{1,0:T(8,128)(2,1)}, bf16[128,768]{1,0:T(8,128)(2,1)}, u32[]{:S(2)}, u32[]{:S(2)}) %collective-permute-start.9) | collective-permute-done | bytes 196640 | tf_op jit(solution)/shard_map/ppermute | solution.py:350
  71.4 2.0 %collective-permute-done.8.refs_1_.refs_3_ = bf16[384,768]{1,0:T(8,128)(2,1)} collective-permute-done((bf16[384,768]{1,0:T(8,128)(2,1)}, bf16[384,768]{1,0:T(8,128)(2,1)}, u32[]{:S(2)}, u32[]{:S(2)}) %collective-permute-start.8) | collective-permute-done | bytes 589856 | tf_op jit(solution)/shard_map/ppermute | solution.py:350
  73.6 2.4 %all-to-all-done = bf16[16,48,384]{2,1,0:T(8,128)(2,1)S(1)} async-done(((bf16[16,48,384]{2,1,0:T(8,128)(2,1)}), bf16[16,48,384]{2,1,0:T(8,128)(2,1)S(1)}, u32[]{:S(2)}, u32[]{:S(2)}) %all-to-all-start) | async-done | bytes 589856 | tf_op jit(solution)/shard_map/all_to_all | solution.py:374
  76.5 2.2 %collective-permute-start.12 = (bf16[72,768]{1,0:T(8,128)(2,1)S(1)}, bf16[72,768]{1,0:T(8,128)(2,1)S(1)}, u32[]{:S(2)}, u32[]{:S(2)}) collective-permute-start(bf16[72,768]{1,0:T(8,128)(2,1)S(1)} %pad_maximum_fusion.2), channel_id=1, source_target_pairs={{0,2},{1,3},{2,0},{3,1},{4,6},{5,7},{6,4},{7,5},{8,10},{9,11},{10,... | collective-permute-start | bytes 331784 | tf_op jit(solution)/shard_map/ppermute | solution.py:350
  78.8 1.5 %collective-permute-start.13 = (bf16[72,768]{1,0:T(8,128)(2,1)S(1)}, bf16[72,768]{1,0:T(8,128)(2,1)S(1)}, u32[]{:S(2)}, u32[]{:S(2)}) collective-permute-start(bf16[72,768]{1,0:T(8,128)(2,1)S(1)} %pad_maximum_fusion.3), channel_id=1, source_target_pairs={{0,3},{1,2},{2,1},{3,0},{4,7},{5,6},{6,5},{7,4},{8,11},{9,10},{10,... | collective-permute-start | bytes 331784 | tf_op jit(solution)/shard_map/ppermute | solution.py:350
  80.3 3.4 %spread_rows.2 = (f32[1,256,768]{2,1,0:T(8,128)}, f32[1,256,768]{2,1,0:T(8,128)}) custom-call(s32[3,12]{1,0:T(4,128)} %offsets_ref.5, f32[2,256,768]{2,1,0:T(8,128)} %bitcast.22, f32[2,256,768]{2,1,0:T(8,128)} %bitcast.23, f32[256,768]{1,0:T(8,128)} %get-tuple-element.56.refs_0_, bf16[384,768]{1,0:T(8,128)(2,1)} %collective-permute-done.8.refs_1_.refs_3_, ...), custom_call_target="tpu_custom_call" | custom-call | flops 2000000000 | bytes 4000000 | tf_op jit(solution)/shard_map/spread_rows/pallas_call | solution.py:332
  83.6 2.6 %collective-permute-done.12.refs_2_ = bf16[72,768]{1,0:T(8,128)(2,1)S(1)} collective-permute-done((bf16[72,768]{1,0:T(8,128)(2,1)S(1)}, bf16[72,768]{1,0:T(8,128)(2,1)S(1)}, u32[]{:S(2)}, u32[]{:S(2)}) %collective-permute-start.12) | collective-permute-done | bytes 110624 | tf_op jit(solution)/shard_map/ppermute | solution.py:350
  86.2 6.6 %collective-permute-start.15 = (bf16[6,768]{1,0:T(8,128)(2,1)S(1)}, bf16[6,768]{1,0:T(8,128)(2,1)S(1)}, u32[]{:S(2)}, u32[]{:S(2)}) collective-permute-start(bf16[6,768]{1,0:T(8,128)(2,1)S(1)} %add_convert_fusion.1), channel_id=1, source_target_pairs={{0,128},{64,192},{128,0},{192,64},{1,129},{65,193},{129,1},{193,65... | collective-permute-start | bytes 27656 | tf_op jit(solution)/shard_map/ppermute | solution.py:354
  92.8 2.7 %spread_rows.3 = (bf16[1,256,768]{2,1,0:T(8,128)(2,1)}, bf16[1,256,768]{2,1,0:T(8,128)(2,1)}) custom-call(s32[3,12]{1,0:T(4,128)} %offsets_ref.5, f32[1,256,768]{2,1,0:T(8,128)} %get-tuple-element.64.key_base_ref, f32[1,256,768]{2,1,0:T(8,128)} %get-tuple-element.65.value_base_ref, bf16[256,768]{1,0:T(8,128)(2,1)} %copy-done.3, bf16[72,768]{1,0:T(8,128)(2,1)} %copy-done.8, ...), custom_call_target="tpu_custom_call" | custom-call | flops 2000000000 | bytes 4000000 | tf_op jit(solution)/shard_map/spread_rows/pallas_call | solution.py:332
  95.5 2.7 %collective-permute-start.16 = (bf16[6,768]{1,0:T(8,128)(2,1)S(1)}, bf16[6,768]{1,0:T(8,128)(2,1)S(1)}, u32[]{:S(2)}, u32[]{:S(2)}) collective-permute-start(bf16[6,768]{1,0:T(8,128)(2,1)S(1)} %multiply_convert_fusion), channel_id=1, source_target_pairs={{0,64},{64,0},{128,192},{192,128},{1,65},{65,1},{129,193},{193,129... | collective-permute-start | bytes 27656 | tf_op jit(solution)/shard_map/ppermute | solution.py:354
  (68 shorter events, 11.8 us)
Async XLA Ops:
  0.6 28.7 %copy-start = (bf16[768,768]{1,0:T(8,128)(2,1)S(1)}, bf16[768,768]{1,0:T(8,128)(2,1)}, u32[]{:S(2)}) copy-start(bf16[768,768]{1,0:T(8,128)(2,1)} %param.9) | copy-start | bytes 3538948
  3.3 9.0 %collective-permute-start.3 = (bf16[64,768]{1,0:T(8,128)(2,1)}, bf16[64,768]{1,0:T(8,128)(2,1)S(1)}, u32[]{:S(2)}, u32[]{:S(2)}) collective-permute-start(bf16[64,768]{1,0:T(8,128)(2,1)} %get-tuple-element.41.far_ref.refs_3_), channel_id=1, source_target_pairs={{0,1},{1,0},{2,3},{3,2},{4,5},{5,4},{6,7},{7,6},{8,9},{9,8},{10,11... | collective-permute-start | bytes 294920 | tf_op jit(solution)/shard_map/ppermute | solution.py:350
  5.8 6.5 %collective-permute-start.4 = (bf16[64,768]{1,0:T(8,128)(2,1)}, bf16[64,768]{1,0:T(8,128)(2,1)S(1)}, u32[]{:S(2)}, u32[]{:S(2)}) collective-permute-start(bf16[64,768]{1,0:T(8,128)(2,1)} %get-tuple-element.41.far_ref.refs_3_), channel_id=1, source_target_pairs={{0,2},{1,3},{2,0},{3,1},{4,6},{5,7},{6,4},{7,5},{8,10},{9,11},{10,... | collective-permute-start | bytes 294920 | tf_op jit(solution)/shard_map/ppermute | solution.py:350
  8.8 6.5 %collective-permute-start.5 = (bf16[64,768]{1,0:T(8,128)(2,1)}, bf16[64,768]{1,0:T(8,128)(2,1)S(1)}, u32[]{:S(2)}, u32[]{:S(2)}) collective-permute-start(bf16[64,768]{1,0:T(8,128)(2,1)} %get-tuple-element.41.far_ref.refs_3_), channel_id=1, source_target_pairs={{0,3},{1,2},{2,1},{3,0},{4,7},{5,6},{6,5},{7,4},{8,11},{9,10},{10,... | collective-permute-start | bytes 294920 | tf_op jit(solution)/shard_map/ppermute | solution.py:350
  8.8 27.7 %collective-permute-start = (bf16[384,768]{1,0:T(8,128)(2,1)}, bf16[384,768]{1,0:T(8,128)(2,1)S(1)}, u32[]{:S(2)}, u32[]{:S(2)}) collective-permute-start(bf16[384,768]{1,0:T(8,128)(2,1)} %get-tuple-element.38.near_ref), channel_id=1, source_target_pairs={{0,1},{1,0},{2,3},{3,2},{4,5},{5,4},{6,7},{7,6},{8,9},{9,8},{10,11... | collective-permute-start | bytes 1769480 | tf_op jit(solution)/shard_map/ppermute | solution.py:350
  9.1 20.3 %collective-permute-start.1 = (bf16[128,768]{1,0:T(8,128)(2,1)}, bf16[128,768]{1,0:T(8,128)(2,1)S(1)}, u32[]{:S(2)}, u32[]{:S(2)}) collective-permute-start(bf16[128,768]{1,0:T(8,128)(2,1)} %get-tuple-element.39.mid_ref.refs_9_), channel_id=1, source_target_pairs={{0,2},{1,3},{2,0},{3,1},{4,6},{5,7},{6,4},{7,5},{8,10},{9,11},{10,... | collective-permute-start | bytes 589832 | tf_op jit(solution)/shard_map/ppermute | solution.py:350
  12.3 14.0 %copy-start.5 = (bf16[64,768]{1,0:T(8,128)(2,1)}, bf16[64,768]{1,0:T(8,128)(2,1)S(1)}, u32[]{:S(2)}) copy-start(bf16[64,768]{1,0:T(8,128)(2,1)S(1)} %collective-permute-done.3.refs_4_) | copy-start | bytes 294916
  12.3 14.0 %copy-start.6 = (bf16[64,768]{1,0:T(8,128)(2,1)}, bf16[64,768]{1,0:T(8,128)(2,1)S(1)}, u32[]{:S(2)}) copy-start(bf16[64,768]{1,0:T(8,128)(2,1)S(1)} %collective-permute-done.4.refs_5_) | copy-start | bytes 294916
  15.3 11.1 %copy-start.7 = (bf16[64,768]{1,0:T(8,128)(2,1)}, bf16[64,768]{1,0:T(8,128)(2,1)S(1)}, u32[]{:S(2)}) copy-start(bf16[64,768]{1,0:T(8,128)(2,1)S(1)} %collective-permute-done.5.refs_6_) | copy-start | bytes 294916
  16.2 13.1 %copy-start.1 = (bf16[1,256,768]{2,1,0:T(8,128)(2,1)S(1)}, bf16[1,256,768]{2,1,0:T(8,128)(2,1)}, u32[]{:S(2)}) copy-start(bf16[1,256,768]{2,1,0:T(8,128)(2,1)} %param.10) | copy-start | bytes 1179652
  16.2 20.2 %collective-permute-start.6 = (bf16[256,768]{1,0:T(8,128)(2,1)S(1)}, bf16[256,768]{1,0:T(8,128)(2,1)S(1)}, u32[]{:S(2)}, u32[]{:S(2)}) collective-permute-start(bf16[256,768]{1,0:T(8,128)(2,1)S(1)} %pad_maximum_fusion), channel_id=1, source_target_pairs={{0,4},{1,5},{2,6},{3,7},{4,0},{5,1},{6,2},{7,3},{8,12},{9,13},{10,... | collective-permute-start | bytes 1179656 | tf_op jit(solution)/shard_map/ppermute | solution.py:350
  17.5 19.0 %collective-permute-start.2 = (bf16[128,768]{1,0:T(8,128)(2,1)}, bf16[128,768]{1,0:T(8,128)(2,1)}, u32[]{:S(2)}, u32[]{:S(2)}) collective-permute-start(bf16[128,768]{1,0:T(8,128)(2,1)} %get-tuple-element.39.mid_ref.refs_9_), channel_id=1, source_target_pairs={{0,3},{1,2},{2,1},{3,0},{4,7},{5,6},{6,5},{7,4},{8,11},{9,10},{10,... | collective-permute-start | bytes 589832 | tf_op jit(solution)/shard_map/ppermute | solution.py:350
  52.5 4.6 %collective-permute-start.7 = (bf16[768,384]{0,1:T(8,128)(2,1)S(1)}, bf16[768,384]{0,1:T(8,128)(2,1)S(1)}, u32[]{:S(2)}, u32[]{:S(2)}) collective-permute-start(bf16[768,384]{0,1:T(8,128)(2,1)S(1)} %fusion.2), channel_id=1, source_target_pairs={{0,64},{64,0},{128,192},{192,128},{1,65},{65,1},{129,193},{193,129... | collective-permute-start | bytes 1769480 | tf_op jit(solution)/shard_map/ppermute | solution.py:354
  54.0 19.4 %collective-permute-start.8 = (bf16[384,768]{1,0:T(8,128)(2,1)}, bf16[384,768]{1,0:T(8,128)(2,1)}, u32[]{:S(2)}, u32[]{:S(2)}) collective-permute-start(bf16[384,768]{1,0:T(8,128)(2,1)} %get-tuple-element.51), channel_id=1, source_target_pairs={{0,1},{1,0},{2,3},{3,2},{4,5},{5,4},{6,7},{7,6},{8,9},{9,8},{10,11... | collective-permute-start | bytes 1769480 | tf_op jit(solution)/shard_map/ppermute | solution.py:350
  54.0 17.4 %collective-permute-start.9 = (bf16[128,768]{1,0:T(8,128)(2,1)}, bf16[128,768]{1,0:T(8,128)(2,1)}, u32[]{:S(2)}, u32[]{:S(2)}) collective-permute-start(bf16[128,768]{1,0:T(8,128)(2,1)} %get-tuple-element.52), channel_id=1, source_target_pairs={{0,2},{1,3},{2,0},{3,1},{4,6},{5,7},{6,4},{7,5},{8,10},{9,11},{10,... | collective-permute-start | bytes 589832 | tf_op jit(solution)/shard_map/ppermute | solution.py:350
  55.9 17.5 %collective-permute-start.10 = (bf16[256,768]{1,0:T(8,128)(2,1)}, bf16[256,768]{1,0:T(8,128)(2,1)S(1)}, u32[]{:S(2)}, u32[]{:S(2)}) collective-permute-start(bf16[256,768]{1,0:T(8,128)(2,1)} %get-tuple-element.54), channel_id=1, source_target_pairs={{0,4},{1,5},{2,6},{3,7},{4,0},{5,1},{6,2},{7,3},{8,12},{9,13},{10,... | collective-permute-start | bytes 1179656 | tf_op jit(solution)/shard_map/ppermute | solution.py:350
  58.6 17.4 %all-to-all-start = ((bf16[16,48,384]{2,1,0:T(8,128)(2,1)}), bf16[16,48,384]{2,1,0:T(8,128)(2,1)S(1)}, u32[]{:S(2)}, u32[]{:S(2)}) async-start(bf16[16,48,384]{2,1,0:T(8,128)(2,1)} %bitcast.3), calls=%async_computation | async-start | bytes 1179648 | tf_op jit(solution)/shard_map/all_to_all | solution.py:374
  66.3 14.0 %collective-permute-start.14 = (bf16[128,768]{1,0:T(8,128)(2,1)S(1)}, bf16[128,768]{1,0:T(8,128)(2,1)}, u32[]{:S(2)}, u32[]{:S(2)}) collective-permute-start(bf16[128,768]{1,0:T(8,128)(2,1)S(1)} %copy-done.13), channel_id=1, source_target_pairs={{0,3},{1,2},{2,1},{3,0},{4,7},{5,6},{6,5},{7,4},{8,11},{9,10},{10,... | collective-permute-start | bytes 589832 | tf_op jit(solution)/shard_map/ppermute | solution.py:350
  73.5 10.1 %copy-start.3 = (bf16[256,768]{1,0:T(8,128)(2,1)}, bf16[256,768]{1,0:T(8,128)(2,1)S(1)}, u32[]{:S(2)}) copy-start(bf16[256,768]{1,0:T(8,128)(2,1)S(1)} %add_convert_fusion.refs_0_) | copy-start | bytes 1179652
  76.2 7.4 %collective-permute-start.11 = (bf16[72,768]{1,0:T(8,128)(2,1)S(1)}, bf16[72,768]{1,0:T(8,128)(2,1)S(1)}, u32[]{:S(2)}, u32[]{:S(2)}) collective-permute-start(bf16[72,768]{1,0:T(8,128)(2,1)S(1)} %pad_maximum_fusion.1), channel_id=1, source_target_pairs={{0,1},{1,0},{2,3},{3,2},{4,5},{5,4},{6,7},{7,6},{8,9},{9,8},{10,11... | collective-permute-start | bytes 331784 | tf_op jit(solution)/shard_map/ppermute | solution.py:350
  76.5 9.7 %collective-permute-start.12 = (bf16[72,768]{1,0:T(8,128)(2,1)S(1)}, bf16[72,768]{1,0:T(8,128)(2,1)S(1)}, u32[]{:S(2)}, u32[]{:S(2)}) collective-permute-start(bf16[72,768]{1,0:T(8,128)(2,1)S(1)} %pad_maximum_fusion.2), channel_id=1, source_target_pairs={{0,2},{1,3},{2,0},{3,1},{4,6},{5,7},{6,4},{7,5},{8,10},{9,11},{10,... | collective-permute-start | bytes 331784 | tf_op jit(solution)/shard_map/ppermute | solution.py:350
  78.8 7.5 %collective-permute-start.13 = (bf16[72,768]{1,0:T(8,128)(2,1)S(1)}, bf16[72,768]{1,0:T(8,128)(2,1)S(1)}, u32[]{:S(2)}, u32[]{:S(2)}) collective-permute-start(bf16[72,768]{1,0:T(8,128)(2,1)S(1)} %pad_maximum_fusion.3), channel_id=1, source_target_pairs={{0,3},{1,2},{2,1},{3,0},{4,7},{5,6},{6,5},{7,4},{8,11},{9,10},{10,... | collective-permute-start | bytes 331784 | tf_op jit(solution)/shard_map/ppermute | solution.py:350
  86.2 9.2 %collective-permute-start.15 = (bf16[6,768]{1,0:T(8,128)(2,1)S(1)}, bf16[6,768]{1,0:T(8,128)(2,1)S(1)}, u32[]{:S(2)}, u32[]{:S(2)}) collective-permute-start(bf16[6,768]{1,0:T(8,128)(2,1)S(1)} %add_convert_fusion.1), channel_id=1, source_target_pairs={{0,128},{64,192},{128,0},{192,64},{1,129},{65,193},{129,1},{193,65... | collective-permute-start | bytes 27656 | tf_op jit(solution)/shard_map/ppermute | solution.py:354
  95.5 3.6 %collective-permute-start.16 = (bf16[6,768]{1,0:T(8,128)(2,1)S(1)}, bf16[6,768]{1,0:T(8,128)(2,1)S(1)}, u32[]{:S(2)}, u32[]{:S(2)}) collective-permute-start(bf16[6,768]{1,0:T(8,128)(2,1)S(1)} %multiply_convert_fusion), channel_id=1, source_target_pairs={{0,64},{64,0},{128,192},{192,128},{1,65},{65,1},{129,193},{193,129... | collective-permute-start | bytes 27656 | tf_op jit(solution)/shard_map/ppermute | solution.py:354
  (9 other events, 46.9 us)

commit v7 on v6

--- a/solution.py
+++ b/solution.py
@@ -5,6 +5,7 @@
 import jax.numpy as jnp
 from jax import lax
 from jax.experimental import pallas as pl
+from jax.experimental.layout import Layout as Order, with_layout_constraint
 from jax.experimental.pallas import tpu as pltpu
 from jax.sharding import PartitionSpec as P
 
@@ -365,7 +366,8 @@
 
     def columns(which):
         block = lax.dynamic_slice_in_dim(attended, which * half, half, 1)
-        return lax.dot_general(cotangent, block, (((0,), (0,)), ((), ())), preferred_element_type=F32)
+        result = lax.dot_general(cotangent, block, (((0,), (0,)), ((), ())), preferred_element_type=F32)
+        return with_layout_constraint(result, Order(major_to_minor=(0, 1)))
 
     sent = slide_swap(columns(1 - core).astype(BF16), 1)
     total = (columns(core) + sent.astype(F32)).astype(BF16)

time: 100 us -> 100 us (level)
  waiting for transfers between devices: 23 us -> 21.3 us
    all_to_all x1, waiting for transfers between devices: 2.43 us -> 1.25 us  [plane_share(): lax.all_to_all(total, 'seq', 0, 0, axis_index_groups=groups, tiled=True)]
    convert_element_type x1 -> x0, local copies, waits for them, and re-layouts: 1.08 us -> none  [plane_share(): total = (columns(core) + sent.astype(F32)).astype(BF16)]
  transfers between devices with their start and end apart: 18 -> 18, of which waited for: 8 -> 8; matrix products, arithmetic and copies ran while one was open for 5% -> 6% of each run, Pallas kernels for 14% -> 14%
where the time goes in v7:
time: 100 us; the launch traced here: 99.7 us
  starting transfers between devices  37.3 us (37%)
  Pallas kernels  30.4 us (30%)
  waiting for transfers between devices  21.3 us (21%)
  matrix products  5.14 us (5%)
  other arithmetic  2.84 us (3%)
  local copies, waits for them, and re-layouts  1.82 us (2%)
    pallas_call x2, Pallas kernels, call(): pl.pallas_call(kernel, grid=(self.count,), in_specs=list(in_specs) + [pl....  21.6 us
    ppermute x14, starting transfers between devices, swap(): lax.ppermute(block, 'seq', [(i, i ^ bits) for i in range(lax.axis_size('s...  20 us
    ppermute x14, waiting for transfers between devices, swap(): lax.ppermute(block, 'seq', [(i, i ^ bits) for i in range(lax.axis_size('s...  19.2 us
    ppermute x3, starting transfers between devices, slide_swap(): lax.ppermute(block, 'dp', [(i, i ^ bits) for i in range(lax.axis_size('dp...  10.8 us
    all_to_all x1, starting transfers between devices, plane_share(): lax.all_to_all(total, 'seq', 0, 0, axis_index_groups=groups, tiled=True)  6.46 us
    pallas_call x2, Pallas kernels, spread(): pl.pallas_call(functools.partial(spread_kernel, [(level, len(parts)) for...  6.09 us
    pallas_call x1, Pallas kernels, pick(): pl.pallas_call(pick_kernel, grid=(feature // width,), in_specs=[pl.BlockS...  2.67 us
    dot_general x2, matrix products, columns(): lax.dot_general(cotangent, block, (((0,), (0,)), ((), ())), preferred_ele...  2.67 us
  transfers between devices with their start and end apart: 18, of which 8 were waited for; matrix products, arithmetic and copies ran while one was open for 6% of the time, Pallas kernels for 14%

profile of v7, /device:TPU:1, one launch (start us, length us, event | category | flops | bytes accessed | tf_op | source)
XLA Modules:
  0.0 99.7 jit_solution(12645682254934570421)
XLA Ops:
  0.6 2.7 %pick_rows.1 = (bf16[64,768]{1,0:T(8,128)(2,1)}, bf16[384,768]{1,0:T(8,128)(2,1)}, bf16[128,768]{1,0:T(8,128)(2,1)}) custom-call(s32[3,12]{1,0:T(4,128)} %offsets_ref.5, bf16[1,256,768]{2,1,0:T(8,128)(2,1)} %key_ref.5, bf16[1,256,768]{2,1,0:T(8,128)(2,1)} %value_ref.5), custom_call_target="tpu_custom_call" | custom-call | flops 2000000000 | bytes 2000000 | tf_op jit(solution)/shard_map/pick_rows/pallas_call | solution.py:78
  3.3 2.5 %collective-permute-start.3 = (bf16[64,768]{1,0:T(8,128)(2,1)}, bf16[64,768]{1,0:T(8,128)(2,1)S(1)}, u32[]{:S(2)}, u32[]{:S(2)}) collective-permute-start(bf16[64,768]{1,0:T(8,128)(2,1)} %get-tuple-element.41.far_ref.refs_3_), channel_id=1, source_target_pairs={{0,1},{1,0},{2,3},{3,2},{4,5},{5,4},{6,7},{7,6},{8,9},{9,8},{10,11... | collective-permute-start | bytes 294920 | tf_op jit(solution)/shard_map/ppermute | solution.py:351
  5.8 3.0 %collective-permute-start.4 = (bf16[64,768]{1,0:T(8,128)(2,1)}, bf16[64,768]{1,0:T(8,128)(2,1)S(1)}, u32[]{:S(2)}, u32[]{:S(2)}) collective-permute-start(bf16[64,768]{1,0:T(8,128)(2,1)} %get-tuple-element.41.far_ref.refs_3_), channel_id=1, source_target_pairs={{0,2},{1,3},{2,0},{3,1},{4,6},{5,7},{6,4},{7,5},{8,10},{9,11},{10,... | collective-permute-start | bytes 294920 | tf_op jit(solution)/shard_map/ppermute | solution.py:351
  9.1 3.3 %collective-permute-start.1 = (bf16[128,768]{1,0:T(8,128)(2,1)}, bf16[128,768]{1,0:T(8,128)(2,1)S(1)}, u32[]{:S(2)}, u32[]{:S(2)}) collective-permute-start(bf16[128,768]{1,0:T(8,128)(2,1)} %get-tuple-element.39.mid_ref.refs_9_), channel_id=1, source_target_pairs={{0,2},{1,3},{2,0},{3,1},{4,6},{5,7},{6,4},{7,5},{8,10},{9,11},{10,... | collective-permute-start | bytes 589832 | tf_op jit(solution)/shard_map/ppermute | solution.py:351
  12.3 2.9 %collective-permute-done.5.refs_6_ = bf16[64,768]{1,0:T(8,128)(2,1)S(1)} collective-permute-done((bf16[64,768]{1,0:T(8,128)(2,1)}, bf16[64,768]{1,0:T(8,128)(2,1)S(1)}, u32[]{:S(2)}, u32[]{:S(2)}) %collective-permute-start.5) | collective-permute-done | bytes 98336 | tf_op jit(solution)/shard_map/ppermute | solution.py:351
  18.4 7.9 %attend_own.1 = (bf16[6,480,512]{2,1,0:T(8,128)(2,1)}, f32[6,32,256]{2,1,0:T(8,128)}, f32[6,128,256]{2,1,0:T(8,128)}) custom-call(bf16[1,256,768]{2,1,0:T(8,128)(2,1)} %query_ref.3, bf16[1,256,768]{2,1,0:T(8,128)(2,1)} %key_ref.5, bf16[1,256,768]{2,1,0:T(8,128)(2,1)} %value_ref.5, bf16[384,768]{1,0:T(8,128)(2,1)} %get-tuple-element.38.near_ref, ...), custom_call_target="tpu_custom_call" | custom-call | flops 600000000 | bytes 1000000 | tf_op jit(solution)/shard_map/attend_own/pallas_call | solution.py:243
  26.3 3.0 %collective-permute-done.1.refs_1_ = bf16[128,768]{1,0:T(8,128)(2,1)S(1)} collective-permute-done((bf16[128,768]{1,0:T(8,128)(2,1)}, bf16[128,768]{1,0:T(8,128)(2,1)S(1)}, u32[]{:S(2)}, u32[]{:S(2)}) %collective-permute-start.1) | collective-permute-done | bytes 196640 | tf_op jit(solution)/shard_map/ppermute | solution.py:351
  30.6 5.9 %collective-permute-done.2.refs_2_ = bf16[128,768]{1,0:T(8,128)(2,1)} collective-permute-done((bf16[128,768]{1,0:T(8,128)(2,1)}, bf16[128,768]{1,0:T(8,128)(2,1)}, u32[]{:S(2)}, u32[]{:S(2)}) %collective-permute-start.2) | collective-permute-done | bytes 196640 | tf_op jit(solution)/shard_map/ppermute | solution.py:351
  37.4 13.7 %attend_both.1 = (bf16[256,768]{1,0:T(8,128)(2,1)}, bf16[1,256,768]{2,1,0:T(8,128)(2,1)}, f32[512,768]{1,0:T(8,128)}, f32[256,768]{1,0:T(8,128)}, f32[128,768]{1...) custom-call(bf16[1,256,768]{2,1,0:T(8,128)(2,1)} %query_ref.3, ...), custom_call_target="tpu_custom_call" | custom-call | flops 15600000000 | bytes 1000000 | tf_op jit(solution)/shard_map/attend_both/pallas_call | solution.py:243
  51.2 1.4 %fusion.2 = bf16[768,384]{1,0:T(8,128)(2,1)S(1)} fusion(bf16[256,768]{1,0:T(8,128)(2,1)} %get-tuple-element.46, s32[]{:T(128)S(6)} %select_n.45, bf16[1,256,768]{2,1,0:T(8,128)(2,1)S(1)} %copy-done.1), kind=kOutput, calls=%fused_computation.4 | convolution fusion | flops 151289856 | bytes 1179652 | tf_op jit(solution)/shard_map/dot_general | solution.py:369
  52.6 1.5 %collective-permute-start.7 = (bf16[768,384]{1,0:T(8,128)(2,1)S(1)}, bf16[768,384]{1,0:T(8,128)(2,1)S(1)}, u32[]{:S(2)}, u32[]{:S(2)}) collective-permute-start(bf16[768,384]{1,0:T(8,128)(2,1)S(1)} %fusion.2), channel_id=1, source_target_pairs={{0,64},{64,0},{128,192},{192,128},{1,65},{65,1},{129,193},{193,129... | collective-permute-start | bytes 1769480 | tf_op jit(solution)/shard_map/ppermute | solution.py:355
  54.2 1.8 %collective-permute-start.9 = (bf16[128,768]{1,0:T(8,128)(2,1)}, bf16[128,768]{1,0:T(8,128)(2,1)}, u32[]{:S(2)}, u32[]{:S(2)}) collective-permute-start(bf16[128,768]{1,0:T(8,128)(2,1)} %get-tuple-element.52), channel_id=1, source_target_pairs={{0,2},{1,3},{2,0},{3,1},{4,6},{5,7},{6,4},{7,5},{8,10},{9,11},{10,... | collective-permute-start | bytes 589832 | tf_op jit(solution)/shard_map/ppermute | solution.py:351
  56.0 1.3 %collective-permute-start.10 = (bf16[256,768]{1,0:T(8,128)(2,1)S(1)}, bf16[256,768]{1,0:T(8,128)(2,1)}, u32[]{:S(2)}, u32[]{:S(2)}) collective-permute-start(bf16[256,768]{1,0:T(8,128)(2,1)S(1)} %copy-done.12), channel_id=1, source_target_pairs={{0,4},{1,5},{2,6},{3,7},{4,0},{5,1},{6,2},{7,3},{8,12},{9,13},{10,... | collective-permute-start | bytes 1179656 | tf_op jit(solution)/shard_map/ppermute | solution.py:351
  58.5 6.5 %all-to-all-start = ((bf16[16,48,384]{2,1,0:T(8,128)(2,1)}), bf16[16,48,384]{2,1,0:T(8,128)(2,1)S(1)}, u32[]{:S(2)}, u32[]{:S(2)}) async-start(bf16[16,48,384]{2,1,0:T(8,128)(2,1)} %bitcast.3), calls=%async_computation | async-start | bytes 1179648 | tf_op jit(solution)/shard_map/all_to_all | solution.py:376
  66.2 1.8 %collective-permute-start.14 = (bf16[128,768]{1,0:T(8,128)(2,1)S(1)}, bf16[128,768]{1,0:T(8,128)(2,1)S(1)}, u32[]{:S(2)}, u32[]{:S(2)}) collective-permute-start(bf16[128,768]{1,0:T(8,128)(2,1)S(1)} %copy-done.14), channel_id=1, source_target_pairs={{0,3},{1,2},{2,1},{3,0},{4,7},{5,6},{6,5},{7,4},{8,11},{9,10},{10,... | collective-permute-start | bytes 589832 | tf_op jit(solution)/shard_map/ppermute | solution.py:351
  68.0 3.6 %collective-permute-done.9.refs_4_ = bf16[128,768]{1,0:T(8,128)(2,1)} collective-permute-done((bf16[128,768]{1,0:T(8,128)(2,1)}, bf16[128,768]{1,0:T(8,128)(2,1)}, u32[]{:S(2)}, u32[]{:S(2)}) %collective-permute-start.9) | collective-permute-done | bytes 196640 | tf_op jit(solution)/shard_map/ppermute | solution.py:351
  71.6 2.0 %collective-permute-done.8.refs_1_.refs_3_ = bf16[384,768]{1,0:T(8,128)(2,1)} collective-permute-done((bf16[384,768]{1,0:T(8,128)(2,1)}, bf16[384,768]{1,0:T(8,128)(2,1)}, u32[]{:S(2)}, u32[]{:S(2)}) %collective-permute-start.8) | collective-permute-done | bytes 589856 | tf_op jit(solution)/shard_map/ppermute | solution.py:351
  76.5 2.1 %collective-permute-start.12 = (bf16[72,768]{1,0:T(8,128)(2,1)S(1)}, bf16[72,768]{1,0:T(8,128)(2,1)S(1)}, u32[]{:S(2)}, u32[]{:S(2)}) collective-permute-start(bf16[72,768]{1,0:T(8,128)(2,1)S(1)} %pad_maximum_fusion.2), channel_id=1, source_target_pairs={{0,2},{1,3},{2,0},{3,1},{4,6},{5,7},{6,4},{7,5},{8,10},{9,11},{10,... | collective-permute-start | bytes 331784 | tf_op jit(solution)/shard_map/ppermute | solution.py:351
  78.7 1.6 %collective-permute-start.13 = (bf16[72,768]{1,0:T(8,128)(2,1)S(1)}, bf16[72,768]{1,0:T(8,128)(2,1)S(1)}, u32[]{:S(2)}, u32[]{:S(2)}) collective-permute-start(bf16[72,768]{1,0:T(8,128)(2,1)S(1)} %pad_maximum_fusion.3), channel_id=1, source_target_pairs={{0,3},{1,2},{2,1},{3,0},{4,7},{5,6},{6,5},{7,4},{8,11},{9,10},{10,... | collective-permute-start | bytes 331784 | tf_op jit(solution)/shard_map/ppermute | solution.py:351
  80.9 3.4 %spread_rows.2 = (f32[1,256,768]{2,1,0:T(8,128)}, f32[1,256,768]{2,1,0:T(8,128)}) custom-call(s32[3,12]{1,0:T(4,128)} %offsets_ref.5, f32[2,256,768]{2,1,0:T(8,128)} %bitcast.24, f32[2,256,768]{2,1,0:T(8,128)} %bitcast.25, f32[256,768]{1,0:T(8,128)} %get-tuple-element.56.refs_0_, bf16[384,768]{1,0:T(8,128)(2,1)} %collective-permute-done.8.refs_1_.refs_3_, ...), custom_call_target="tpu_custom_call" | custom-call | flops 2000000000 | bytes 4000000 | tf_op jit(solution)/shard_map/spread_rows/pallas_call | solution.py:333
  84.3 1.8 %collective-permute-done.12.refs_2_ = bf16[72,768]{1,0:T(8,128)(2,1)S(1)} collective-permute-done((bf16[72,768]{1,0:T(8,128)(2,1)S(1)}, bf16[72,768]{1,0:T(8,128)(2,1)S(1)}, u32[]{:S(2)}, u32[]{:S(2)}) %collective-permute-start.12) | collective-permute-done | bytes 110624 | tf_op jit(solution)/shard_map/ppermute | solution.py:351
  86.2 5.3 %collective-permute-start.15 = (bf16[6,768]{1,0:T(8,128)(2,1)S(1)}, bf16[6,768]{1,0:T(8,128)(2,1)S(1)}, u32[]{:S(2)}, u32[]{:S(2)}) collective-permute-start(bf16[6,768]{1,0:T(8,128)(2,1)S(1)} %add_convert_fusion.1), channel_id=1, source_target_pairs={{0,128},{64,192},{128,0},{192,64},{1,129},{65,193},{129,1},{193,65... | collective-permute-start | bytes 27656 | tf_op jit(solution)/shard_map/ppermute | solution.py:355
  91.5 2.7 %spread_rows.3 = (bf16[1,256,768]{2,1,0:T(8,128)(2,1)}, bf16[1,256,768]{2,1,0:T(8,128)(2,1)}) custom-call(s32[3,12]{1,0:T(4,128)} %offsets_ref.5, f32[1,256,768]{2,1,0:T(8,128)} %get-tuple-element.64.key_base_ref, f32[1,256,768]{2,1,0:T(8,128)} %get-tuple-element.65.value_base_ref, bf16[256,768]{1,0:T(8,128)(2,1)} %copy-done.3, bf16[72,768]{1,0:T(8,128)(2,1)} %copy-done.8, ...), custom_call_target="tpu_custom_call" | custom-call | flops 2000000000 | bytes 4000000 | tf_op jit(solution)/shard_map/spread_rows/pallas_call | solution.py:333
  94.2 4.0 %collective-permute-start.16 = (bf16[6,768]{1,0:T(8,128)(2,1)S(1)}, bf16[6,768]{1,0:T(8,128)(2,1)S(1)}, u32[]{:S(2)}, u32[]{:S(2)}) collective-permute-start(bf16[6,768]{1,0:T(8,128)(2,1)S(1)} %multiply_convert_fusion), channel_id=1, source_target_pairs={{0,64},{64,0},{128,192},{192,128},{1,65},{65,1},{129,193},{193,129... | collective-permute-start | bytes 27656 | tf_op jit(solution)/shard_map/ppermute | solution.py:355
  (71 shorter events, 13.3 us)
Async XLA Ops:
  0.6 28.7 %copy-start = (bf16[768,768]{1,0:T(8,128)(2,1)S(1)}, bf16[768,768]{1,0:T(8,128)(2,1)}, u32[]{:S(2)}) copy-start(bf16[768,768]{1,0:T(8,128)(2,1)} %param.9) | copy-start | bytes 3538948
  3.3 9.0 %collective-permute-start.3 = (bf16[64,768]{1,0:T(8,128)(2,1)}, bf16[64,768]{1,0:T(8,128)(2,1)S(1)}, u32[]{:S(2)}, u32[]{:S(2)}) collective-permute-start(bf16[64,768]{1,0:T(8,128)(2,1)} %get-tuple-element.41.far_ref.refs_3_), channel_id=1, source_target_pairs={{0,1},{1,0},{2,3},{3,2},{4,5},{5,4},{6,7},{7,6},{8,9},{9,8},{10,11... | collective-permute-start | bytes 294920 | tf_op jit(solution)/shard_map/ppermute | solution.py:351
  5.8 6.5 %collective-permute-start.4 = (bf16[64,768]{1,0:T(8,128)(2,1)}, bf16[64,768]{1,0:T(8,128)(2,1)S(1)}, u32[]{:S(2)}, u32[]{:S(2)}) collective-permute-start(bf16[64,768]{1,0:T(8,128)(2,1)} %get-tuple-element.41.far_ref.refs_3_), channel_id=1, source_target_pairs={{0,2},{1,3},{2,0},{3,1},{4,6},{5,7},{6,4},{7,5},{8,10},{9,11},{10,... | collective-permute-start | bytes 294920 | tf_op jit(solution)/shard_map/ppermute | solution.py:351
  8.8 6.5 %collective-permute-start.5 = (bf16[64,768]{1,0:T(8,128)(2,1)}, bf16[64,768]{1,0:T(8,128)(2,1)S(1)}, u32[]{:S(2)}, u32[]{:S(2)}) collective-permute-start(bf16[64,768]{1,0:T(8,128)(2,1)} %get-tuple-element.41.far_ref.refs_3_), channel_id=1, source_target_pairs={{0,3},{1,2},{2,1},{3,0},{4,7},{5,6},{6,5},{7,4},{8,11},{9,10},{10,... | collective-permute-start | bytes 294920 | tf_op jit(solution)/shard_map/ppermute | solution.py:351
  8.8 27.7 %collective-permute-start = (bf16[384,768]{1,0:T(8,128)(2,1)}, bf16[384,768]{1,0:T(8,128)(2,1)S(1)}, u32[]{:S(2)}, u32[]{:S(2)}) collective-permute-start(bf16[384,768]{1,0:T(8,128)(2,1)} %get-tuple-element.38.near_ref), channel_id=1, source_target_pairs={{0,1},{1,0},{2,3},{3,2},{4,5},{5,4},{6,7},{7,6},{8,9},{9,8},{10,11... | collective-permute-start | bytes 1769480 | tf_op jit(solution)/shard_map/ppermute | solution.py:351
  9.1 20.3 %collective-permute-start.1 = (bf16[128,768]{1,0:T(8,128)(2,1)}, bf16[128,768]{1,0:T(8,128)(2,1)S(1)}, u32[]{:S(2)}, u32[]{:S(2)}) collective-permute-start(bf16[128,768]{1,0:T(8,128)(2,1)} %get-tuple-element.39.mid_ref.refs_9_), channel_id=1, source_target_pairs={{0,2},{1,3},{2,0},{3,1},{4,6},{5,7},{6,4},{7,5},{8,10},{9,11},{10,... | collective-permute-start | bytes 589832 | tf_op jit(solution)/shard_map/ppermute | solution.py:351
  12.3 14.0 %copy-start.5 = (bf16[64,768]{1,0:T(8,128)(2,1)}, bf16[64,768]{1,0:T(8,128)(2,1)S(1)}, u32[]{:S(2)}) copy-start(bf16[64,768]{1,0:T(8,128)(2,1)S(1)} %collective-permute-done.3.refs_4_) | copy-start | bytes 294916
  12.3 14.0 %copy-start.6 = (bf16[64,768]{1,0:T(8,128)(2,1)}, bf16[64,768]{1,0:T(8,128)(2,1)S(1)}, u32[]{:S(2)}) copy-start(bf16[64,768]{1,0:T(8,128)(2,1)S(1)} %collective-permute-done.4.refs_5_) | copy-start | bytes 294916
  15.3 11.1 %copy-start.7 = (bf16[64,768]{1,0:T(8,128)(2,1)}, bf16[64,768]{1,0:T(8,128)(2,1)S(1)}, u32[]{:S(2)}) copy-start(bf16[64,768]{1,0:T(8,128)(2,1)S(1)} %collective-permute-done.5.refs_6_) | copy-start | bytes 294916
  16.2 13.1 %copy-start.1 = (bf16[1,256,768]{2,1,0:T(8,128)(2,1)S(1)}, bf16[1,256,768]{2,1,0:T(8,128)(2,1)}, u32[]{:S(2)}) copy-start(bf16[1,256,768]{2,1,0:T(8,128)(2,1)} %param.10) | copy-start | bytes 1179652
  16.2 20.2 %collective-permute-start.6 = (bf16[256,768]{1,0:T(8,128)(2,1)S(1)}, bf16[256,768]{1,0:T(8,128)(2,1)S(1)}, u32[]{:S(2)}, u32[]{:S(2)}) collective-permute-start(bf16[256,768]{1,0:T(8,128)(2,1)S(1)} %pad_maximum_fusion), channel_id=1, source_target_pairs={{0,4},{1,5},{2,6},{3,7},{4,0},{5,1},{6,2},{7,3},{8,12},{9,13},{10,... | collective-permute-start | bytes 1179656 | tf_op jit(solution)/shard_map/ppermute | solution.py:351
  17.5 19.0 %collective-permute-start.2 = (bf16[128,768]{1,0:T(8,128)(2,1)}, bf16[128,768]{1,0:T(8,128)(2,1)}, u32[]{:S(2)}, u32[]{:S(2)}) collective-permute-start(bf16[128,768]{1,0:T(8,128)(2,1)} %get-tuple-element.39.mid_ref.refs_9_), channel_id=1, source_target_pairs={{0,3},{1,2},{2,1},{3,0},{4,7},{5,6},{6,5},{7,4},{8,11},{9,10},{10,... | collective-permute-start | bytes 589832 | tf_op jit(solution)/shard_map/ppermute | solution.py:351
  52.6 4.6 %collective-permute-start.7 = (bf16[768,384]{1,0:T(8,128)(2,1)S(1)}, bf16[768,384]{1,0:T(8,128)(2,1)S(1)}, u32[]{:S(2)}, u32[]{:S(2)}) collective-permute-start(bf16[768,384]{1,0:T(8,128)(2,1)S(1)} %fusion.2), channel_id=1, source_target_pairs={{0,64},{64,0},{128,192},{192,128},{1,65},{65,1},{129,193},{193,129... | collective-permute-start | bytes 1769480 | tf_op jit(solution)/shard_map/ppermute | solution.py:355
  54.2 19.4 %collective-permute-start.8 = (bf16[384,768]{1,0:T(8,128)(2,1)}, bf16[384,768]{1,0:T(8,128)(2,1)}, u32[]{:S(2)}, u32[]{:S(2)}) collective-permute-start(bf16[384,768]{1,0:T(8,128)(2,1)} %get-tuple-element.51), channel_id=1, source_target_pairs={{0,1},{1,0},{2,3},{3,2},{4,5},{5,4},{6,7},{7,6},{8,9},{9,8},{10,11... | collective-permute-start | bytes 1769480 | tf_op jit(solution)/shard_map/ppermute | solution.py:351
  54.2 17.4 %collective-permute-start.9 = (bf16[128,768]{1,0:T(8,128)(2,1)}, bf16[128,768]{1,0:T(8,128)(2,1)}, u32[]{:S(2)}, u32[]{:S(2)}) collective-permute-start(bf16[128,768]{1,0:T(8,128)(2,1)} %get-tuple-element.52), channel_id=1, source_target_pairs={{0,2},{1,3},{2,0},{3,1},{4,6},{5,7},{6,4},{7,5},{8,10},{9,11},{10,... | collective-permute-start | bytes 589832 | tf_op jit(solution)/shard_map/ppermute | solution.py:351
  56.0 17.6 %collective-permute-start.10 = (bf16[256,768]{1,0:T(8,128)(2,1)S(1)}, bf16[256,768]{1,0:T(8,128)(2,1)}, u32[]{:S(2)}, u32[]{:S(2)}) collective-permute-start(bf16[256,768]{1,0:T(8,128)(2,1)S(1)} %copy-done.12), channel_id=1, source_target_pairs={{0,4},{1,5},{2,6},{3,7},{4,0},{5,1},{6,2},{7,3},{8,12},{9,13},{10,... | collective-permute-start | bytes 1179656 | tf_op jit(solution)/shard_map/ppermute | solution.py:351
  58.5 17.5 %all-to-all-start = ((bf16[16,48,384]{2,1,0:T(8,128)(2,1)}), bf16[16,48,384]{2,1,0:T(8,128)(2,1)S(1)}, u32[]{:S(2)}, u32[]{:S(2)}) async-start(bf16[16,48,384]{2,1,0:T(8,128)(2,1)} %bitcast.3), calls=%async_computation | async-start | bytes 1179648 | tf_op jit(solution)/shard_map/all_to_all | solution.py:376
  66.2 14.0 %collective-permute-start.14 = (bf16[128,768]{1,0:T(8,128)(2,1)S(1)}, bf16[128,768]{1,0:T(8,128)(2,1)S(1)}, u32[]{:S(2)}, u32[]{:S(2)}) collective-permute-start(bf16[128,768]{1,0:T(8,128)(2,1)S(1)} %copy-done.14), channel_id=1, source_target_pairs={{0,3},{1,2},{2,1},{3,0},{4,7},{5,6},{6,5},{7,4},{8,11},{9,10},{10,... | collective-permute-start | bytes 589832 | tf_op jit(solution)/shard_map/ppermute | solution.py:351
  74.7 9.6 %copy-start.3 = (bf16[256,768]{1,0:T(8,128)(2,1)}, bf16[256,768]{1,0:T(8,128)(2,1)S(1)}, u32[]{:S(2)}) copy-start(bf16[256,768]{1,0:T(8,128)(2,1)S(1)} %add_convert_fusion.refs_0_) | copy-start | bytes 1179652
  76.2 8.2 %collective-permute-start.11 = (bf16[72,768]{1,0:T(8,128)(2,1)S(1)}, bf16[72,768]{1,0:T(8,128)(2,1)S(1)}, u32[]{:S(2)}, u32[]{:S(2)}) collective-permute-start(bf16[72,768]{1,0:T(8,128)(2,1)S(1)} %pad_maximum_fusion.1), channel_id=1, source_target_pairs={{0,1},{1,0},{2,3},{3,2},{4,5},{5,4},{6,7},{7,6},{8,9},{9,8},{10,11... | collective-permute-start | bytes 331784 | tf_op jit(solution)/shard_map/ppermute | solution.py:351
  76.5 9.7 %collective-permute-start.12 = (bf16[72,768]{1,0:T(8,128)(2,1)S(1)}, bf16[72,768]{1,0:T(8,128)(2,1)S(1)}, u32[]{:S(2)}, u32[]{:S(2)}) collective-permute-start(bf16[72,768]{1,0:T(8,128)(2,1)S(1)} %pad_maximum_fusion.2), channel_id=1, source_target_pairs={{0,2},{1,3},{2,0},{3,1},{4,6},{5,7},{6,4},{7,5},{8,10},{9,11},{10,... | collective-permute-start | bytes 331784 | tf_op jit(solution)/shard_map/ppermute | solution.py:351
  78.7 7.5 %collective-permute-start.13 = (bf16[72,768]{1,0:T(8,128)(2,1)S(1)}, bf16[72,768]{1,0:T(8,128)(2,1)S(1)}, u32[]{:S(2)}, u32[]{:S(2)}) collective-permute-start(bf16[72,768]{1,0:T(8,128)(2,1)S(1)} %pad_maximum_fusion.3), channel_id=1, source_target_pairs={{0,3},{1,2},{2,1},{3,0},{4,7},{5,6},{6,5},{7,4},{8,11},{9,10},{10,... | collective-permute-start | bytes 331784 | tf_op jit(solution)/shard_map/ppermute | solution.py:351
  86.2 7.9 %collective-permute-start.15 = (bf16[6,768]{1,0:T(8,128)(2,1)S(1)}, bf16[6,768]{1,0:T(8,128)(2,1)S(1)}, u32[]{:S(2)}, u32[]{:S(2)}) collective-permute-start(bf16[6,768]{1,0:T(8,128)(2,1)S(1)} %add_convert_fusion.1), channel_id=1, source_target_pairs={{0,128},{64,192},{128,0},{192,64},{1,129},{65,193},{129,1},{193,65... | collective-permute-start | bytes 27656 | tf_op jit(solution)/shard_map/ppermute | solution.py:355
  94.2 4.9 %collective-permute-start.16 = (bf16[6,768]{1,0:T(8,128)(2,1)S(1)}, bf16[6,768]{1,0:T(8,128)(2,1)S(1)}, u32[]{:S(2)}, u32[]{:S(2)}) collective-permute-start(bf16[6,768]{1,0:T(8,128)(2,1)S(1)} %multiply_convert_fusion), channel_id=1, source_target_pairs={{0,64},{64,0},{128,192},{192,128},{1,65},{65,1},{129,193},{193,129... | collective-permute-start | bytes 27656 | tf_op jit(solution)/shard_map/ppermute | solution.py:355
  (11 other events, 48.0 us)
